TPU v7x, 256 devices: a whole 4x4x8 slice. The times are simulated.
256 devices in a mesh: ctx: 16 (over z, core), head: 16 (over x, y).
Axes of the slice: x: 4, y: 4, z: 8, core: 2. Of those that a mesh axis runs over, the one named last changes fastest.
Arguments:
- tokens: bfloat16 [32768, 16384], P(('ctx', 'head')), may hold values from -6 to 6
- b_proj: bfloat16 [32768, 2048], P(('ctx', 'head')), may hold values from -0.375 to 0.375
- c_proj: bfloat16 [32768, 2048], P(('ctx', 'head')), may hold values from -0.119628906 to 0.119628906
- log_decay: bfloat16 [32768, 256], P(('ctx', 'head')), may hold values from -2 to 0, as said below
- bypass_gain_vector: float32 [256], P('head'), may hold values from 0.5 to 1.5
Outputs:
- mixed: bfloat16 [32768, 16384], P(('ctx', 'head'))
Inputs may be any that keep to these rules, and one draw needn't show every extreme that they name: `log_decay`: non-positive log decays.
All inputs are finite; a program needn't handle non-finite values.
Results may differ from a plain program's by a relative error of at most 0.014.
Values may be sent and summed in bfloat16 or wider, within the bound.
No kernel may reach another device: no remote copies, remote signals or barrier semaphores. Data moves between devices by JAX's collectives and lax.ppermute only.
A program may use at most 192 MiB of HBM per device.

v0:
```python
import jax
import jax.numpy as jnp
from jax import lax
from jax.sharding import PartitionSpec as P

H = 256
P_SIZE = 64
N = 256
G = 8
Q = 256


def passed_along(block, axis, distance):
    devices = range(lax.axis_size(axis))
    route = [(i - distance, i) for i in devices if i - distance in devices]
    return lax.ppermute(block, axis, route)


def combine(earlier, later):
    return (earlier[0] + later[0], jnp.exp(later[0])[..., None, None] * earlier[1] + later[1])


def local(tokens, b_proj, c_proj, log_decay, bypass_gain_vector):
    heads_here = bypass_gain_vector.shape[0]
    tok_rows = tokens.shape[0]
    repeat = max(1, H // G // heads_here)
    input_projection_outgoing = jnp.repeat(b_proj.reshape(tok_rows, G, N), repeat, axis=1).reshape(
        tok_rows, G * repeat * N
    )
    c_send = jnp.repeat(c_proj.reshape(tok_rows, G, N), repeat, axis=1).reshape(
        tok_rows, G * repeat * N
    )
    values, b_rows, c_rows, rates = (
        lax.all_to_all(tokens, "head", split_axis=1, concat_axis=0, tiled=True),
        lax.all_to_all(input_projection_outgoing, "head", split_axis=1, concat_axis=0, tiled=True),
        lax.all_to_all(c_send, "head", split_axis=1, concat_axis=0, tiled=True),
        lax.all_to_all(log_decay, "head", split_axis=1, concat_axis=0, tiled=True),
    )
    length = values.shape[0]
    block_list = length // Q
    local_groups = b_rows.shape[1] // N
    per_group = heads_here // local_groups
    value_blocks = values.reshape(block_list, Q, local_groups, per_group, P_SIZE)
    b_blocks = b_rows.reshape(block_list, Q, local_groups, N)
    c_blocks = c_rows.reshape(block_list, Q, local_groups, N)
    cumul = jnp.cumsum(
        rates.astype(jnp.float32).reshape(block_list, Q, local_groups, per_group), axis=1
    )
    totals = cumul[:, -1]
    forward_only_masking = jnp.arange(Q)[:, None] >= jnp.arange(Q)[None, :]

    def one_block(item):
        value_blk, b_blk, c_blk, cum_blk = item
        scores = jnp.einsum("qgn,kgn->gqk", c_blk, b_blk, preferred_element_type=jnp.float32)
        moved = jnp.moveaxis(cum_blk, 0, -1)
        spread = moved[..., :, None] - moved[..., None, :]
        decays = jnp.exp(jnp.where(forward_only_masking, spread, -jnp.inf))
        weights = (scores[:, None] * decays).astype(jnp.bfloat16)
        inner = jnp.einsum(
            "ghqk,kghp->qghp", weights, value_blk, preferred_element_type=jnp.float32
        )
        tail = jnp.exp(cum_blk[-1][None] - cum_blk)
        b_weighted = (b_blk[:, :, None, :].astype(jnp.float32) * tail[..., None]).astype(
            jnp.bfloat16
        )
        block_state = jnp.einsum(
            "kghn,kghp->ghpn", b_weighted, value_blk, preferred_element_type=jnp.float32
        )
        return (inner, block_state)

    inner, block_states = lax.map(one_block, (value_blocks, b_blocks, c_blocks, cumul))

    def advance(carry, item):
        total_blk, state_blk = item
        return (jnp.exp(total_blk)[..., None, None] * carry + state_blk, carry)

    zero_state = jnp.zeros((local_groups, per_group, P_SIZE, N), jnp.float32)
    zero_total = jnp.zeros((local_groups, per_group), jnp.float32)
    end_local, starts_local = lax.scan(advance, zero_state, (totals, block_states))
    running = jnp.cumsum(totals, axis=0)
    device_number = running[-1]
    prefix_decay = running - totals

    def relay(turn_index, carry):
        joined_result = combine(carry, (device_number, end_local))
        return passed_along((joined_result[0], joined_result[1]), "ctx", 1)

    in_total, in_state = lax.fori_loop(0, lax.axis_size("ctx") - 1, relay, (zero_total, zero_state))
    starts = starts_local + jnp.exp(prefix_decay)[..., None, None] * in_state[None]
    start_rounded = starts.astype(jnp.bfloat16)
    outer = jnp.einsum(
        "cqgn,cghpn->cqghp", c_blocks, start_rounded, preferred_element_type=jnp.float32
    )
    outer = outer * jnp.exp(cumul)[..., None]
    gains = bypass_gain_vector.reshape(local_groups, per_group)
    result = inner + outer + gains[None, None, :, :, None] * value_blocks.astype(jnp.float32)
    mixed_rows = result.astype(jnp.bfloat16).reshape(length, heads_here * P_SIZE)
    return lax.all_to_all(mixed_rows, "head", split_axis=0, concat_axis=1, tiled=True)


def solution(mesh):
    placed = (
        P(("ctx", "head"), None),
        P(("ctx", "head"), None),
        P(("ctx", "head"), None),
        P(("ctx", "head"), None),
        P("head"),
    )
    return jax.shard_map(
        local, mesh=mesh, in_specs=placed, out_specs=P(("ctx", "head"), None), check_vma=False
    )
```

profile of v0, /device:TPU:32, one launch (start us, length us, event | category | flops | bytes accessed | tf_op | source)
XLA Modules:
  0.0 540.0 jit_solution(11540945614785674225)
XLA Ops:
  27.5 9.5 %all-to-all-done.1 = bf16[128,16,256]{2,0,1:T(8,128)(2,1)S(1)} async-done(((bf16[128,16,256]{2,0,1:T(8,128)(2,1)}), bf16[128,16,256]{2,0,1:T(8,128)(2,1)S(1)}, u32[]{:S(2)}, u32[]{:S(2)}) %all-to-all-start.1) | async-done | bytes 1048608 | tf_op jit(solution)/shard_map/all_to_all | solution.py:36
  46.8 47.3 %all-to-all-done = bf16[128,16,1024]{0,2,1:T(8,128)(2,1)} async-done(((bf16[128,16,1024]{0,2,1:T(8,128)(2,1)}), bf16[128,16,1024]{0,2,1:T(8,128)(2,1)}, u32[]{:S(2)}, u32[]{:S(2)}) %all-to-all-start) | async-done | bytes 4194336 | tf_op jit(solution)/shard_map/all_to_all | solution.py:34
  107.7 7.1 %reshape.248 = bf16[8,256,1,16,64]{1,0,4,3,2:T(8,128)(2,1)} reshape(bf16[16,128,1024]{1,0,2:T(8,128)(2,1)} %copy.51) | data formatting | bytes 8388608 | tf_op jit(solution)/shard_map/reshape | solution.py:43
  124.3 53.5 %while.39 = (s32[]{:T(128)}, f32[8,256,1,16,64]{1,4,3,2,0:T(8,128)}, f32[8,1,16,64,256]{4,3,2,1,0:T(8,128)}, bf16[8,256,1,16,64]{1,4,3,2,0:T(8,128)(2,1)}, bf16[...) while((s32[]{:T(128)}, ...), condition=%wide.region_3.4_spmd.clone, body=%wide.region_2.3_spmd.clone.sunk | while | flops 308416512 | bytes 4869405 | solution.py:71
  182.0 20.3 %while.40 = (s32[]{:T(128)}, f32[1,16,64,256]{3,2,1,0:T(8,128)S(1)}, f32[8,1,16,64,256]{4,3,2,1,0:T(8,128)}, f32[8,1,16]{2,1,0:T(1,128)S(1)}, f32[8,1,16,64,256]{4,3,2,1,0:T(8,128)}, /*index=5*/s32[]{:T(128)}, s32[]{:T(128)}) while((s32[]{:T(128)}, f32[1,16,64,256]{3,2,1,0:T(8,128)S(1)}, f32[8,1,16,64,256]{4,3,2,1,0:T(8,128)}, ...), condition=%wide.region_5.6_spmd.clone, body=%wide.region_4.5_spmd.clone.sunk | while | flops 1048579 | bytes 5243680 | solution.py:79
  202.5 244.3 %while.38 = (s32[]{:T(128)}, f32[1,16,64,256]{3,2,1,0:T(8,128)S(1)}, f32[1,16,1,1]{1,3,2,0:T(1,128)S(1)}, f32[1,16,64,256]{3,2,1,0:T(8,128)S(1)}, s32[]{:T(128)}) while((s32[]{:T(128)}, f32[1,16,64,256]{3,2,1,0:T(8,128)S(1)}, f32[1,16,1,1]{1,3,2,0:T(1,128)S(1)}, f32[1,16,64,256]{3,2,1,0:T(8,128)S(1)}, s32[]{:T(128)}) %tuple.76), condition=%wide.region_8.9_spmd, body=%wide.region_7.8_spmd.sunk | while | flops 524290 | bytes 7340197 | solution.py:88
  204.6 14.2 %collective-permute-done = f32[1,16,64,256]{3,2,1,0:T(8,128)S(1)} collective-permute-done((f32[1,16,64,256]{3,2,1,0:T(8,128)S(1)}, f32[1,16,64,256]{3,2,1,0:T(8,128)S(1)}, u32[]{:S(2)}, u32[]{:S(2)}) %collective-permute-start) | collective-permute-done | bytes 1048608 | tf_op jit(solution)/shard_map/while/body/eval_jaxpr/ppermute | solution.py:16
  220.9 14.2 %collective-permute-done = f32[1,16,64,256]{3,2,1,0:T(8,128)S(1)} collective-permute-done((f32[1,16,64,256]{3,2,1,0:T(8,128)S(1)}, f32[1,16,64,256]{3,2,1,0:T(8,128)S(1)}, u32[]{:S(2)}, u32[]{:S(2)}) %collective-permute-start) | collective-permute-done | bytes 1048608 | tf_op jit(solution)/shard_map/while/body/eval_jaxpr/ppermute | solution.py:16
  237.2 14.2 %collective-permute-done = f32[1,16,64,256]{3,2,1,0:T(8,128)S(1)} collective-permute-done((f32[1,16,64,256]{3,2,1,0:T(8,128)S(1)}, f32[1,16,64,256]{3,2,1,0:T(8,128)S(1)}, u32[]{:S(2)}, u32[]{:S(2)}) %collective-permute-start) | collective-permute-done | bytes 1048608 | tf_op jit(solution)/shard_map/while/body/eval_jaxpr/ppermute | solution.py:16
  253.4 14.2 %collective-permute-done = f32[1,16,64,256]{3,2,1,0:T(8,128)S(1)} collective-permute-done((f32[1,16,64,256]{3,2,1,0:T(8,128)S(1)}, f32[1,16,64,256]{3,2,1,0:T(8,128)S(1)}, u32[]{:S(2)}, u32[]{:S(2)}) %collective-permute-start) | collective-permute-done | bytes 1048608 | tf_op jit(solution)/shard_map/while/body/eval_jaxpr/ppermute | solution.py:16
  269.7 14.2 %collective-permute-done = f32[1,16,64,256]{3,2,1,0:T(8,128)S(1)} collective-permute-done((f32[1,16,64,256]{3,2,1,0:T(8,128)S(1)}, f32[1,16,64,256]{3,2,1,0:T(8,128)S(1)}, u32[]{:S(2)}, u32[]{:S(2)}) %collective-permute-start) | collective-permute-done | bytes 1048608 | tf_op jit(solution)/shard_map/while/body/eval_jaxpr/ppermute | solution.py:16
  286.0 14.2 %collective-permute-done = f32[1,16,64,256]{3,2,1,0:T(8,128)S(1)} collective-permute-done((f32[1,16,64,256]{3,2,1,0:T(8,128)S(1)}, f32[1,16,64,256]{3,2,1,0:T(8,128)S(1)}, u32[]{:S(2)}, u32[]{:S(2)}) %collective-permute-start) | collective-permute-done | bytes 1048608 | tf_op jit(solution)/shard_map/while/body/eval_jaxpr/ppermute | solution.py:16
  302.3 14.2 %collective-permute-done = f32[1,16,64,256]{3,2,1,0:T(8,128)S(1)} collective-permute-done((f32[1,16,64,256]{3,2,1,0:T(8,128)S(1)}, f32[1,16,64,256]{3,2,1,0:T(8,128)S(1)}, u32[]{:S(2)}, u32[]{:S(2)}) %collective-permute-start) | collective-permute-done | bytes 1048608 | tf_op jit(solution)/shard_map/while/body/eval_jaxpr/ppermute | solution.py:16
  318.6 14.2 %collective-permute-done = f32[1,16,64,256]{3,2,1,0:T(8,128)S(1)} collective-permute-done((f32[1,16,64,256]{3,2,1,0:T(8,128)S(1)}, f32[1,16,64,256]{3,2,1,0:T(8,128)S(1)}, u32[]{:S(2)}, u32[]{:S(2)}) %collective-permute-start) | collective-permute-done | bytes 1048608 | tf_op jit(solution)/shard_map/while/body/eval_jaxpr/ppermute | solution.py:16
  334.9 14.2 %collective-permute-done = f32[1,16,64,256]{3,2,1,0:T(8,128)S(1)} collective-permute-done((f32[1,16,64,256]{3,2,1,0:T(8,128)S(1)}, f32[1,16,64,256]{3,2,1,0:T(8,128)S(1)}, u32[]{:S(2)}, u32[]{:S(2)}) %collective-permute-start) | collective-permute-done | bytes 1048608 | tf_op jit(solution)/shard_map/while/body/eval_jaxpr/ppermute | solution.py:16
  351.2 14.2 %collective-permute-done = f32[1,16,64,256]{3,2,1,0:T(8,128)S(1)} collective-permute-done((f32[1,16,64,256]{3,2,1,0:T(8,128)S(1)}, f32[1,16,64,256]{3,2,1,0:T(8,128)S(1)}, u32[]{:S(2)}, u32[]{:S(2)}) %collective-permute-start) | collective-permute-done | bytes 1048608 | tf_op jit(solution)/shard_map/while/body/eval_jaxpr/ppermute | solution.py:16
  367.5 14.2 %collective-permute-done = f32[1,16,64,256]{3,2,1,0:T(8,128)S(1)} collective-permute-done((f32[1,16,64,256]{3,2,1,0:T(8,128)S(1)}, f32[1,16,64,256]{3,2,1,0:T(8,128)S(1)}, u32[]{:S(2)}, u32[]{:S(2)}) %collective-permute-start) | collective-permute-done | bytes 1048608 | tf_op jit(solution)/shard_map/while/body/eval_jaxpr/ppermute | solution.py:16
  383.8 14.2 %collective-permute-done = f32[1,16,64,256]{3,2,1,0:T(8,128)S(1)} collective-permute-done((f32[1,16,64,256]{3,2,1,0:T(8,128)S(1)}, f32[1,16,64,256]{3,2,1,0:T(8,128)S(1)}, u32[]{:S(2)}, u32[]{:S(2)}) %collective-permute-start) | collective-permute-done | bytes 1048608 | tf_op jit(solution)/shard_map/while/body/eval_jaxpr/ppermute | solution.py:16
  400.1 14.2 %collective-permute-done = f32[1,16,64,256]{3,2,1,0:T(8,128)S(1)} collective-permute-done((f32[1,16,64,256]{3,2,1,0:T(8,128)S(1)}, f32[1,16,64,256]{3,2,1,0:T(8,128)S(1)}, u32[]{:S(2)}, u32[]{:S(2)}) %collective-permute-start) | collective-permute-done | bytes 1048608 | tf_op jit(solution)/shard_map/while/body/eval_jaxpr/ppermute | solution.py:16
  416.3 14.2 %collective-permute-done = f32[1,16,64,256]{3,2,1,0:T(8,128)S(1)} collective-permute-done((f32[1,16,64,256]{3,2,1,0:T(8,128)S(1)}, f32[1,16,64,256]{3,2,1,0:T(8,128)S(1)}, u32[]{:S(2)}, u32[]{:S(2)}) %collective-permute-start) | collective-permute-done | bytes 1048608 | tf_op jit(solution)/shard_map/while/body/eval_jaxpr/ppermute | solution.py:16
  432.6 14.2 %collective-permute-done = f32[1,16,64,256]{3,2,1,0:T(8,128)S(1)} collective-permute-done((f32[1,16,64,256]{3,2,1,0:T(8,128)S(1)}, f32[1,16,64,256]{3,2,1,0:T(8,128)S(1)}, u32[]{:S(2)}, u32[]{:S(2)}) %collective-permute-start) | collective-permute-done | bytes 1048608 | tf_op jit(solution)/shard_map/while/body/eval_jaxpr/ppermute | solution.py:16
  446.8 11.8 %fusion.33 = bf16[8,256,1,16,64]{1,4,3,0,2:T(8,128)(2,1)} fusion(f32[8,256,1,16,64]{1,4,3,2,0:T(8,128)} %get-tuple-element.126, bf16[8,256,1,16,64]{1,0,4,3,2:T(8,128)(2,1)} %reshape.248, f32[16]{0:T(128)S(1)} %copy-done.2, f32[8,256,16]{1,2,0:T(8,128)S(1)} %bitcast.158, bf16[8,256,256,1]{2,1,3,0:T(8,128)(2,1)} %bitcast.152, ...), kind=kOutput, calls=%fused_computation.45 | convolution fusion | flops 1092616192 | bytes 27394624 | tf_op jit(solution)/shard_map/cqgn,cghpn->cqghp/dot_general | solution.py:91
  465.6 7.1 %all_to_all.71 = bf16[16,128,1024]{1,0,2:T(8,128)(2,1)} reshape(bf16[8,256,1,16,64]{1,0,4,3,2:T(8,128)(2,1)} %copy.67) | data formatting | bytes 8388608 | tf_op jit(solution)/shard_map/all_to_all | solution.py:98
  476.0 57.6 %all_to_all.80 = bf16[16,128,1024]{1,2,0:T(8,128)(2,1)} all-to-all(bf16[16,128,1024]{1,2,0:T(8,128)(2,1)S(1)} %copy.68), channel_id=1, replica_groups=mesh['ctx'=16,'head'=16] {'head'}, dimensions={0} | all-to-all | bytes 8388608 | tf_op jit(solution)/shard_map/all_to_all | solution.py:98
  (173 shorter events, 185.9 us)
Async XLA Ops:
  1.6 14.7 %all-to-all-start.3 = ((bf16[128,16,16]{0,2,1:T(8,128)(2,1)}), bf16[128,16,16]{0,2,1:T(8,128)(2,1)S(1)}, u32[]{:S(2)}, u32[]{:S(2)}) async-start(bf16[128,16,16]{0,2,1:T(8,128)(2,1)} %bitcast.10), calls=%async_computation.3 | async-start | bytes 131072 | tf_op jit(solution)/shard_map/all_to_all | solution.py:37
  17.4 19.6 %all-to-all-start.1 = ((bf16[128,16,256]{2,0,1:T(8,128)(2,1)}), bf16[128,16,256]{2,0,1:T(8,128)(2,1)S(1)}, u32[]{:S(2)}, u32[]{:S(2)}) async-start(bf16[128,16,256]{2,0,1:T(8,128)(2,1)} %bitcast.3), calls=%async_computation.1 | async-start | bytes 2097152 | tf_op jit(solution)/shard_map/all_to_all | solution.py:36
  21.0 20.5 %copy-start.1 = (bf16[128,2048]{1,0:T(8,128)(2,1)S(1)}, bf16[128,2048]{1,0:T(8,128)(2,1)}, u32[]{:S(2)}) copy-start(bf16[128,2048]{1,0:T(8,128)(2,1)} %param.12) | copy-start | bytes 1572868
  36.9 57.2 %all-to-all-start = ((bf16[128,16,1024]{0,2,1:T(8,128)(2,1)}), bf16[128,16,1024]{0,2,1:T(8,128)(2,1)}, u32[]{:S(2)}, u32[]{:S(2)}) async-start(bf16[128,16,1024]{0,2,1:T(8,128)(2,1)} %bitcast.149), calls=%async_computation | async-start | bytes 8388608 | tf_op jit(solution)/shard_map/all_to_all | solution.py:34
  95.3 24.7 %all-to-all-start.2 = ((bf16[128,16,256]{2,0,1:T(8,128)(2,1)}), bf16[128,16,256]{2,0,1:T(8,128)(2,1)S(1)}, u32[]{:S(2)}, u32[]{:S(2)}) async-start(bf16[128,16,256]{2,0,1:T(8,128)(2,1)} %bitcast.154), calls=%async_computation.2 | async-start | bytes 2097152 | tf_op jit(solution)/shard_map/all_to_all | solution.py:35
  177.8 4.3 copy-start
  202.4 244.5 %copy-start.2 = (f32[16]{0:T(128)S(1)}, f32[16]{0:T(128)}, u32[]{:S(2)}) copy-start(f32[16]{0:T(128)} %param.15) | copy-start | bytes 196
  202.7 16.1 %collective-permute-start = (f32[1,16,64,256]{3,2,1,0:T(8,128)S(1)}, f32[1,16,64,256]{3,2,1,0:T(8,128)S(1)}, u32[]{:S(2)}, u32[]{:S(2)}) collective-permute-start(f32[1,16,64,256]{3,2,1,0:T(8,128)S(1)} %multiply_add_fusion.2), channel_id=1, source_target_pairs={{0,16},{16,32},{32,48},{48,64},{64,80},{80,96},{96,112},{112,128},... | collective-permute-start | bytes 3145736 | tf_op jit(solution)/shard_map/while/body/eval_jaxpr/ppermute | solution.py:16
  218.9 16.1 %collective-permute-start = (f32[1,16,64,256]{3,2,1,0:T(8,128)S(1)}, f32[1,16,64,256]{3,2,1,0:T(8,128)S(1)}, u32[]{:S(2)}, u32[]{:S(2)}) collective-permute-start(f32[1,16,64,256]{3,2,1,0:T(8,128)S(1)} %multiply_add_fusion.2), channel_id=1, source_target_pairs={{0,16},{16,32},{32,48},{48,64},{64,80},{80,96},{96,112},{112,128},... | collective-permute-start | bytes 3145736 | tf_op jit(solution)/shard_map/while/body/eval_jaxpr/ppermute | solution.py:16
  235.2 16.1 %collective-permute-start = (f32[1,16,64,256]{3,2,1,0:T(8,128)S(1)}, f32[1,16,64,256]{3,2,1,0:T(8,128)S(1)}, u32[]{:S(2)}, u32[]{:S(2)}) collective-permute-start(f32[1,16,64,256]{3,2,1,0:T(8,128)S(1)} %multiply_add_fusion.2), channel_id=1, source_target_pairs={{0,16},{16,32},{32,48},{48,64},{64,80},{80,96},{96,112},{112,128},... | collective-permute-start | bytes 3145736 | tf_op jit(solution)/shard_map/while/body/eval_jaxpr/ppermute | solution.py:16
  251.5 16.1 %collective-permute-start = (f32[1,16,64,256]{3,2,1,0:T(8,128)S(1)}, f32[1,16,64,256]{3,2,1,0:T(8,128)S(1)}, u32[]{:S(2)}, u32[]{:S(2)}) collective-permute-start(f32[1,16,64,256]{3,2,1,0:T(8,128)S(1)} %multiply_add_fusion.2), channel_id=1, source_target_pairs={{0,16},{16,32},{32,48},{48,64},{64,80},{80,96},{96,112},{112,128},... | collective-permute-start | bytes 3145736 | tf_op jit(solution)/shard_map/while/body/eval_jaxpr/ppermute | solution.py:16
  267.8 16.1 %collective-permute-start = (f32[1,16,64,256]{3,2,1,0:T(8,128)S(1)}, f32[1,16,64,256]{3,2,1,0:T(8,128)S(1)}, u32[]{:S(2)}, u32[]{:S(2)}) collective-permute-start(f32[1,16,64,256]{3,2,1,0:T(8,128)S(1)} %multiply_add_fusion.2), channel_id=1, source_target_pairs={{0,16},{16,32},{32,48},{48,64},{64,80},{80,96},{96,112},{112,128},... | collective-permute-start | bytes 3145736 | tf_op jit(solution)/shard_map/while/body/eval_jaxpr/ppermute | solution.py:16
  284.1 16.1 %collective-permute-start = (f32[1,16,64,256]{3,2,1,0:T(8,128)S(1)}, f32[1,16,64,256]{3,2,1,0:T(8,128)S(1)}, u32[]{:S(2)}, u32[]{:S(2)}) collective-permute-start(f32[1,16,64,256]{3,2,1,0:T(8,128)S(1)} %multiply_add_fusion.2), channel_id=1, source_target_pairs={{0,16},{16,32},{32,48},{48,64},{64,80},{80,96},{96,112},{112,128},... | collective-permute-start | bytes 3145736 | tf_op jit(solution)/shard_map/while/body/eval_jaxpr/ppermute | solution.py:16
  300.4 16.1 %collective-permute-start = (f32[1,16,64,256]{3,2,1,0:T(8,128)S(1)}, f32[1,16,64,256]{3,2,1,0:T(8,128)S(1)}, u32[]{:S(2)}, u32[]{:S(2)}) collective-permute-start(f32[1,16,64,256]{3,2,1,0:T(8,128)S(1)} %multiply_add_fusion.2), channel_id=1, source_target_pairs={{0,16},{16,32},{32,48},{48,64},{64,80},{80,96},{96,112},{112,128},... | collective-permute-start | bytes 3145736 | tf_op jit(solution)/shard_map/while/body/eval_jaxpr/ppermute | solution.py:16
  316.7 16.1 %collective-permute-start = (f32[1,16,64,256]{3,2,1,0:T(8,128)S(1)}, f32[1,16,64,256]{3,2,1,0:T(8,128)S(1)}, u32[]{:S(2)}, u32[]{:S(2)}) collective-permute-start(f32[1,16,64,256]{3,2,1,0:T(8,128)S(1)} %multiply_add_fusion.2), channel_id=1, source_target_pairs={{0,16},{16,32},{32,48},{48,64},{64,80},{80,96},{96,112},{112,128},... | collective-permute-start | bytes 3145736 | tf_op jit(solution)/shard_map/while/body/eval_jaxpr/ppermute | solution.py:16
  333.0 16.1 %collective-permute-start = (f32[1,16,64,256]{3,2,1,0:T(8,128)S(1)}, f32[1,16,64,256]{3,2,1,0:T(8,128)S(1)}, u32[]{:S(2)}, u32[]{:S(2)}) collective-permute-start(f32[1,16,64,256]{3,2,1,0:T(8,128)S(1)} %multiply_add_fusion.2), channel_id=1, source_target_pairs={{0,16},{16,32},{32,48},{48,64},{64,80},{80,96},{96,112},{112,128},... | collective-permute-start | bytes 3145736 | tf_op jit(solution)/shard_map/while/body/eval_jaxpr/ppermute | solution.py:16
  349.3 16.1 %collective-permute-start = (f32[1,16,64,256]{3,2,1,0:T(8,128)S(1)}, f32[1,16,64,256]{3,2,1,0:T(8,128)S(1)}, u32[]{:S(2)}, u32[]{:S(2)}) collective-permute-start(f32[1,16,64,256]{3,2,1,0:T(8,128)S(1)} %multiply_add_fusion.2), channel_id=1, source_target_pairs={{0,16},{16,32},{32,48},{48,64},{64,80},{80,96},{96,112},{112,128},... | collective-permute-start | bytes 3145736 | tf_op jit(solution)/shard_map/while/body/eval_jaxpr/ppermute | solution.py:16
  365.5 16.1 %collective-permute-start = (f32[1,16,64,256]{3,2,1,0:T(8,128)S(1)}, f32[1,16,64,256]{3,2,1,0:T(8,128)S(1)}, u32[]{:S(2)}, u32[]{:S(2)}) collective-permute-start(f32[1,16,64,256]{3,2,1,0:T(8,128)S(1)} %multiply_add_fusion.2), channel_id=1, source_target_pairs={{0,16},{16,32},{32,48},{48,64},{64,80},{80,96},{96,112},{112,128},... | collective-permute-start | bytes 3145736 | tf_op jit(solution)/shard_map/while/body/eval_jaxpr/ppermute | solution.py:16
  381.8 16.1 %collective-permute-start = (f32[1,16,64,256]{3,2,1,0:T(8,128)S(1)}, f32[1,16,64,256]{3,2,1,0:T(8,128)S(1)}, u32[]{:S(2)}, u32[]{:S(2)}) collective-permute-start(f32[1,16,64,256]{3,2,1,0:T(8,128)S(1)} %multiply_add_fusion.2), channel_id=1, source_target_pairs={{0,16},{16,32},{32,48},{48,64},{64,80},{80,96},{96,112},{112,128},... | collective-permute-start | bytes 3145736 | tf_op jit(solution)/shard_map/while/body/eval_jaxpr/ppermute | solution.py:16
  398.1 16.1 %collective-permute-start = (f32[1,16,64,256]{3,2,1,0:T(8,128)S(1)}, f32[1,16,64,256]{3,2,1,0:T(8,128)S(1)}, u32[]{:S(2)}, u32[]{:S(2)}) collective-permute-start(f32[1,16,64,256]{3,2,1,0:T(8,128)S(1)} %multiply_add_fusion.2), channel_id=1, source_target_pairs={{0,16},{16,32},{32,48},{48,64},{64,80},{80,96},{96,112},{112,128},... | collective-permute-start | bytes 3145736 | tf_op jit(solution)/shard_map/while/body/eval_jaxpr/ppermute | solution.py:16
  414.4 16.1 %collective-permute-start = (f32[1,16,64,256]{3,2,1,0:T(8,128)S(1)}, f32[1,16,64,256]{3,2,1,0:T(8,128)S(1)}, u32[]{:S(2)}, u32[]{:S(2)}) collective-permute-start(f32[1,16,64,256]{3,2,1,0:T(8,128)S(1)} %multiply_add_fusion.2), channel_id=1, source_target_pairs={{0,16},{16,32},{32,48},{48,64},{64,80},{80,96},{96,112},{112,128},... | collective-permute-start | bytes 3145736 | tf_op jit(solution)/shard_map/while/body/eval_jaxpr/ppermute | solution.py:16
  430.7 16.1 %collective-permute-start = (f32[1,16,64,256]{3,2,1,0:T(8,128)S(1)}, f32[1,16,64,256]{3,2,1,0:T(8,128)S(1)}, u32[]{:S(2)}, u32[]{:S(2)}) collective-permute-start(f32[1,16,64,256]{3,2,1,0:T(8,128)S(1)} %multiply_add_fusion.2), channel_id=1, source_target_pairs={{0,16},{16,32},{32,48},{48,64},{64,80},{80,96},{96,112},{112,128},... | collective-permute-start | bytes 3145736 | tf_op jit(solution)/shard_map/while/body/eval_jaxpr/ppermute | solution.py:16
where the time goes:
time: 549 us; the launch traced here: 540 us
  waiting for transfers between devices  276 us (50%)
  local copies, waits for them, and re-layouts  65.8 us (12%)
  matrix products  62.5 us (11%)
  blocking collectives  57.6 us (10%)
  starting transfers between devices  48.5 us (9%)
  other arithmetic  28.5 us (5%)
    ppermute x15, waiting for transfers between devices, passed_along(): return lax.ppermute(block, axis, route)  213 us
    all_to_all x1, blocking collectives, local(): lax.all_to_all(mixed_rows, 'head', split_axis=0, concat_axis=1, tiled=True)  57.6 us
    all_to_all x1, waiting for transfers between devices, local(): lax.all_to_all(tokens, 'head', split_axis=1, concat_axis=0, tiled=True)  47.3 us
    ppermute x15, starting transfers between devices, passed_along(): return lax.ppermute(block, axis, route)  28.8 us
    dot_general x8, matrix products, one_block(): jnp.einsum('ghqk,kghp->qghp', weights, value_blk, preferred_element_type=...  26.3 us
    dot_general x8, matrix products, one_block(): jnp.einsum('kghn,kghp->ghpn', b_weighted, value_blk, preferred_element_ty...  22.7 us
    all_to_all x3, local copies, waits for them, and re-layouts, local(): lax.all_to_all(mixed_rows, 'head', split_axis=0, concat_axis=1, tiled=True)  16.7 us
    unnamed x10, local copies, waits for them, and re-layouts  13.2 us
  transfers between devices with their start and end apart: 19, of which 18 were waited for; matrix products, arithmetic and copies ran while one was open for 6% of the time, Pallas kernels for 0%

commit v1 on v0

v1 whole, which is shorter than its diff:
```python
import functools

import jax
import jax.numpy as jnp
from jax import lax
from jax.experimental import pallas as pl
from jax.experimental.pallas import tpu as pltpu
from jax.sharding import PartitionSpec as P

P_SIZE = 64
N = 256
Q = 256
SUB = 64
PARTS = 2
ROWS = 128
HALF = ROWS // 2
HEADS = 16
SLABS = 4
LANES = 128
PIECES = 16
LOG2E = 1.4426950408889634
F32 = jnp.float32
BF16 = jnp.bfloat16
VMEM_LIMIT = 60 * 1024 * 1024


def dot(a, b, dims):
    return lax.dot_general(a, b, (dims, ((), ())), preferred_element_type=F32)


def call(kernel, name, cost, limit=VMEM_LIMIT, **kwargs):
    flops, mib, exps = cost
    return pl.pallas_call(
        kernel,
        name=name,
        compiler_params=pltpu.CompilerParams(vmem_limit_bytes=limit),
        cost_estimate=pl.CostEstimate(
            flops=flops, bytes_accessed=mib * 2**20, transcendentals=exps
        ),
        **kwargs,
    )


def pack_kernel(x_ref, b_ref, c_ref, d_ref, first_ref, second_ref):
    width = second_ref.shape[2]
    turned = jnp.transpose(d_ref[...].astype(F32)).astype(BF16)
    turned = jnp.where(pl.program_id(0) % 2 == 0, turned[: 4 * HEADS], turned[4 * HEADS :])
    for k in range(second_ref.shape[0]):
        cols = slice((k // 2) * N, (k // 2 + 1) * N)
        for part, (out_ref, ref) in enumerate(((first_ref, b_ref), (second_ref, c_ref))):
            at = (PARTS * k + part) * width
            out_ref[k, :ROWS] = x_ref[:, at : at + width]
            out_ref[k, ROWS : ROWS + HALF, :N] = ref[:HALF, cols]
            out_ref[k, ROWS : ROWS + HALF, N:] = ref[HALF:, cols]
        first_ref[k, ROWS + HALF :, :ROWS] = turned[k * HEADS : (k + 1) * HEADS]
        first_ref[k, ROWS + HALF :, ROWS:] = jnp.zeros((HEADS, width - ROWS), BF16)


def pack(tokens, b_proj, c_proj, log_decay, n_head):
    cols = tokens.shape[1]
    width = cols // n_head // PARTS
    heights = (ROWS + HALF + HEADS, ROWS + HALF)
    return call(
        pack_kernel,
        "pack",
        (0, 12, 0),
        grid=(n_head // 4,),
        in_specs=[
            pl.BlockSpec((ROWS, 4 * PARTS * width), lambda i: (0, i)),
            pl.BlockSpec((ROWS, 2 * N), lambda i: (0, i)),
            pl.BlockSpec((ROWS, 2 * N), lambda i: (0, i)),
            pl.BlockSpec((ROWS, ROWS), lambda i: (0, i // 2)),
        ],
        out_specs=[pl.BlockSpec((4, height, width), lambda i: (i, 0, 0)) for height in heights],
        out_shape=[jax.ShapeDtypeStruct((n_head, height, width), BF16) for height in heights],
    )(tokens, b_proj, c_proj, log_decay)


def folded(ref):
    pieces = []
    for k in range(ref.shape[0]):
        pieces += [ref[k, :, :N], ref[k, :, N:]]
    return jnp.concatenate(pieces, axis=0)


def rows_of(ref):
    return jnp.concatenate([ref[k] for k in range(ref.shape[0])], axis=0)


def three(whole):
    high = whole.astype(BF16).astype(F32)
    mid = (whole - high).astype(BF16).astype(F32)
    return high, mid, whole - high - mid


def in_pieces(whole):
    high, mid, low = three(whole)
    row = lax.broadcasted_iota(jnp.int32, (PIECES, whole.shape[1]), 0)
    out = jnp.where(row == 0, high, jnp.where(row == 1, mid, jnp.where(row == 2, low, 0.0)))
    return out.astype(BF16)


def of_pieces(rows):
    return jnp.sum(rows.astype(F32), axis=0, keepdims=True)


def block_sums(d_ref, block):
    turned = jnp.concatenate([d_ref[2 * block], d_ref[2 * block + 1]], axis=1)
    u = lax.broadcasted_iota(jnp.int32, (Q, Q), 0)
    t = lax.broadcasted_iota(jnp.int32, (Q, Q), 1)
    upper = (u <= t).astype(F32).astype(BF16)
    sums = dot(turned, upper, ((1,), (0,))) * LOG2E
    rest = jnp.zeros((LANES - 3 * HEADS, Q), F32)
    return jnp.transpose(jnp.concatenate([*three(sums), rest], axis=0)).astype(BF16)


def spread_sums(part, pieces, width):
    row = lax.broadcasted_iota(jnp.int32, (LANES, width), 0)
    col = lax.broadcasted_iota(jnp.int32, (LANES, width), 1)
    head = col // P_SIZE + part * (HEADS // PARTS)
    taken = jnp.logical_and(row % HEADS == head, row < 3 * HEADS)
    return dot(pieces, taken.astype(F32).astype(BF16), ((1,), (0,)))


def step_of(i, shift):
    return jnp.maximum(i - shift, 0)


def x_spec(width, shift=0):
    return pl.BlockSpec((SLABS, ROWS, width), lambda i: (step_of(i, shift), 0, 0))


def bc_spec(width, shift=0):
    return pl.BlockSpec((SLABS, HALF, width), lambda i: (step_of(i, shift), ROWS // HALF, 0))


def flat_spec(width, shift=0):
    return pl.BlockSpec((SLABS * ROWS, width), lambda i: (step_of(i, shift), 0))


def smem_spec():
    return pl.BlockSpec(memory_space=pltpu.SMEM)


BLOCKS = SLABS * ROWS // Q


def states_kernel(part, *refs):
    if part == 0:
        x_ref, b_ref, d_ref, end_ref, sums_ref, state, total = refs
    else:
        x_ref, b_ref, sums_ref, end_ref, state, total = refs
    step = pl.program_id(0)
    width = x_ref.shape[2]

    @pl.when(step == 0)
    def _():
        state[...] = jnp.zeros_like(state)
        total[...] = jnp.zeros_like(total)

    if part == 0:
        pieces = jnp.concatenate([block_sums(d_ref, k) for k in range(BLOCKS)], axis=0)
        sums_ref[...] = pieces
    else:
        pieces = sums_ref[...]
    s = spread_sums(part, pieces, width)
    later = jnp.zeros((1, width), F32)
    shares = []
    for k in reversed(range(BLOCKS)):
        here = s[k * Q : (k + 1) * Q]
        later = later + here[Q - 1 : Q]
        shares = [jnp.exp2(later - here)] + shares
    xw = (rows_of(x_ref).astype(F32) * jnp.concatenate(shares, axis=0)).astype(BF16)
    state[...] = state[...] * jnp.exp2(later) + dot(folded(b_ref), xw, ((0,), (0,)))
    total[...] += later

    @pl.when(step == pl.num_programs(0) - 1)
    def _():
        end_ref[:N] = state[...].astype(BF16)
        end_ref[N:] = in_pieces(total[...])


def end_states(part, first, msg, sums=None):
    slabs, _, width = first.shape
    shape = (N + PIECES, width)
    at = (ROWS + HALF) // HEADS
    d_spec = pl.BlockSpec((SLABS, HEADS, ROWS), lambda i: (i, at, 0))
    out_specs = [pl.BlockSpec(shape, lambda i: (0, 0))]
    out_shape = [jax.ShapeDtypeStruct(shape, BF16)]
    if part == 0:
        out_specs.append(flat_spec(LANES))
        out_shape.append(jax.ShapeDtypeStruct((slabs * ROWS, LANES), BF16))
    return call(
        functools.partial(states_kernel, part),
        "states%d" % part,
        (2**30, 5, 2**20),
        grid=(slabs // SLABS,),
        in_specs=[x_spec(width), bc_spec(width), d_spec if part == 0 else flat_spec(LANES)],
        out_specs=out_specs,
        out_shape=out_shape,
        scratch_shapes=[pltpu.VMEM((N, width), F32), pltpu.VMEM((1, width), F32)],
    )(msg, first, first if part == 0 else sums)


def gain_row(part, gain_ref, width):
    head = lax.broadcasted_iota(jnp.int32, (1, width), 1) // P_SIZE
    row = jnp.zeros((1, width), F32)
    for h in range(HEADS // PARTS):
        row = jnp.where(head == h, gain_ref[part * (HEADS // PARTS) + h], row)
    return row


def own_tokens(part, x_ref, b_ref, c_ref, sums_ref, gain_ref, state, write):
    width = x_ref.shape[2]
    t = lax.broadcasted_iota(jnp.int32, (Q, Q), 0)
    u = lax.broadcasted_iota(jnp.int32, (Q, Q), 1)
    gain = gain_row(part, gain_ref, width)
    x_all = rows_of(x_ref).astype(F32)
    b_all = folded(b_ref)
    c_all = folded(c_ref)
    s_all = spread_sums(part, sums_ref[...], width)
    for k in range(BLOCKS):
        block = slice(k * Q, (k + 1) * Q)
        xf, b, c, s = x_all[block], b_all[block], c_all[block], s_all[block]
        end = s[Q - 1 : Q]
        scores = jnp.where(t >= u, dot(c, b, ((1,), (1,))), 0.0).astype(BF16)
        before = state[...]
        rest = dot(c, before.astype(BF16), ((1,), (0,))) * jnp.exp2(s) + gain * xf
        state[...] = before * jnp.exp2(end) + dot(
            b, (xf * jnp.exp2(end - s)).astype(BF16), ((0,), (0,))
        )
        for i in range(Q // SUB):
            here = slice(i * SUB, (i + 1) * SUB)
            upto = (i + 1) * SUB
            mid = s[i * SUB + SUB // 2 - 1 : i * SUB + SUB // 2]
            xw = (xf[:upto] * jnp.exp2(mid - s[:upto])).astype(BF16)
            inner = dot(scores[here, :upto], xw, ((1,), (0,))) * jnp.exp2(s[here] - mid)
            write(k * Q + i * SUB, inner + rest[here])


def weigh_ends(me, tail_ref, weights):
    later = jnp.zeros((1, weights.shape[1]), F32)
    for k in reversed(range(tail_ref.shape[0])):
        before = k < me
        weights[k : k + 1] = jnp.where(before, jnp.exp2(later), 0.0)
        later = later + jnp.where(before, of_pieces(tail_ref[k]), 0.0)


def load_start(loads, me_ref, ends_ref, tail_ref, weights, state):
    step = pl.program_id(0)
    rows = ends_ref.shape[1]

    @pl.when(step == 0)
    def _():
        weigh_ends(me_ref[0], tail_ref, weights)

    @pl.when(step < loads)
    def _():
        half = rows // 2
        for j in range(2):
            some = slice(j * half, (j + 1) * half)
            whole = jnp.zeros((half, ends_ref.shape[2]), F32)
            for k in range(ends_ref.shape[0]):
                whole = whole + ends_ref[k, some].astype(F32) * weights[k : k + 1]
            at = pl.multiple_of(step * rows + j * half, half)
            state[pl.ds(at, half), :] = whole.astype(state.dtype)


LOADS = 4


def ends_specs(ends):
    shards, _, width = ends.shape
    rows = N // LOADS
    return [
        pl.BlockSpec((shards, rows, width), lambda i: (0, jnp.minimum(i, LOADS - 1), 0)),
        pl.BlockSpec((shards, PIECES, width), lambda i: (0, N // PIECES, 0)),
    ]


def mix_kernel(part, me_ref, gain_ref, ends_ref, tail_ref, x_ref, b_ref, c_ref, sums_ref, out_ref, state, weights):
    load_start(LOADS, me_ref, ends_ref, tail_ref, weights, state)

    def write(at, rows):
        out_ref[at // ROWS, at % ROWS : at % ROWS + rows.shape[0]] = rows.astype(BF16)

    @pl.when(pl.program_id(0) >= LOADS)
    def _():
        own_tokens(part, x_ref, b_ref, c_ref, sums_ref, gain_ref, state, write)


def mix(part, me, ends, first, second, sums, gains):
    slabs, _, width = first.shape
    return call(
        functools.partial(mix_kernel, part),
        "mix%d" % part,
        (4 * 2**30, 14, 2**22),
        grid=(LOADS + slabs // SLABS,),
        in_specs=[smem_spec()] * 2
        + ends_specs(ends)
        + [
            x_spec(width, LOADS),
            bc_spec(width, LOADS),
            bc_spec(width, LOADS),
            flat_spec(LANES, LOADS),
        ],
        out_specs=x_spec(width, LOADS),
        out_shape=jax.ShapeDtypeStruct((slabs, ROWS, width), BF16),
        scratch_shapes=[pltpu.VMEM((N, width), F32), pltpu.VMEM((ends.shape[0], width), F32)],
    )(me, gains, ends, ends, (first, second)[part], first, second, sums)


def inside_kernel(part, gain_ref, x_ref, b_ref, c_ref, sums_ref, out_ref, state):
    @pl.when(pl.program_id(0) == 0)
    def _():
        state[...] = jnp.zeros_like(state)

    def write(at, rows):
        out_ref[at : at + rows.shape[0]] = rows.astype(out_ref.dtype)

    own_tokens(part, x_ref, b_ref, c_ref, sums_ref, gain_ref, state, write)


def inside(part, first, second, sums, gains):
    slabs, _, width = first.shape
    return call(
        functools.partial(inside_kernel, part),
        "inside%d" % part,
        (4 * 2**30, 14, 2**22),
        grid=(slabs // SLABS,),
        in_specs=[
            smem_spec(),
            x_spec(width),
            bc_spec(width),
            bc_spec(width),
            flat_spec(LANES),
        ],
        out_specs=flat_spec(width),
        out_shape=jax.ShapeDtypeStruct((slabs * ROWS, width), F32),
        scratch_shapes=[pltpu.VMEM((N, width), F32)],
    )(gains, (first, second)[part], first, second, sums)


def join_kernel(part, me_ref, ends_ref, tail_ref, c_ref, sums_ref, own_ref, out_ref, start, weights, total):
    step = pl.program_id(0)
    width = own_ref.shape[1]
    load_start(LOADS, me_ref, ends_ref, tail_ref, weights, start)

    @pl.when(step == 0)
    def _():
        total[...] = jnp.zeros_like(total)

    @pl.when(step >= LOADS)
    def _():
        s = spread_sums(part, sums_ref[...], width)
        outer = dot(folded(c_ref), start[...], ((1,), (0,)))
        since = total[...]
        for k in range(BLOCKS):
            here = s[k * Q : (k + 1) * Q]
            for j in range(Q // ROWS):
                some = slice(j * ROWS, (j + 1) * ROWS)
                at = slice(k * Q + j * ROWS, k * Q + (j + 1) * ROWS)
                out_ref[at.start // ROWS] = (
                    own_ref[at] + outer[at] * jnp.exp2(here[some] + since)
                ).astype(BF16)
            since = since + here[Q - 1 : Q]
        total[...] = since


def join(part, me, ends, first, second, sums, own):
    slabs, _, width = first.shape
    return call(
        functools.partial(join_kernel, part),
        "join%d" % part,
        (2**30, 12, 2**20),
        grid=(LOADS + slabs // SLABS,),
        in_specs=[smem_spec()]
        + ends_specs(ends)
        + [bc_spec(width, LOADS), flat_spec(LANES, LOADS), flat_spec(width, LOADS)],
        out_specs=x_spec(width, LOADS),
        out_shape=jax.ShapeDtypeStruct((slabs, ROWS, width), BF16),
        scratch_shapes=[
            pltpu.VMEM((N, width), BF16),
            pltpu.VMEM((ends.shape[0], width), F32),
            pltpu.VMEM((1, width), F32),
        ],
    )(me, ends, ends, second, sums, own)


def unpack_kernel(part, *refs):
    y_ref, out_ref, sems = refs[0], refs[-2], refs[-1]
    width = y_ref.shape[2]
    copies = []
    for k in range(y_ref.shape[0]):
        at = (PARTS * k + part) * width
        copies.append(
            pltpu.make_async_copy(y_ref.at[k], out_ref.at[:, at : at + width], sems.at[k])
        )
    for copy in copies:
        copy.start()
    for copy in copies:
        copy.wait()


def unpack(part, y, before=()):
    n_head, rows, width = y.shape
    return call(
        functools.partial(unpack_kernel, part),
        "unpack%d" % part,
        (0, 4, 0),
        in_specs=[pl.BlockSpec(memory_space=pltpu.VMEM)]
        + [pl.BlockSpec(memory_space=pl.ANY)] * len(before),
        out_specs=pl.BlockSpec(memory_space=pl.ANY),
        out_shape=jax.ShapeDtypeStruct((rows, n_head * PARTS * width), BF16),
        scratch_shapes=[pltpu.SemaphoreType.DMA((n_head,))],
        input_output_aliases={1: 0} if before else {},
    )(y, *before)


def exchange(msg):
    return lax.all_to_all(msg, "head", split_axis=0, concat_axis=0, tiled=True)


def local(tokens, b_proj, c_proj, log_decay, bypass_gain_vector):
    n_head = lax.axis_size("head")
    me = lax.axis_index("ctx").astype(jnp.int32).reshape(1)
    gains = bypass_gain_vector
    after = lax.optimization_barrier
    packed0, packed1 = pack(tokens, b_proj, c_proj, log_decay, n_head)
    first = exchange(packed0)
    packed1, first = after((packed1, first))
    second = exchange(packed1)
    end0, sums = end_states(0, first, first)
    ends0 = lax.all_gather(end0, "ctx")

    (end1,) = end_states(1, first, second, sums)
    ends1 = lax.all_gather(end1, "ctx")
    second, end1 = after((second, end1))
    mixed0 = mix(0, me, ends0, first, second, sums, gains)
    second, mixed0 = after((second, mixed0))
    y0 = exchange(mixed0)

    own1 = inside(1, first, second, sums, gains)
    mixed1 = join(1, me, ends1, first, second, sums, own1)
    mixed1, y0 = after((mixed1, y0))
    out = unpack(0, y0)
    return unpack(1, exchange(mixed1), (out,))


def solution(mesh):
    rows = P(("ctx", "head"), None)
    return jax.shard_map(
        local,
        mesh=mesh,
        in_specs=(rows, rows, rows, rows, P("head")),
        out_specs=rows,
        check_vma=False,
    )
```

time: 549 us -> 215 us (0.39); the launches traced: 540 us -> 214 us
  waiting for transfers between devices: 276 us -> 47.2 us
  local copies, waits for them, and re-layouts: 65.8 us -> 0.01 us
  matrix products: 62.5 us -> 0 us
  Pallas kernels: 0 us -> 50.7 us
  starting transfers between devices: 48.5 us -> 10.8 us
  blocking collectives: 57.6 us -> 91.6 us
  other arithmetic: 28.5 us -> 0 us
  between operations: 0.22 us -> 13.5 us
    ppermute x15 -> x0, waiting for transfers between devices: 213 us -> none  [passed_along(): return lax.ppermute(block, axis, route)]
    dot_general x25 -> x0, matrix products: 62.5 us -> none  [the longest x8 26.3 us: one_block(): jnp.einsum('ghqk,kghp->qghp', weights, value_blk, preferred_element_type=...]
    pallas_call x0 -> x8, Pallas kernels: none -> 50.7 us  [the longest x2 11.6 us: end_states(): call(functools.partial(states_kernel, part), 'states%d' % part, (2 ** 30,...]
    all_to_all x4 -> x2, waiting for transfers between devices: 63.4 us -> 28 us  [exchange(): return lax.all_to_all(msg, 'head', split_axis=0, concat_axis=0, tiled=True)]
    all_to_all x1 -> x2, blocking collectives: 57.6 us -> 91.6 us  [exchange(): return lax.all_to_all(msg, 'head', split_axis=0, concat_axis=0, tiled=True)]
    ppermute x15 -> x0, starting transfers between devices: 28.8 us -> none  [passed_along(): return lax.ppermute(block, axis, route)]
    all_to_all x4 -> x0, local copies, waits for them, and re-layouts: 23.6 us -> none  [the longest x3 16.7 us: local(): lax.all_to_all(mixed_rows, 'head', split_axis=0, concat_axis=1, tiled=True)]
    all_gather x0 -> x2, waiting for transfers between devices: none -> 19.2 us  [the longest x1 19.1 us: local(): ends1 = lax.all_gather(end1, 'ctx')]
  transfers between devices with their start and end apart: 19 -> 4, of which waited for: 18 -> 2; matrix products, arithmetic and copies ran while one was open for 6% -> 0% of each run, Pallas kernels for 0% -> 17%
where the time goes in v1:
time: 215 us; the launch traced here: 214 us
  blocking collectives  91.6 us (43%)
  Pallas kernels  50.7 us (24%)
  waiting for transfers between devices  47.2 us (22%)
  between operations  13.5 us (6%)
  starting transfers between devices  10.8 us (5%)
    all_to_all x2, blocking collectives, exchange(): return lax.all_to_all(msg, 'head', split_axis=0, concat_axis=0, tiled=True)  91.6 us
    all_to_all x2, waiting for transfers between devices, exchange(): return lax.all_to_all(msg, 'head', split_axis=0, concat_axis=0, tiled=True)  28 us
    all_gather x1, waiting for transfers between devices, local(): ends1 = lax.all_gather(end1, 'ctx')  19.1 us
    pallas_call x2, Pallas kernels, end_states(): call(functools.partial(states_kernel, part), 'states%d' % part, (2 ** 30,...  11.6 us
    all_to_all x2, starting transfers between devices, exchange(): return lax.all_to_all(msg, 'head', split_axis=0, concat_axis=0, tiled=True)  10.7 us
    pallas_call x1, Pallas kernels, mix(): call(functools.partial(mix_kernel, part), 'mix%d' % part, (4 * 2 ** 30, 1...  10.6 us
    pallas_call x1, Pallas kernels, join(): call(functools.partial(join_kernel, part), 'join%d' % part, (2 ** 30, 12,...  8.62 us
    pallas_call x1, Pallas kernels, inside(): call(functools.partial(inside_kernel, part), 'inside%d' % part, (4 * 2 **...  8.22 us
  transfers between devices with their start and end apart: 4, of which 2 were waited for; matrix products, arithmetic and copies ran while one was open for 0% of the time, Pallas kernels for 17%

profile of v1, /device:TPU:32, one launch (start us, length us, event | category | flops | bytes accessed | tf_op | source)
XLA Modules:
  0.0 213.7 jit_solution(5211311500177573384)
XLA Ops:
  6.5 0.0 all-gather.7.cloned.1.call-start
  6.5 5.6 %pack.1 = (bf16[16,208,512]{2,1,0:T(8,128)(2,1)}, bf16[16,192,512]{2,1,0:T(8,128)(2,1)}) custom-call(bf16[128,16384]{1,0:T(8,128)(2,1)} %x_ref.1, bf16[128,2048]{1,0:T(8,128)(2,1)} %b_ref.1, bf16[128,2048]{1,0:T(8,128)(2,1)} %c_ref.1, bf16[128,256]{1,0:T(8,128)(2,1)} %d_ref.1), custom_call_target="tpu_custom_call" | custom-call | bytes 12582912 | tf_op jit(solution)/shard_map/pack/pallas_call | solution.py:63
  12.2 49.6 %all_to_all.20.refs_0_.refs_1_.refs_2_.x_ref.b_ref = bf16[16,208,512]{2,1,0:T(8,128)(2,1)} all-to-all(bf16[16,208,512]{2,1,0:T(8,128)(2,1)} %get-tuple-element.17), channel_id=1, replica_groups=mesh['ctx'=16,'head'=16] {'head'}, dimensions={0} | all-to-all | bytes 6815744 | tf_op jit(solution)/shard_map/all_to_all | solution.py:421
  61.8 0.0 copy-start.1
  61.8 6.2 %states0.1 = (bf16[272,512]{1,0:T(8,128)(2,1)}, bf16[2048,128]{1,0:T(8,128)(2,1)}) custom-call(bf16[16,208,512]{2,1,0:T(8,128)(2,1)} %all_to_all.20.refs_0_.refs_1_.refs_2_.x_ref.b_ref, bf16[16,208,512]{2,1,0:T(8,128)(2,1)} %all_to_all.20.refs_0_.refs_1_.refs_2_.x_ref.b_ref, bf16[16,208,512]{2,1,0:T(8,128)(2,1)} %all_to_all.20.refs_0_.refs_1_.refs_2_.x_ref.b_ref), custom_call_target="tpu_custom_call" | custom-call | flops 1073741824 | bytes 5242880 | tf_op jit(solution)/shard_map/states0/pallas_call | solution.py:193
  68.0 0.0 all-gather.7.cloned.1.call-update
  68.0 0.0 all-gather.5.cloned.1.call-start
  68.0 0.0 copy-done.1
  68.1 42.0 %all_to_all.21.refs_0_.c_ref.x_ref = bf16[16,192,512]{2,1,0:T(8,128)(2,1)} all-to-all(bf16[16,192,512]{2,1,0:T(8,128)(2,1)S(1)} %copy-done.1), channel_id=1, replica_groups=mesh['ctx'=16,'head'=16] {'head'}, dimensions={0} | all-to-all | bytes 6291456 | tf_op jit(solution)/shard_map/all_to_all | solution.py:421
  110.1 5.4 %states1.1 = bf16[272,512]{1,0:T(8,128)(2,1)} custom-call(bf16[16,192,512]{2,1,0:T(8,128)(2,1)} %all_to_all.21.refs_0_.c_ref.x_ref, bf16[16,208,512]{2,1,0:T(8,128)(2,1)} %all_to_all.20.refs_0_.refs_1_.refs_2_.x_ref.b_ref, bf16[2048,128]{1,0:T(8,128)(2,1)} %get-tuple-element.20.refs_2_.sums_ref), custom_call_target="tpu_custom_call" | custom-call | flops 1073741824 | bytes 5242880 | tf_op jit(solution)/shard_map/states1/pallas_call | solution.py:193
  115.4 0.0 all-gather.5.cloned.1.call-update
  115.4 0.0 all-gather.7.cloned.1.call-done
  115.5 10.6 %mix0.1 = bf16[16,128,512]{2,1,0:T(8,128)(2,1)} custom-call(s32[1]{0:T(128)} %bitcast.me_ref, f32[16]{0:T(128)} %gain_ref.3, bf16[16,272,512]{2,1,0:T(8,128)(2,1)} %bitcast.5, bf16[16,272,512]{2,1,0:T(8,128)(2,1)} %bitcast.6, bf16[16,208,512]{2,1,0:T(8,128)(2,1)} %all_to_all.20.refs_0_.refs_1_.refs_2_.x_ref.b_ref, ...), custom_call_target="tpu_custom_call" | custom-call | flops 4294967296 | bytes 14680064 | tf_op jit(solution)/shard_map/mix0/pallas_call | solution.py:294
  126.1 4.0 %all-to-all-start.2 = ((bf16[16,128,512]{2,1,0:T(8,128)(2,1)}), bf16[16,128,512]{2,1,0:T(8,128)(2,1)S(1)}, u32[]{:S(2)}, u32[]{:S(2)}) async-start(bf16[16,128,512]{2,1,0:T(8,128)(2,1)} %mix0.1), calls=%async_computation.2 | async-start | bytes 4194304 | tf_op jit(solution)/shard_map/all_to_all | solution.py:421
  130.1 8.2 %inside1.1.own_ref = f32[2048,512]{1,0:T(8,128)} custom-call(f32[16]{0:T(128)} %gain_ref.3, bf16[16,192,512]{2,1,0:T(8,128)(2,1)} %all_to_all.21.refs_0_.c_ref.x_ref, bf16[16,208,512]{2,1,0:T(8,128)(2,1)} %all_to_all.20.refs_0_.refs_1_.refs_2_.x_ref.b_ref, bf16[16,192,512]{2,1,0:T(8,128)(2,1)} %all_to_all.21.refs_0_.c_ref.x_ref, ...), custom_call_target="tpu_custom_call" | custom-call | flops 4294967296 | bytes 14680064 | tf_op jit(solution)/shard_map/inside1/pallas_call | solution.py:326
  138.4 19.1 %all-gather.5.cloned.1.call-done = bf16[4352,512]{1,0:T(8,128)(2,1)} async-done(((bf16[272,512]{1,0:T(8,128)(2,1)}), bf16[4352,512]{1,0:T(8,128)(2,1)}) %all-gather.5.cloned.1.call-update) | async-done | bytes 4456464 | tf_op jit(solution)/shard_map/all_gather | solution.py:437
  157.5 8.6 %join1.1 = bf16[16,128,512]{2,1,0:T(8,128)(2,1)} custom-call(s32[1]{0:T(128)} %bitcast.me_ref, bf16[16,272,512]{2,1,0:T(8,128)(2,1)} %bitcast.3, bf16[16,272,512]{2,1,0:T(8,128)(2,1)} %bitcast.4, bf16[16,192,512]{2,1,0:T(8,128)(2,1)} %all_to_all.21.refs_0_.c_ref.x_ref, bf16[2048,128]{1,0:T(8,128)(2,1)} %get-tuple-element.20.refs_2_.sums_ref, ...), custom_call_target="tpu_custom_call" | custom-call | flops 1073741824 | bytes 12582912 | tf_op jit(solution)/shard_map/join1/pallas_call | solution.py:372
  166.1 0.0 all-to-all-done.2.refs_0_
  166.1 0.0 copy-start
  166.1 6.7 %all-to-all-start.3 = ((bf16[16,128,512]{2,1,0:T(8,128)(2,1)}), bf16[16,128,512]{2,1,0:T(8,128)(2,1)}, u32[]{:S(2)}, u32[]{:S(2)}) async-start(bf16[16,128,512]{2,1,0:T(8,128)(2,1)} %join1.1), calls=%async_computation.3 | async-start | bytes 4194304 | tf_op jit(solution)/shard_map/all_to_all | solution.py:421
  172.8 0.0 copy-done
  172.9 3.0 %unpack0.1.refs_1_ = bf16[128,16384]{1,0:T(8,128)(2,1)} custom-call(bf16[16,128,512]{2,1,0:T(8,128)(2,1)} %copy-done), custom_call_target="tpu_custom_call" | custom-call | bytes 4194304 | tf_op jit(solution)/shard_map/unpack0/pallas_call | solution.py:407
  175.9 28.0 %all-to-all-done.3.refs_0_ = bf16[16,128,512]{2,1,0:T(8,128)(2,1)} async-done(((bf16[16,128,512]{2,1,0:T(8,128)(2,1)}), bf16[16,128,512]{2,1,0:T(8,128)(2,1)}, u32[]{:S(2)}, u32[]{:S(2)}) %all-to-all-start.3) | async-done | bytes 2097184 | tf_op jit(solution)/shard_map/all_to_all | solution.py:421
  203.8 3.0 %unpack1.1 = bf16[128,16384]{1,0:T(8,128)(2,1)} custom-call(bf16[16,128,512]{2,1,0:T(8,128)(2,1)} %all-to-all-done.3.refs_0_, bf16[128,16384]{1,0:T(8,128)(2,1)} %unpack0.1.refs_1_), custom_call_target="tpu_custom_call", output_to_operand_aliasing={{}: (1, {})} | custom-call | bytes 4194304 | tf_op jit(solution)/shard_map/unpack1/pallas_call | solution.py:407
Async XLA Ops:
  6.5 108.9 %all-gather.7.cloned.1.call-start = ((), (), s32[]{:S(2)}) async-start(), calls=%async_computation.5 | async-start | bytes 4734976 | tf_op jit(solution)/shard_map/all_gather | solution.py:434
  61.8 6.3 %copy-start.1 = (bf16[16,192,512]{2,1,0:T(8,128)(2,1)S(1)}, bf16[16,192,512]{2,1,0:T(8,128)(2,1)}, u32[]{:S(2)}) copy-start(bf16[16,192,512]{2,1,0:T(8,128)(2,1)} %get-tuple-element.18) | copy-start | bytes 9437188
  68.0 89.5 %all-gather.5.cloned.1.call-start = ((), (), s32[]{:S(2)}) async-start(), calls=%async_computation.4 | async-start | bytes 4734976 | tf_op jit(solution)/shard_map/all_gather | solution.py:437
  126.1 40.0 %all-to-all-start.2 = ((bf16[16,128,512]{2,1,0:T(8,128)(2,1)}), bf16[16,128,512]{2,1,0:T(8,128)(2,1)S(1)}, u32[]{:S(2)}, u32[]{:S(2)}) async-start(bf16[16,128,512]{2,1,0:T(8,128)(2,1)} %mix0.1), calls=%async_computation.2 | async-start | bytes 4194304 | tf_op jit(solution)/shard_map/all_to_all | solution.py:421
  166.1 6.7 %copy-start = (bf16[16,128,512]{2,1,0:T(8,128)(2,1)}, bf16[16,128,512]{2,1,0:T(8,128)(2,1)S(1)}, u32[]{:S(2)}) copy-start(bf16[16,128,512]{2,1,0:T(8,128)(2,1)S(1)} %all-to-all-done.2.refs_0_) | copy-start | bytes 6291460
  166.1 37.7 %all-to-all-start.3 = ((bf16[16,128,512]{2,1,0:T(8,128)(2,1)}), bf16[16,128,512]{2,1,0:T(8,128)(2,1)}, u32[]{:S(2)}, u32[]{:S(2)}) async-start(bf16[16,128,512]{2,1,0:T(8,128)(2,1)} %join1.1), calls=%async_computation.3 | async-start | bytes 4194304 | tf_op jit(solution)/shard_map/all_to_all | solution.py:421
Sparse Core Ops, SparseCore 0:
  68.1 41.5 all-gather.6
  115.6 41.8 all-gather.4

commit v2 on v1

v2 whole, which is shorter than its diff:
```python
import functools

import jax
import jax.numpy as jnp
from jax import lax
from jax.experimental import pallas as pl
from jax.experimental.pallas import tpu as pltpu
from jax.sharding import PartitionSpec as P

P_SIZE = 64
N = 256
Q = 256
SUB = 64
PART_HEADS = (10, 6)
ROWS = 128
HALF = ROWS // 2
HEADS = 16
SLABS = 4
LANES = 128
PIECES = 16
CORES = 2
LOG2E = 1.4426950408889634
F32 = jnp.float32
BF16 = jnp.bfloat16
VMEM_LIMIT = 60 * 1024 * 1024


def dot(a, b, dims):
    return lax.dot_general(a, b, (dims, ((), ())), preferred_element_type=F32)


def call(kernel, name, cost, limit=VMEM_LIMIT, **kwargs):
    flops, mib, exps = cost
    return pl.pallas_call(
        kernel,
        name=name,
        compiler_params=pltpu.CompilerParams(vmem_limit_bytes=limit),
        cost_estimate=pl.CostEstimate(
            flops=flops, bytes_accessed=mib * 2**20, transcendentals=exps
        ),
        **kwargs,
    )


def first_head(part):
    return sum(PART_HEADS[:part])


def pack_kernel(x_ref, b_ref, c_ref, d_ref, first_ref, second_ref):
    dests, _, wide = first_ref.shape
    narrow = second_ref.shape[2]
    turned = jnp.transpose(d_ref[...].astype(F32)).astype(BF16)
    turned = jnp.where(pl.program_id(0) % 2 == 0, turned[: 4 * HEADS], turned[4 * HEADS :])
    low, high = slice(0, LANES), slice(LANES, 2 * LANES)
    for k in range(dests):
        cols = slice((k // 2) * N, (k // 2 + 1) * N)
        at = k * (wide + narrow)
        first_ref[k, :ROWS] = x_ref[:, at : at + wide]
        first_ref[k, ROWS:, :N] = b_ref[:HALF, cols]
        first_ref[k, ROWS:, N : 2 * N] = b_ref[HALF:, cols]
        first_ref[k, ROWS : ROWS + HEADS, 2 * N :] = turned[k * HEADS : (k + 1) * HEADS]
        first_ref[k, ROWS + HEADS :, 2 * N :] = jnp.zeros((HALF - HEADS, LANES), BF16)
        second_ref[k, :ROWS] = x_ref[:, at + wide : at + wide + narrow]
        second_ref[k, ROWS : ROWS + HALF, :N] = c_ref[:HALF, cols]
        rest = c_ref[HALF:, cols]
        second_ref[k, ROWS : ROWS + HALF, N:] = rest[:, low]
        second_ref[k, ROWS + HALF :, low] = rest[: HALF // 2, high]
        second_ref[k, ROWS + HALF :, high] = rest[HALF // 2 :, high]
        second_ref[k, ROWS + HALF :, N:] = jnp.zeros((HALF // 2, LANES), BF16)


def pack(tokens, b_proj, c_proj, log_decay, n_head):
    cols = tokens.shape[1]
    widths = [heads * P_SIZE for heads in PART_HEADS]
    heights = (ROWS + HALF, ROWS + HALF + HALF // 2)
    shapes = list(zip(heights, widths))
    return call(
        pack_kernel,
        "pack",
        (0, 12, 0),
        grid=(n_head // 4,),
        in_specs=[
            pl.BlockSpec((ROWS, 4 * cols // n_head), lambda i: (0, i)),
            pl.BlockSpec((ROWS, 2 * N), lambda i: (0, i)),
            pl.BlockSpec((ROWS, 2 * N), lambda i: (0, i)),
            pl.BlockSpec((ROWS, ROWS), lambda i: (0, i // 2)),
        ],
        out_specs=[pl.BlockSpec((4,) + shape, lambda i: (i, 0, 0)) for shape in shapes],
        out_shape=[jax.ShapeDtypeStruct((n_head,) + shape, BF16) for shape in shapes],
    )(tokens, b_proj, c_proj, log_decay)


def b_rows(ref):
    pieces = []
    for k in range(ref.shape[0]):
        pieces += [ref[k, :, :N], ref[k, :, N:]]
    return jnp.concatenate(pieces, axis=0)


def c_rows(ref, more_ref):
    pieces = []
    for k in range(ref.shape[0]):
        rest = jnp.concatenate([more_ref[k, :, :LANES], more_ref[k, :, LANES:N]], axis=0)
        pieces += [ref[k, :, :N], jnp.concatenate([ref[k, :, N:], rest], axis=1)]
    return jnp.concatenate(pieces, axis=0)


def rows_of(ref):
    return jnp.concatenate([ref[k] for k in range(ref.shape[0])], axis=0)


def three(whole):
    high = whole.astype(BF16).astype(F32)
    mid = (whole - high).astype(BF16).astype(F32)
    return high, mid, whole - high - mid


def in_pieces(whole):
    high, mid, low = three(whole)
    row = lax.broadcasted_iota(jnp.int32, (PIECES, whole.shape[1]), 0)
    out = jnp.where(row == 0, high, jnp.where(row == 1, mid, jnp.where(row == 2, low, 0.0)))
    return out.astype(BF16)


def of_pieces(rows):
    return jnp.sum(rows.astype(F32), axis=0, keepdims=True)


def block_sums(d_ref, block):
    turned = jnp.concatenate([d_ref[2 * block], d_ref[2 * block + 1]], axis=1)
    u = lax.broadcasted_iota(jnp.int32, (Q, Q), 0)
    t = lax.broadcasted_iota(jnp.int32, (Q, Q), 1)
    upper = (u <= t).astype(F32).astype(BF16)
    sums = dot(turned, upper, ((1,), (0,))) * LOG2E
    rest = jnp.zeros((LANES - 3 * HEADS, Q), F32)
    return jnp.transpose(jnp.concatenate([*three(sums), rest], axis=0)).astype(BF16)


def spread_sums(part, pieces, width):
    row = lax.broadcasted_iota(jnp.int32, (LANES, width), 0)
    col = lax.broadcasted_iota(jnp.int32, (LANES, width), 1)
    head = col // P_SIZE + first_head(part)
    taken = jnp.logical_and(row % HEADS == head, row < 3 * HEADS)
    return dot(pieces, taken.astype(F32).astype(BF16), ((1,), (0,)))


def step_of(i, shift):
    return jnp.maximum(i - shift, 0)


def x_spec(width, shift=0):
    return pl.BlockSpec((SLABS, ROWS, width), lambda i: (step_of(i, shift), 0, 0))


def b_spec(shift=0):
    return pl.BlockSpec((SLABS, HALF, 2 * N), lambda i: (step_of(i, shift), ROWS // HALF, 0))


def c_specs(shift=0):
    width = PART_HEADS[1] * P_SIZE
    return [
        pl.BlockSpec((SLABS, HALF, width), lambda i: (step_of(i, shift), ROWS // HALF, 0)),
        pl.BlockSpec(
            (SLABS, HALF // 2, width),
            lambda i: (step_of(i, shift), 2 * (ROWS + HALF) // HALF, 0),
        ),
    ]


def flat_spec(width, shift=0):
    return pl.BlockSpec((SLABS * ROWS, width), lambda i: (step_of(i, shift), 0))


def smem_spec():
    return pl.BlockSpec(memory_space=pltpu.SMEM)


BLOCKS = SLABS * ROWS // Q


def states_kernel(part, *refs):
    if part == 0:
        core_ref, x_ref, b_ref, d_ref, keep_ref, send_ref, sums_ref, state, total = refs
    else:
        core_ref, x_ref, b_ref, sums_ref, keep_ref, send_ref, state, total = refs
    step = pl.program_id(0)
    width = x_ref.shape[2]

    @pl.when(step == 0)
    def _():
        state[...] = jnp.zeros_like(state)
        total[...] = jnp.zeros_like(total)

    if part == 0:
        pieces = jnp.concatenate([block_sums(d_ref, k) for k in range(BLOCKS)], axis=0)
        sums_ref[...] = pieces
    else:
        pieces = sums_ref[...]
    s = spread_sums(part, pieces, width)
    later = jnp.zeros((1, width), F32)
    shares = []
    for k in reversed(range(BLOCKS)):
        here = s[k * Q : (k + 1) * Q]
        later = later + here[Q - 1 : Q]
        shares = [jnp.exp2(later - here)] + shares
    xw = (rows_of(x_ref).astype(F32) * jnp.concatenate(shares, axis=0)).astype(BF16)
    state[...] = state[...] * jnp.exp2(later) + dot(b_rows(b_ref), xw, ((0,), (0,)))
    total[...] += later

    @pl.when(step == pl.num_programs(0) - 1)
    def _():
        pieces = in_pieces(total[...])
        top, low = state[: N // 2], state[N // 2 :]
        first = core_ref[0] == 0
        keep_ref[: N // 2] = jnp.where(first, top, low).astype(BF16)
        send_ref[: N // 2] = jnp.where(first, low, top).astype(BF16)
        keep_ref[N // 2 :] = pieces
        send_ref[N // 2 :] = pieces


def end_states(part, core, first, msg, sums=None):
    slabs, _, width = msg.shape
    shape = (N // 2 + PIECES, width)
    d_spec = pl.BlockSpec((SLABS, HEADS, LANES), lambda i: (i, ROWS // HEADS, 2 * N // LANES))
    out_specs = [pl.BlockSpec(shape, lambda i: (0, 0))] * 2
    out_shape = [jax.ShapeDtypeStruct(shape, BF16)] * 2
    if part == 0:
        out_specs.append(flat_spec(LANES))
        out_shape.append(jax.ShapeDtypeStruct((slabs * ROWS, LANES), BF16))
    return call(
        functools.partial(states_kernel, part),
        "states%d" % part,
        (2**30, 5, 2**20),
        grid=(slabs // SLABS,),
        in_specs=[
            smem_spec(),
            x_spec(width),
            b_spec(),
            d_spec if part == 0 else flat_spec(LANES),
        ],
        out_specs=out_specs,
        out_shape=out_shape,
        scratch_shapes=[pltpu.VMEM((N, width), F32), pltpu.VMEM((1, width), F32)],
    )(core, msg, first, first if part == 0 else sums)


def halves(core_ref, keep_ref, got_ref):
    first = core_ref[0] == 0
    keep, got = keep_ref[...].astype(F32), got_ref[...].astype(F32)
    early, late = jnp.where(first, keep, got), jnp.where(first, got, keep)
    rows = N // 2
    return early[:rows], of_pieces(early[rows:]), late[:rows], of_pieces(late[rows:])


def chip_kernel(core_ref, keep_ref, got_ref, out_ref):
    early, early_total, late, late_total = halves(core_ref, keep_ref, got_ref)
    out_ref[: N // 2] = (early * jnp.exp2(late_total) + late).astype(BF16)
    out_ref[N // 2 :] = in_pieces(early_total + late_total)


def chip_state(part, core, keep, got):
    return call(
        chip_kernel,
        "chip%d" % part,
        (2**18, 1, 0),
        limit=16 * 1024 * 1024,
        in_specs=[smem_spec()] + [pl.BlockSpec(memory_space=pltpu.VMEM)] * 2,
        out_specs=pl.BlockSpec(memory_space=pltpu.VMEM),
        out_shape=jax.ShapeDtypeStruct(keep.shape, BF16),
    )(core, keep, got)


def start_kernel(core_ref, chip_ref, keep_ref, got_ref, *refs):
    mine_ref, theirs_ref, state = refs[-3:]
    others = refs[:-3]
    state[...] = jnp.zeros_like(state)
    for k in reversed(range(len(others))):

        @pl.when(k + 1 <= chip_ref[0])
        def _():
            ref = others[k]
            state[...] = state[...] * jnp.exp2(of_pieces(ref[N // 2 :])) + ref[: N // 2].astype(F32)

    early, early_total, _, _ = halves(core_ref, keep_ref, got_ref)
    before = state[...]
    after = before * jnp.exp2(early_total) + early
    first = core_ref[0] == 0
    mine_ref[...] = jnp.where(first, before, after).astype(BF16)
    theirs_ref[...] = jnp.where(first, after, before).astype(BF16)


def start_state(part, core, chip, keep, got, others):
    shape = (N // 2, keep.shape[1])
    vmem = pl.BlockSpec(memory_space=pltpu.VMEM)
    return call(
        start_kernel,
        "start%d" % part,
        (2**20, 2, 0),
        limit=16 * 1024 * 1024,
        in_specs=[smem_spec()] * 2 + [vmem] * (2 + len(others)),
        out_specs=[vmem] * 2,
        out_shape=[jax.ShapeDtypeStruct(shape, BF16)] * 2,
        scratch_shapes=[pltpu.VMEM(shape, F32)],
    )(core, chip, keep, got, *others)


def incoming(part, core, chip, keep, send, beside=None):
    shards = lax.axis_size("ctx")
    swap = [(i, i ^ 1) for i in range(shards)]
    ahead = [(i, (i + CORES) % shards) for i in range(shards)]
    back = [(i, (i - CORES) % shards) for i in range(shards)]
    got = lax.ppermute(send, "ctx", swap)
    own = chip_state(part, core, keep, got)
    chips = shards // CORES
    forward, backward = [own], [own]
    for step in range(chips // 2):
        forward.append(lax.ppermute(forward[-1], "ctx", ahead))
        if step < chips - 1 - chips // 2:
            backward.append(lax.ppermute(backward[-1], "ctx", back))
        if step == 0 and beside is not None:
            forward[-1], backward[-1], beside = lax.optimization_barrier(
                (forward[-1], backward[-1], beside)
            )
    mine, theirs = start_state(part, core, chip, keep, got, forward[1:] + backward[:0:-1])
    return mine, lax.ppermute(theirs, "ctx", swap), beside


def gain_row(part, gain_ref, width):
    head = lax.broadcasted_iota(jnp.int32, (1, width), 1) // P_SIZE
    row = jnp.zeros((1, width), F32)
    for h in range(PART_HEADS[part]):
        row = jnp.where(head == h, gain_ref[first_head(part) + h], row)
    return row


def own_tokens(part, x_ref, b_ref, c_refs, sums_ref, gain_ref, state, write):
    width = x_ref.shape[2]
    t = lax.broadcasted_iota(jnp.int32, (Q, Q), 0)
    u = lax.broadcasted_iota(jnp.int32, (Q, Q), 1)
    gain = gain_row(part, gain_ref, width)
    x_all = rows_of(x_ref).astype(F32)
    b_all = b_rows(b_ref)
    c_all = c_rows(*c_refs)
    s_all = spread_sums(part, sums_ref[...], width)
    for k in range(BLOCKS):
        block = slice(k * Q, (k + 1) * Q)
        xf, b, c, s = x_all[block], b_all[block], c_all[block], s_all[block]
        end = s[Q - 1 : Q]
        scores = jnp.where(t >= u, dot(c, b, ((1,), (1,))), 0.0).astype(BF16)
        before = state[...]
        rest = dot(c, before.astype(BF16), ((1,), (0,))) * jnp.exp2(s) + gain * xf
        state[...] = before * jnp.exp2(end) + dot(
            b, (xf * jnp.exp2(end - s)).astype(BF16), ((0,), (0,))
        )
        for i in range(Q // SUB):
            here = slice(i * SUB, (i + 1) * SUB)
            upto = (i + 1) * SUB
            mid = s[i * SUB + SUB // 2 - 1 : i * SUB + SUB // 2]
            xw = (xf[:upto] * jnp.exp2(mid - s[:upto])).astype(BF16)
            inner = dot(scores[here, :upto], xw, ((1,), (0,))) * jnp.exp2(s[here] - mid)
            write(k * Q + i * SUB, inner + rest[here])


def start_from(core_ref, mine_ref, got_ref, state):
    @pl.when(pl.program_id(0) == 0)
    def _():
        first = core_ref[0] == 0
        mine, got = mine_ref[...].astype(F32), got_ref[...].astype(F32)
        state[: N // 2] = jnp.where(first, mine, got).astype(state.dtype)
        state[N // 2 :] = jnp.where(first, got, mine).astype(state.dtype)


def half_spec(width):
    return pl.BlockSpec((N // 2, width), lambda i: (0, 0))


def mix_kernel(
    part, core_ref, gain_ref, mine_ref, got_ref, x_ref, b_ref, c_ref, more_ref, sums_ref, out_ref, state
):
    start_from(core_ref, mine_ref, got_ref, state)

    def write(at, rows):
        out_ref[at // ROWS, at % ROWS : at % ROWS + rows.shape[0]] = rows.astype(BF16)

    own_tokens(part, x_ref, b_ref, (c_ref, more_ref), sums_ref, gain_ref, state, write)


def mix(part, core, mine, got, first, second, sums, gains):
    slabs, _, width = (first, second)[part].shape
    return call(
        functools.partial(mix_kernel, part),
        "mix%d" % part,
        (4 * 2**30, 14, 2**22),
        grid=(slabs // SLABS,),
        in_specs=[smem_spec()] * 2
        + [half_spec(width)] * 2
        + [x_spec(width), b_spec(), *c_specs(), flat_spec(LANES)],
        out_specs=x_spec(width),
        out_shape=jax.ShapeDtypeStruct((slabs, ROWS, width), BF16),
        scratch_shapes=[pltpu.VMEM((N, width), F32)],
    )(core, gains, mine, got, (first, second)[part], first, second, second, sums)


def inside_kernel(part, gain_ref, x_ref, b_ref, c_ref, more_ref, sums_ref, out_ref, state):
    @pl.when(pl.program_id(0) == 0)
    def _():
        state[...] = jnp.zeros_like(state)

    def write(at, rows):
        out_ref[at : at + rows.shape[0]] = rows.astype(out_ref.dtype)

    own_tokens(part, x_ref, b_ref, (c_ref, more_ref), sums_ref, gain_ref, state, write)


def inside(part, first, second, sums, gains):
    slabs, _, width = (first, second)[part].shape
    return call(
        functools.partial(inside_kernel, part),
        "inside%d" % part,
        (4 * 2**30, 14, 2**22),
        grid=(slabs // SLABS,),
        in_specs=[
            smem_spec(),
            x_spec(width),
            b_spec(),
            *c_specs(),
            flat_spec(LANES),
        ],
        out_specs=flat_spec(width),
        out_shape=jax.ShapeDtypeStruct((slabs * ROWS, width), BF16),
        scratch_shapes=[pltpu.VMEM((N, width), F32)],
    )(gains, (first, second)[part], first, second, second, sums)


def join_kernel(
    part, core_ref, mine_ref, got_ref, c_ref, more_ref, sums_ref, own_ref, out_ref, start, total
):
    width = own_ref.shape[1]
    start_from(core_ref, mine_ref, got_ref, start)

    @pl.when(pl.program_id(0) == 0)
    def _():
        total[...] = jnp.zeros_like(total)

    s = spread_sums(part, sums_ref[...], width)
    outer = dot(c_rows(c_ref, more_ref), start[...], ((1,), (0,)))
    since = total[...]
    for k in range(BLOCKS):
        here = s[k * Q : (k + 1) * Q]
        for j in range(Q // ROWS):
            some = slice(j * ROWS, (j + 1) * ROWS)
            at = slice(k * Q + j * ROWS, k * Q + (j + 1) * ROWS)
            out_ref[at.start // ROWS] = (
                own_ref[at].astype(F32) + outer[at] * jnp.exp2(here[some] + since)
            ).astype(BF16)
        since = since + here[Q - 1 : Q]
    total[...] = since


def join(part, core, mine, got, first, second, sums, own):
    slabs, _, width = (first, second)[part].shape
    return call(
        functools.partial(join_kernel, part),
        "join%d" % part,
        (2**30, 8, 2**20),
        grid=(slabs // SLABS,),
        in_specs=[smem_spec()]
        + [half_spec(width)] * 2
        + [*c_specs(), flat_spec(LANES), flat_spec(width)],
        out_specs=x_spec(width),
        out_shape=jax.ShapeDtypeStruct((slabs, ROWS, width), BF16),
        scratch_shapes=[pltpu.VMEM((N, width), BF16), pltpu.VMEM((1, width), F32)],
    )(core, mine, got, second, second, sums, own)


def unpack_kernel(part, *refs):
    y_ref, out_ref, sems = refs[0], refs[-2], refs[-1]
    width = y_ref.shape[2]
    copies = []
    for k in range(y_ref.shape[0]):
        at = (k * HEADS + first_head(part)) * P_SIZE
        copies.append(
            pltpu.make_async_copy(y_ref.at[k], out_ref.at[:, at : at + width], sems.at[k])
        )
    for copy in copies:
        copy.start()
    for copy in copies:
        copy.wait()


def unpack(part, y, before=()):
    n_head, rows, width = y.shape
    return call(
        functools.partial(unpack_kernel, part),
        "unpack%d" % part,
        (0, 4, 0),
        limit=16 * 1024 * 1024,
        in_specs=[pl.BlockSpec(memory_space=pltpu.VMEM)]
        + [pl.BlockSpec(memory_space=pl.ANY)] * len(before),
        out_specs=pl.BlockSpec(memory_space=pl.ANY),
        out_shape=jax.ShapeDtypeStruct((rows, n_head * HEADS * P_SIZE), BF16),
        scratch_shapes=[pltpu.SemaphoreType.DMA((n_head,))],
        input_output_aliases={1: 0} if before else {},
    )(y, *before)


def exchange(msg):
    return lax.all_to_all(msg, "head", split_axis=0, concat_axis=0, tiled=True)


def local(tokens, b_proj, c_proj, log_decay, bypass_gain_vector):
    n_head = lax.axis_size("head")
    me = lax.axis_index("ctx").astype(jnp.int32).reshape(1)
    core, chip = me % CORES, me // CORES
    gains = bypass_gain_vector
    after = lax.optimization_barrier
    packed0, packed1 = pack(tokens, b_proj, c_proj, log_decay, n_head)
    first = exchange(packed0)
    packed1, first = after((packed1, first))
    second = exchange(packed1)
    keep0, send0, sums = end_states(0, core, first, first)
    mine0, got0, _ = incoming(0, core, chip, keep0, send0)
    mixed0 = mix(0, core, mine0, got0, first, second, sums, gains)
    second, mixed0 = after((second, mixed0))
    y0 = exchange(mixed0)

    keep1, send1 = end_states(1, core, first, second, sums)
    own1 = inside(1, first, second, sums, gains)
    mine1, got1, own1 = incoming(1, core, chip, keep1, send1, own1)
    mixed1 = join(1, core, mine1, got1, first, second, sums, own1)
    mixed1, y0 = after((mixed1, y0))
    out = unpack(0, y0)
    return unpack(1, exchange(mixed1), (out,))


def solution(mesh):
    rows = P(("ctx", "head"), None)
    return jax.shard_map(
        local,
        mesh=mesh,
        in_specs=(rows, rows, rows, rows, P("head")),
        out_specs=rows,
        check_vma=False,
    )
```

time: 215 us -> 204 us (0.949)
  blocking collectives: 91.6 us -> 55.3 us
  starting transfers between devices: 10.8 us -> 36.7 us
  between operations: 13.5 us -> 0.3 us
  waiting for transfers between devices: 47.2 us -> 60.3 us
  Pallas kernels: 50.7 us -> 43 us
  local copies, waits for them, and re-layouts: 0.01 us -> 5.33 us
    ppermute x0 -> x18, waiting for transfers between devices: none -> 37.4 us  [the longest x8 29.8 us: incoming(): forward.append(lax.ppermute(forward[-1], 'ctx', ahead))]
    all_to_all x2 -> x1, blocking collectives: 91.6 us -> 55.3 us  [exchange(): return lax.all_to_all(msg, 'head', split_axis=0, concat_axis=0, tiled=True)]
    all_gather x2 -> x0, waiting for transfers between devices: 19.2 us -> none  [the longest x1 19.1 us: local(): ends1 = lax.all_gather(end1, 'ctx')]
    ppermute x0 -> x18, starting transfers between devices: none -> 18.4 us  [the longest x6 14 us: incoming(): backward.append(lax.ppermute(backward[-1], 'ctx', back))]
    all_to_all x2 -> x3, starting transfers between devices: 10.7 us -> 18.3 us  [exchange(): return lax.all_to_all(msg, 'head', split_axis=0, concat_axis=0, tiled=True)]
    unnamed x4 -> x16, local copies, waits for them, and re-layouts: 0.01 us -> 5.33 us
    all_to_all x2 -> x3, waiting for transfers between devices: 28 us -> 22.8 us  [exchange(): return lax.all_to_all(msg, 'head', split_axis=0, concat_axis=0, tiled=True)]
    pallas_call x1 -> x5, Pallas kernels: 8.62 us -> 5.34 us  [the longest x1 4.78 us: join(): call(functools.partial(join_kernel, part), 'join%d' % part, (2 ** 30, 8,...]
  transfers between devices with their start and end apart: 4 -> 21, of which waited for: 2 -> 16; matrix products, arithmetic and copies ran while one was open for 0% -> 0% of each run, Pallas kernels for 17% -> 13%
where the time goes in v2:
time: 204 us; the launch traced here: 201 us
  waiting for transfers between devices  60.3 us (30%)
  blocking collectives  55.3 us (27%)
  Pallas kernels  43 us (21%)
  starting transfers between devices  36.7 us (18%)
  local copies, waits for them, and re-layouts  5.33 us (3%)
    all_to_all x1, blocking collectives, exchange(): return lax.all_to_all(msg, 'head', split_axis=0, concat_axis=0, tiled=True)  55.3 us
    ppermute x8, waiting for transfers between devices, incoming(): forward.append(lax.ppermute(forward[-1], 'ctx', ahead))  29.8 us
    all_to_all x3, waiting for transfers between devices, exchange(): return lax.all_to_all(msg, 'head', split_axis=0, concat_axis=0, tiled=True)  22.8 us
    all_to_all x3, starting transfers between devices, exchange(): return lax.all_to_all(msg, 'head', split_axis=0, concat_axis=0, tiled=True)  18.3 us
    ppermute x6, starting transfers between devices, incoming(): backward.append(lax.ppermute(backward[-1], 'ctx', back))  14 us
    pallas_call x2, Pallas kernels, end_states(): call(functools.partial(states_kernel, part), 'states%d' % part, (2 ** 30,...  11.4 us
    pallas_call x1, Pallas kernels, mix(): call(functools.partial(mix_kernel, part), 'mix%d' % part, (4 * 2 ** 30, 1...  9.39 us
    pallas_call x1, Pallas kernels, inside(): call(functools.partial(inside_kernel, part), 'inside%d' % part, (4 * 2 **...  6.86 us
  transfers between devices with their start and end apart: 21, of which 16 were waited for; matrix products, arithmetic and copies ran while one was open for 0% of the time, Pallas kernels for 13%

profile of v2, /device:TPU:32, one launch (start us, length us, event | category | flops | bytes accessed | tf_op | source)
XLA Modules:
  0.0 200.9 jit_solution(10526537286505132509)
XLA Ops:
  0.0 5.7 %pack.1 = (bf16[16,192,640]{2,1,0:T(8,128)(2,1)}, bf16[16,224,384]{2,1,0:T(8,128)(2,1)}) custom-call(bf16[128,16384]{1,0:T(8,128)(2,1)} %x_ref.1, bf16[128,2048]{1,0:T(8,128)(2,1)} %b_ref.1, bf16[128,2048]{1,0:T(8,128)(2,1)} %c_ref.1, bf16[128,256]{1,0:T(8,128)(2,1)} %d_ref.1), custom_call_target="tpu_custom_call" | custom-call | bytes 12582912 | tf_op jit(solution)/shard_map/pack/pallas_call | solution.py:77
  5.7 55.3 %all_to_all.20.refs_1_.refs_2_.refs_3_.x_ref.b_ref = bf16[16,192,640]{2,1,0:T(8,128)(2,1)} all-to-all(bf16[16,192,640]{2,1,0:T(8,128)(2,1)} %get-tuple-element.26), channel_id=1, replica_groups=mesh['ctx'=16,'head'=16] {'head'}, dimensions={0} | all-to-all | bytes 7864320 | tf_op jit(solution)/shard_map/all_to_all | solution.py:508
  61.0 3.8 %all-to-all-start.1 = ((bf16[16,224,384]{2,1,0:T(8,128)(2,1)}), bf16[16,224,384]{2,1,0:T(8,128)(2,1)S(1)}, u32[]{:S(2)}, u32[]{:S(2)}) async-start(bf16[16,224,384]{2,1,0:T(8,128)(2,1)} %get-tuple-element.27), calls=%async_computation.1 | async-start | bytes 5505024 | tf_op jit(solution)/shard_map/all_to_all | solution.py:508
  64.9 6.5 %states0.1 = (bf16[144,640]{1,0:T(8,128)(2,1)}, bf16[144,640]{1,0:T(8,128)(2,1)}, bf16[2048,128]{1,0:T(8,128)(2,1)}) custom-call(s32[1]{0:T(128)S(6)} %select_n.12.refs_0_.core_ref, bf16[16,192,640]{2,1,0:T(8,128)(2,1)} %all_to_all.20.refs_1_.refs_2_.refs_3_.x_ref.b_ref, bf16[16,192,640]{2,1,0:T(8,128)(2,1)} %all_to_all.20.refs_1_.refs_2_.refs_3_.x_ref.b_ref, ...), custom_call_target="tpu_custom_call" | custom-call | flops 1073741824 | bytes 5242880 | tf_op jit(solution)/shard_map/states0/pallas_call | solution.py:230
  76.1 4.7 %collective-permute-done.1.refs_0_ = bf16[144,640]{1,0:T(8,128)(2,1)S(1)} collective-permute-done((bf16[144,640]{1,0:T(8,128)(2,1)S(1)}, bf16[144,640]{1,0:T(8,128)(2,1)S(1)}, u32[]{:S(2)}, u32[]{:S(2)}) %collective-permute-start.1) | collective-permute-done | bytes 184352 | tf_op jit(solution)/shard_map/ppermute | solution.py:317
  82.7 2.3 %collective-permute-start.6 = (bf16[144,640]{1,0:T(8,128)(2,1)S(1)}, bf16[144,640]{1,0:T(8,128)(2,1)S(1)}, u32[]{:S(2)}, u32[]{:S(2)}) collective-permute-start(bf16[144,640]{1,0:T(8,128)(2,1)S(1)} %collective-permute-done.5.refs_6_), channel_id=1, source_target_pairs={{0,224},{16,240},{32,0},{48,16},{64,32},{80,48},{96,64},{112,80},{... | collective-permute-start | bytes 552968 | tf_op jit(solution)/shard_map/ppermute | solution.py:319
  85.0 4.4 %collective-permute-done.2.refs_1_ = bf16[144,640]{1,0:T(8,128)(2,1)S(1)} collective-permute-done((bf16[144,640]{1,0:T(8,128)(2,1)S(1)}, bf16[144,640]{1,0:T(8,128)(2,1)S(1)}, u32[]{:S(2)}, u32[]{:S(2)}) %collective-permute-start.2) | collective-permute-done | bytes 184352 | tf_op jit(solution)/shard_map/ppermute | solution.py:317
  89.8 2.6 %collective-permute-start.7 = (bf16[144,640]{1,0:T(8,128)(2,1)S(1)}, bf16[144,640]{1,0:T(8,128)(2,1)S(1)}, u32[]{:S(2)}, u32[]{:S(2)}) collective-permute-start(bf16[144,640]{1,0:T(8,128)(2,1)S(1)} %collective-permute-done.6.refs_5_), channel_id=1, source_target_pairs={{0,224},{16,240},{32,0},{48,16},{64,32},{80,48},{96,64},{112,80},{... | collective-permute-start | bytes 552968 | tf_op jit(solution)/shard_map/ppermute | solution.py:319
  92.4 3.5 %collective-permute-done.3.refs_2_ = bf16[144,640]{1,0:T(8,128)(2,1)S(1)} collective-permute-done((bf16[144,640]{1,0:T(8,128)(2,1)S(1)}, bf16[144,640]{1,0:T(8,128)(2,1)S(1)}, u32[]{:S(2)}, u32[]{:S(2)}) %collective-permute-start.3) | collective-permute-done | bytes 184352 | tf_op jit(solution)/shard_map/ppermute | solution.py:317
  96.3 6.3 %collective-permute-done.4.refs_3_ = bf16[144,640]{1,0:T(8,128)(2,1)S(1)} collective-permute-done((bf16[144,640]{1,0:T(8,128)(2,1)S(1)}, bf16[144,640]{1,0:T(8,128)(2,1)S(1)}, u32[]{:S(2)}, u32[]{:S(2)}) %collective-permute-start.4) | collective-permute-done | bytes 184352 | tf_op jit(solution)/shard_map/ppermute | solution.py:317
  106.5 9.4 %mix0.1 = bf16[16,128,640]{2,1,0:T(8,128)(2,1)} custom-call(s32[1]{0:T(128)S(6)} %select_n.12.refs_0_.core_ref, f32[16]{0:T(128)} %gain_ref.3, bf16[128,640]{1,0:T(8,128)(2,1)} %copy-done.3, bf16[128,640]{1,0:T(8,128)(2,1)} %copy-done.6, bf16[16,192,640]{2,1,0:T(8,128)(2,1)} %all_to_all.20.refs_1_.refs_2_.refs_3_.x_ref.b_ref, ...), custom_call_target="tpu_custom_call" | custom-call | flops 4294967296 | bytes 14680064 | tf_op jit(solution)/shard_map/mix0/pallas_call | solution.py:390
  115.9 7.2 %all-to-all-start.2 = ((bf16[16,128,640]{2,1,0:T(8,128)(2,1)}), bf16[16,128,640]{2,1,0:T(8,128)(2,1)S(1)}, u32[]{:S(2)}, u32[]{:S(2)}) async-start(bf16[16,128,640]{2,1,0:T(8,128)(2,1)} %mix0.1), calls=%async_computation.2 | async-start | bytes 5242880 | tf_op jit(solution)/shard_map/all_to_all | solution.py:508
  123.1 4.9 %states1.1 = (bf16[144,384]{1,0:T(8,128)(2,1)}, bf16[144,384]{1,0:T(8,128)(2,1)}) custom-call(s32[1]{0:T(128)S(6)} %select_n.12.refs_0_.core_ref, bf16[16,224,384]{2,1,0:T(8,128)(2,1)} %copy-done.5, bf16[16,192,640]{2,1,0:T(8,128)(2,1)} %all_to_all.20.refs_1_.refs_2_.refs_3_.x_ref.b_ref, bf16[2048,128]{1,0:T(8,128)(2,1)} %get-tuple-element.33.sums_ref.refs_3_), custom_call_target="tpu_custom_call" | custom-call | flops 1073741824 | bytes 5242880 | tf_op jit(solution)/shard_map/states1/pallas_call | solution.py:230
  130.8 3.3 %collective-permute-start.11 = (bf16[144,384]{1,0:T(8,128)(2,1)S(1)}, bf16[144,384]{1,0:T(8,128)(2,1)S(1)}, u32[]{:S(2)}, u32[]{:S(2)}) collective-permute-start(bf16[144,384]{1,0:T(8,128)(2,1)S(1)} %chip1.1), channel_id=1, source_target_pairs={{0,224},{16,240},{32,0},{48,16},{64,32},{80,48},{96,64},{112,80},{... | collective-permute-start | bytes 331784 | tf_op jit(solution)/shard_map/ppermute | solution.py:319
  134.1 6.9 %inside1.1.own_ref = bf16[2048,384]{1,0:T(8,128)(2,1)} custom-call(f32[16]{0:T(128)} %gain_ref.3, bf16[16,224,384]{2,1,0:T(8,128)(2,1)} %copy-done.5, bf16[16,192,640]{2,1,0:T(8,128)(2,1)} %all_to_all.20.refs_1_.refs_2_.refs_3_.x_ref.b_ref, bf16[16,224,384]{2,1,0:T(8,128)(2,1)} %copy-done.5, bf16[16,224,384]{2,1,0:T(8,128)(2,1)} %copy-done.5, ...), custom_call_target="tpu_custom_call" | custom-call | flops 4294967296 | bytes 14680064 | tf_op jit(solution)/shard_map/inside1/pallas_call | solution.py:417
  141.1 3.2 %collective-permute-start.15 = (bf16[144,384]{1,0:T(8,128)(2,1)S(1)}, bf16[144,384]{1,0:T(8,128)(2,1)S(1)}, u32[]{:S(2)}, u32[]{:S(2)}) collective-permute-start(bf16[144,384]{1,0:T(8,128)(2,1)S(1)} %collective-permute-done.11.refs_6_), channel_id=1, source_target_pairs={{0,224},{16,240},{32,0},{48,16},{64,32},{80,48},{96,64},{112,80},{... | collective-permute-start | bytes 331784 | tf_op jit(solution)/shard_map/ppermute | solution.py:319
  144.3 2.7 %collective-permute-done.12.refs_1_ = bf16[144,384]{1,0:T(8,128)(2,1)S(1)} collective-permute-done((bf16[144,384]{1,0:T(8,128)(2,1)S(1)}, bf16[144,384]{1,0:T(8,128)(2,1)S(1)}, u32[]{:S(2)}, u32[]{:S(2)}) %collective-permute-start.12) | collective-permute-done | bytes 110624 | tf_op jit(solution)/shard_map/ppermute | solution.py:317
  147.6 2.6 %collective-permute-start.16 = (bf16[144,384]{1,0:T(8,128)(2,1)S(1)}, bf16[144,384]{1,0:T(8,128)(2,1)S(1)}, u32[]{:S(2)}, u32[]{:S(2)}) collective-permute-start(bf16[144,384]{1,0:T(8,128)(2,1)S(1)} %collective-permute-done.15.refs_5_), channel_id=1, source_target_pairs={{0,224},{16,240},{32,0},{48,16},{64,32},{80,48},{96,64},{112,80},{... | collective-permute-start | bytes 331784 | tf_op jit(solution)/shard_map/ppermute | solution.py:319
  150.2 2.7 %collective-permute-done.13.refs_2_ = bf16[144,384]{1,0:T(8,128)(2,1)S(1)} collective-permute-done((bf16[144,384]{1,0:T(8,128)(2,1)S(1)}, bf16[144,384]{1,0:T(8,128)(2,1)S(1)}, u32[]{:S(2)}, u32[]{:S(2)}) %collective-permute-start.13) | collective-permute-done | bytes 110624 | tf_op jit(solution)/shard_map/ppermute | solution.py:317
  153.4 5.4 %collective-permute-done.14.refs_3_ = bf16[144,384]{1,0:T(8,128)(2,1)S(1)} collective-permute-done((bf16[144,384]{1,0:T(8,128)(2,1)S(1)}, bf16[144,384]{1,0:T(8,128)(2,1)S(1)}, u32[]{:S(2)}, u32[]{:S(2)}) %collective-permute-start.14) | collective-permute-done | bytes 110624 | tf_op jit(solution)/shard_map/ppermute | solution.py:317
  161.6 4.8 %join1.1 = bf16[16,128,384]{2,1,0:T(8,128)(2,1)} custom-call(s32[1]{0:T(128)S(6)} %select_n.12.refs_0_.core_ref, bf16[128,384]{1,0:T(8,128)(2,1)} %copy-done.4, bf16[128,384]{1,0:T(8,128)(2,1)} %copy-done.7, bf16[16,224,384]{2,1,0:T(8,128)(2,1)} %copy-done.5, bf16[16,224,384]{2,1,0:T(8,128)(2,1)} %copy-done.5, ...), custom_call_target="tpu_custom_call" | custom-call | flops 1073741824 | bytes 8388608 | tf_op jit(solution)/shard_map/join1/pallas_call | solution.py:462
  166.4 7.3 %all-to-all-start.3 = ((bf16[16,128,384]{2,1,0:T(8,128)(2,1)}), bf16[16,128,384]{2,1,0:T(8,128)(2,1)}, u32[]{:S(2)}, u32[]{:S(2)}) async-start(bf16[16,128,384]{2,1,0:T(8,128)(2,1)} %join1.1), calls=%async_computation.3 | async-start | bytes 3145728 | tf_op jit(solution)/shard_map/all_to_all | solution.py:508
  175.2 22.8 %all-to-all-done.3.refs_0_ = bf16[16,128,384]{2,1,0:T(8,128)(2,1)} async-done(((bf16[16,128,384]{2,1,0:T(8,128)(2,1)}), bf16[16,128,384]{2,1,0:T(8,128)(2,1)}, u32[]{:S(2)}, u32[]{:S(2)}) %all-to-all-start.3) | async-done | bytes 1572896 | tf_op jit(solution)/shard_map/all_to_all | solution.py:508
  198.1 2.7 %unpack1.1 = bf16[128,16384]{1,0:T(8,128)(2,1)} custom-call(bf16[16,128,384]{2,1,0:T(8,128)(2,1)} %all-to-all-done.3.refs_0_, bf16[128,16384]{1,0:T(8,128)(2,1)} %unpack0.1.refs_1_), custom_call_target="tpu_custom_call", output_to_operand_aliasing={{}: (1, {})} | custom-call | bytes 4194304 | tf_op jit(solution)/shard_map/unpack1/pallas_call | solution.py:493
  (47 shorter events, 19.7 us)
Async XLA Ops:
  61.0 43.9 %all-to-all-start.1 = ((bf16[16,224,384]{2,1,0:T(8,128)(2,1)}), bf16[16,224,384]{2,1,0:T(8,128)(2,1)S(1)}, u32[]{:S(2)}, u32[]{:S(2)}) async-start(bf16[16,224,384]{2,1,0:T(8,128)(2,1)} %get-tuple-element.27), calls=%async_computation.1 | async-start | bytes 5505024 | tf_op jit(solution)/shard_map/all_to_all | solution.py:508
  71.4 1.6 collective-permute-start
  73.0 0.9 copy-start
  74.0 6.8 %collective-permute-start.1 = (bf16[144,640]{1,0:T(8,128)(2,1)S(1)}, bf16[144,640]{1,0:T(8,128)(2,1)S(1)}, u32[]{:S(2)}, u32[]{:S(2)}) collective-permute-start(bf16[144,640]{1,0:T(8,128)(2,1)S(1)} %chip0.1), channel_id=1, source_target_pairs={{0,32},{16,48},{32,64},{48,80},{64,96},{80,112},{96,128},{112,144}... | collective-permute-start | bytes 552968 | tf_op jit(solution)/shard_map/ppermute | solution.py:317
  76.0 6.7 %collective-permute-start.5 = (bf16[144,640]{1,0:T(8,128)(2,1)S(1)}, bf16[144,640]{1,0:T(8,128)(2,1)S(1)}, u32[]{:S(2)}, u32[]{:S(2)}) collective-permute-start(bf16[144,640]{1,0:T(8,128)(2,1)S(1)} %chip0.1), channel_id=1, source_target_pairs={{0,224},{16,240},{32,0},{48,16},{64,32},{80,48},{96,64},{112,80},{... | collective-permute-start | bytes 552968 | tf_op jit(solution)/shard_map/ppermute | solution.py:319
  80.8 8.7 %collective-permute-start.2 = (bf16[144,640]{1,0:T(8,128)(2,1)S(1)}, bf16[144,640]{1,0:T(8,128)(2,1)S(1)}, u32[]{:S(2)}, u32[]{:S(2)}) collective-permute-start(bf16[144,640]{1,0:T(8,128)(2,1)S(1)} %collective-permute-done.1.refs_0_), channel_id=1, source_target_pairs={{0,32},{16,48},{32,64},{48,80},{64,96},{80,112},{96,128},{112,144}... | collective-permute-start | bytes 552968 | tf_op jit(solution)/shard_map/ppermute | solution.py:317
  82.7 7.1 %collective-permute-start.6 = (bf16[144,640]{1,0:T(8,128)(2,1)S(1)}, bf16[144,640]{1,0:T(8,128)(2,1)S(1)}, u32[]{:S(2)}, u32[]{:S(2)}) collective-permute-start(bf16[144,640]{1,0:T(8,128)(2,1)S(1)} %collective-permute-done.5.refs_6_), channel_id=1, source_target_pairs={{0,224},{16,240},{32,0},{48,16},{64,32},{80,48},{96,64},{112,80},{... | collective-permute-start | bytes 552968 | tf_op jit(solution)/shard_map/ppermute | solution.py:319
  89.4 6.5 %collective-permute-start.3 = (bf16[144,640]{1,0:T(8,128)(2,1)S(1)}, bf16[144,640]{1,0:T(8,128)(2,1)S(1)}, u32[]{:S(2)}, u32[]{:S(2)}) collective-permute-start(bf16[144,640]{1,0:T(8,128)(2,1)S(1)} %collective-permute-done.2.refs_1_), channel_id=1, source_target_pairs={{0,32},{16,48},{32,64},{48,80},{64,96},{80,112},{96,128},{112,144}... | collective-permute-start | bytes 552968 | tf_op jit(solution)/shard_map/ppermute | solution.py:317
  89.8 6.5 %collective-permute-start.7 = (bf16[144,640]{1,0:T(8,128)(2,1)S(1)}, bf16[144,640]{1,0:T(8,128)(2,1)S(1)}, u32[]{:S(2)}, u32[]{:S(2)}) collective-permute-start(bf16[144,640]{1,0:T(8,128)(2,1)S(1)} %collective-permute-done.6.refs_5_), channel_id=1, source_target_pairs={{0,224},{16,240},{32,0},{48,16},{64,32},{80,48},{96,64},{112,80},{... | collective-permute-start | bytes 552968 | tf_op jit(solution)/shard_map/ppermute | solution.py:319
  95.9 6.7 %collective-permute-start.4 = (bf16[144,640]{1,0:T(8,128)(2,1)S(1)}, bf16[144,640]{1,0:T(8,128)(2,1)S(1)}, u32[]{:S(2)}, u32[]{:S(2)}) collective-permute-start(bf16[144,640]{1,0:T(8,128)(2,1)S(1)} %collective-permute-done.3.refs_2_), channel_id=1, source_target_pairs={{0,32},{16,48},{32,64},{48,80},{64,96},{80,112},{96,128},{112,144}... | collective-permute-start | bytes 552968 | tf_op jit(solution)/shard_map/ppermute | solution.py:317
  103.6 1.4 collective-permute-start.8
  105.0 1.6 copy-start.5
  115.9 50.4 %all-to-all-start.2 = ((bf16[16,128,640]{2,1,0:T(8,128)(2,1)}), bf16[16,128,640]{2,1,0:T(8,128)(2,1)S(1)}, u32[]{:S(2)}, u32[]{:S(2)}) async-start(bf16[16,128,640]{2,1,0:T(8,128)(2,1)} %mix0.1), calls=%async_computation.2 | async-start | bytes 5242880 | tf_op jit(solution)/shard_map/all_to_all | solution.py:508
  128.0 1.5 collective-permute-start.9
  130.5 28.3 %copy-start.2 = (bf16[144,384]{1,0:T(8,128)(2,1)S(1)}, bf16[144,384]{1,0:T(8,128)(2,1)}, u32[]{:S(2)}) copy-start(bf16[144,384]{1,0:T(8,128)(2,1)} %get-tuple-element.35.keep_ref) | copy-start | bytes 331780
  130.6 10.4 %collective-permute-start.10 = (bf16[144,384]{1,0:T(8,128)(2,1)S(1)}, bf16[144,384]{1,0:T(8,128)(2,1)S(1)}, u32[]{:S(2)}, u32[]{:S(2)}) collective-permute-start(bf16[144,384]{1,0:T(8,128)(2,1)S(1)} %chip1.1), channel_id=1, source_target_pairs={{0,32},{16,48},{32,64},{48,80},{64,96},{80,112},{96,128},{112,144}... | collective-permute-start | bytes 331784 | tf_op jit(solution)/shard_map/ppermute | solution.py:317
  130.8 10.1 %collective-permute-start.11 = (bf16[144,384]{1,0:T(8,128)(2,1)S(1)}, bf16[144,384]{1,0:T(8,128)(2,1)S(1)}, u32[]{:S(2)}, u32[]{:S(2)}) collective-permute-start(bf16[144,384]{1,0:T(8,128)(2,1)S(1)} %chip1.1), channel_id=1, source_target_pairs={{0,224},{16,240},{32,0},{48,16},{64,32},{80,48},{96,64},{112,80},{... | collective-permute-start | bytes 331784 | tf_op jit(solution)/shard_map/ppermute | solution.py:319
  141.0 6.0 %collective-permute-start.12 = (bf16[144,384]{1,0:T(8,128)(2,1)S(1)}, bf16[144,384]{1,0:T(8,128)(2,1)S(1)}, u32[]{:S(2)}, u32[]{:S(2)}) collective-permute-start(bf16[144,384]{1,0:T(8,128)(2,1)S(1)} %collective-permute-done.10.refs_0_), channel_id=1, source_target_pairs={{0,32},{16,48},{32,64},{48,80},{64,96},{80,112},{96,128},{112,144}... | collective-permute-start | bytes 331784 | tf_op jit(solution)/shard_map/ppermute | solution.py:317
  141.1 6.5 %collective-permute-start.15 = (bf16[144,384]{1,0:T(8,128)(2,1)S(1)}, bf16[144,384]{1,0:T(8,128)(2,1)S(1)}, u32[]{:S(2)}, u32[]{:S(2)}) collective-permute-start(bf16[144,384]{1,0:T(8,128)(2,1)S(1)} %collective-permute-done.11.refs_6_), channel_id=1, source_target_pairs={{0,224},{16,240},{32,0},{48,16},{64,32},{80,48},{96,64},{112,80},{... | collective-permute-start | bytes 331784 | tf_op jit(solution)/shard_map/ppermute | solution.py:319
  147.0 5.9 %collective-permute-start.13 = (bf16[144,384]{1,0:T(8,128)(2,1)S(1)}, bf16[144,384]{1,0:T(8,128)(2,1)S(1)}, u32[]{:S(2)}, u32[]{:S(2)}) collective-permute-start(bf16[144,384]{1,0:T(8,128)(2,1)S(1)} %collective-permute-done.12.refs_1_), channel_id=1, source_target_pairs={{0,32},{16,48},{32,64},{48,80},{64,96},{80,112},{96,128},{112,144}... | collective-permute-start | bytes 331784 | tf_op jit(solution)/shard_map/ppermute | solution.py:317
  147.6 5.9 %collective-permute-start.16 = (bf16[144,384]{1,0:T(8,128)(2,1)S(1)}, bf16[144,384]{1,0:T(8,128)(2,1)S(1)}, u32[]{:S(2)}, u32[]{:S(2)}) collective-permute-start(bf16[144,384]{1,0:T(8,128)(2,1)S(1)} %collective-permute-done.15.refs_5_), channel_id=1, source_target_pairs={{0,224},{16,240},{32,0},{48,16},{64,32},{80,48},{96,64},{112,80},{... | collective-permute-start | bytes 331784 | tf_op jit(solution)/shard_map/ppermute | solution.py:319
  152.9 6.0 %collective-permute-start.14 = (bf16[144,384]{1,0:T(8,128)(2,1)S(1)}, bf16[144,384]{1,0:T(8,128)(2,1)S(1)}, u32[]{:S(2)}, u32[]{:S(2)}) collective-permute-start(bf16[144,384]{1,0:T(8,128)(2,1)S(1)} %collective-permute-done.13.refs_2_), channel_id=1, source_target_pairs={{0,32},{16,48},{32,64},{48,80},{64,96},{80,112},{96,128},{112,144}... | collective-permute-start | bytes 331784 | tf_op jit(solution)/shard_map/ppermute | solution.py:317
  159.6 1.3 collective-permute-start.17
  166.4 31.7 %all-to-all-start.3 = ((bf16[16,128,384]{2,1,0:T(8,128)(2,1)}), bf16[16,128,384]{2,1,0:T(8,128)(2,1)}, u32[]{:S(2)}, u32[]{:S(2)}) async-start(bf16[16,128,384]{2,1,0:T(8,128)(2,1)} %join1.1), calls=%async_computation.3 | async-start | bytes 3145728 | tf_op jit(solution)/shard_map/all_to_all | solution.py:508
  (5 other events, 3.5 us)

commit v3 on v2

--- a/solution.py
+++ b/solution.py
@@ -520,11 +520,11 @@
     second = exchange(packed1)
     keep0, send0, sums = end_states(0, core, first, first)
     mine0, got0, _ = incoming(0, core, chip, keep0, send0)
+    keep1, send1 = end_states(1, core, first, second, sums)
+    mine0, send1 = after((mine0, send1))
     mixed0 = mix(0, core, mine0, got0, first, second, sums, gains)
-    second, mixed0 = after((second, mixed0))
     y0 = exchange(mixed0)
 
-    keep1, send1 = end_states(1, core, first, second, sums)
     own1 = inside(1, first, second, sums, gains)
     mine1, got1, own1 = incoming(1, core, chip, keep1, send1, own1)
     mixed1 = join(1, core, mine1, got1, first, second, sums, own1)

time: 204 us -> 202 us (level)
  waiting for transfers between devices: 60.3 us -> 57.8 us
  transfers between devices with their start and end apart: 21 -> 21, of which waited for: 16 -> 15; matrix products, arithmetic and copies ran while one was open for 0% -> 0% of each run, Pallas kernels for 13% -> 13%
where the time goes in v3:
time: 202 us; the launch traced here: 199 us
  waiting for transfers between devices  57.8 us (29%)
  blocking collectives  55.3 us (27%)
  Pallas kernels  42.9 us (21%)
  starting transfers between devices  37.6 us (19%)
  local copies, waits for them, and re-layouts  5.04 us (2%)
    all_to_all x1, blocking collectives, exchange(): return lax.all_to_all(msg, 'head', split_axis=0, concat_axis=0, tiled=True)  55.3 us
    ppermute x8, waiting for transfers between devices, incoming(): forward.append(lax.ppermute(forward[-1], 'ctx', ahead))  29.9 us
    all_to_all x3, waiting for transfers between devices, exchange(): return lax.all_to_all(msg, 'head', split_axis=0, concat_axis=0, tiled=True)  22.1 us
    all_to_all x3, starting transfers between devices, exchange(): return lax.all_to_all(msg, 'head', split_axis=0, concat_axis=0, tiled=True)  18.9 us
    ppermute x6, starting transfers between devices, incoming(): backward.append(lax.ppermute(backward[-1], 'ctx', back))  14 us
    pallas_call x2, Pallas kernels, end_states(): call(functools.partial(states_kernel, part), 'states%d' % part, (2 ** 30,...  11.3 us
    pallas_call x1, Pallas kernels, mix(): call(functools.partial(mix_kernel, part), 'mix%d' % part, (4 * 2 ** 30, 1...  9.4 us
    pallas_call x1, Pallas kernels, inside(): call(functools.partial(inside_kernel, part), 'inside%d' % part, (4 * 2 **...  6.86 us
  transfers between devices with their start and end apart: 21, of which 15 were waited for; matrix products, arithmetic and copies ran while one was open for 0% of the time, Pallas kernels for 13%

profile of v3, /device:TPU:32, one launch (start us, length us, event | category | flops | bytes accessed | tf_op | source)
XLA Modules:
  0.0 198.9 jit_solution(4887341119577057181)
XLA Ops:
  0.0 5.7 %pack.1 = (bf16[16,192,640]{2,1,0:T(8,128)(2,1)}, bf16[16,224,384]{2,1,0:T(8,128)(2,1)}) custom-call(bf16[128,16384]{1,0:T(8,128)(2,1)} %x_ref.1, bf16[128,2048]{1,0:T(8,128)(2,1)} %b_ref.1, bf16[128,2048]{1,0:T(8,128)(2,1)} %c_ref.1, bf16[128,256]{1,0:T(8,128)(2,1)} %d_ref.1), custom_call_target="tpu_custom_call" | custom-call | bytes 12582912 | tf_op jit(solution)/shard_map/pack/pallas_call | solution.py:77
  5.7 55.3 %all_to_all.20.refs_1_.refs_2_.refs_3_.b_ref.x_ref = bf16[16,192,640]{2,1,0:T(8,128)(2,1)} all-to-all(bf16[16,192,640]{2,1,0:T(8,128)(2,1)} %get-tuple-element.26), channel_id=1, replica_groups=mesh['ctx'=16,'head'=16] {'head'}, dimensions={0} | all-to-all | bytes 7864320 | tf_op jit(solution)/shard_map/all_to_all | solution.py:508
  61.0 3.8 %all-to-all-start.1 = ((bf16[16,224,384]{2,1,0:T(8,128)(2,1)}), bf16[16,224,384]{2,1,0:T(8,128)(2,1)S(1)}, u32[]{:S(2)}, u32[]{:S(2)}) async-start(bf16[16,224,384]{2,1,0:T(8,128)(2,1)} %get-tuple-element.27), calls=%async_computation.1 | async-start | bytes 5505024 | tf_op jit(solution)/shard_map/all_to_all | solution.py:508
  64.9 6.5 %states0.1 = (bf16[144,640]{1,0:T(8,128)(2,1)}, bf16[144,640]{1,0:T(8,128)(2,1)}, bf16[2048,128]{1,0:T(8,128)(2,1)}) custom-call(s32[1]{0:T(128)S(6)} %select_n.12.refs_0_.core_ref, bf16[16,192,640]{2,1,0:T(8,128)(2,1)} %all_to_all.20.refs_1_.refs_2_.refs_3_.b_ref.x_ref, bf16[16,192,640]{2,1,0:T(8,128)(2,1)} %all_to_all.20.refs_1_.refs_2_.refs_3_.b_ref.x_ref, ...), custom_call_target="tpu_custom_call" | custom-call | flops 1073741824 | bytes 5242880 | tf_op jit(solution)/shard_map/states0/pallas_call | solution.py:230
  76.1 4.7 %collective-permute-done.1.refs_0_ = bf16[144,640]{1,0:T(8,128)(2,1)S(1)} collective-permute-done((bf16[144,640]{1,0:T(8,128)(2,1)S(1)}, bf16[144,640]{1,0:T(8,128)(2,1)S(1)}, u32[]{:S(2)}, u32[]{:S(2)}) %collective-permute-start.1) | collective-permute-done | bytes 184352 | tf_op jit(solution)/shard_map/ppermute | solution.py:317
  82.7 2.3 %collective-permute-start.6 = (bf16[144,640]{1,0:T(8,128)(2,1)S(1)}, bf16[144,640]{1,0:T(8,128)(2,1)S(1)}, u32[]{:S(2)}, u32[]{:S(2)}) collective-permute-start(bf16[144,640]{1,0:T(8,128)(2,1)S(1)} %collective-permute-done.5.refs_6_), channel_id=1, source_target_pairs={{0,224},{16,240},{32,0},{48,16},{64,32},{80,48},{96,64},{112,80},{... | collective-permute-start | bytes 552968 | tf_op jit(solution)/shard_map/ppermute | solution.py:319
  85.0 4.4 %collective-permute-done.2.refs_1_ = bf16[144,640]{1,0:T(8,128)(2,1)S(1)} collective-permute-done((bf16[144,640]{1,0:T(8,128)(2,1)S(1)}, bf16[144,640]{1,0:T(8,128)(2,1)S(1)}, u32[]{:S(2)}, u32[]{:S(2)}) %collective-permute-start.2) | collective-permute-done | bytes 184352 | tf_op jit(solution)/shard_map/ppermute | solution.py:317
  89.8 2.6 %collective-permute-start.7 = (bf16[144,640]{1,0:T(8,128)(2,1)S(1)}, bf16[144,640]{1,0:T(8,128)(2,1)S(1)}, u32[]{:S(2)}, u32[]{:S(2)}) collective-permute-start(bf16[144,640]{1,0:T(8,128)(2,1)S(1)} %collective-permute-done.6.refs_5_), channel_id=1, source_target_pairs={{0,224},{16,240},{32,0},{48,16},{64,32},{80,48},{96,64},{112,80},{... | collective-permute-start | bytes 552968 | tf_op jit(solution)/shard_map/ppermute | solution.py:319
  92.4 3.5 %collective-permute-done.3.refs_2_ = bf16[144,640]{1,0:T(8,128)(2,1)S(1)} collective-permute-done((bf16[144,640]{1,0:T(8,128)(2,1)S(1)}, bf16[144,640]{1,0:T(8,128)(2,1)S(1)}, u32[]{:S(2)}, u32[]{:S(2)}) %collective-permute-start.3) | collective-permute-done | bytes 184352 | tf_op jit(solution)/shard_map/ppermute | solution.py:317
  96.3 6.3 %collective-permute-done.4.refs_3_ = bf16[144,640]{1,0:T(8,128)(2,1)S(1)} collective-permute-done((bf16[144,640]{1,0:T(8,128)(2,1)S(1)}, bf16[144,640]{1,0:T(8,128)(2,1)S(1)}, u32[]{:S(2)}, u32[]{:S(2)}) %collective-permute-start.4) | collective-permute-done | bytes 184352 | tf_op jit(solution)/shard_map/ppermute | solution.py:317
  105.1 4.9 %states1.1 = (bf16[144,384]{1,0:T(8,128)(2,1)}, bf16[144,384]{1,0:T(8,128)(2,1)}) custom-call(s32[1]{0:T(128)S(6)} %select_n.12.refs_0_.core_ref, bf16[16,224,384]{2,1,0:T(8,128)(2,1)} %copy-done.4, bf16[16,192,640]{2,1,0:T(8,128)(2,1)} %all_to_all.20.refs_1_.refs_2_.refs_3_.b_ref.x_ref, bf16[2048,128]{1,0:T(8,128)(2,1)} %get-tuple-element.29.refs_3_.sums_ref), custom_call_target="tpu_custom_call" | custom-call | flops 1073741824 | bytes 5242880 | tf_op jit(solution)/shard_map/states1/pallas_call | solution.py:230
  110.6 9.4 %mix0.1 = bf16[16,128,640]{2,1,0:T(8,128)(2,1)} custom-call(s32[1]{0:T(128)S(6)} %select_n.12.refs_0_.core_ref, f32[16]{0:T(128)} %gain_ref.3, bf16[128,640]{1,0:T(8,128)(2,1)} %copy-done.2, bf16[128,640]{1,0:T(8,128)(2,1)} %copy-done.5, bf16[16,192,640]{2,1,0:T(8,128)(2,1)} %all_to_all.20.refs_1_.refs_2_.refs_3_.b_ref.x_ref, ...), custom_call_target="tpu_custom_call" | custom-call | flops 4294967296 | bytes 14680064 | tf_op jit(solution)/shard_map/mix0/pallas_call | solution.py:390
  120.1 7.3 %all-to-all-start.2 = ((bf16[16,128,640]{2,1,0:T(8,128)(2,1)}), bf16[16,128,640]{2,1,0:T(8,128)(2,1)S(1)}, u32[]{:S(2)}, u32[]{:S(2)}) async-start(bf16[16,128,640]{2,1,0:T(8,128)(2,1)} %mix0.1), calls=%async_computation.2 | async-start | bytes 5242880 | tf_op jit(solution)/shard_map/all_to_all | solution.py:508
  129.2 3.3 %collective-permute-start.10 = (bf16[144,384]{1,0:T(8,128)(2,1)S(1)}, bf16[144,384]{1,0:T(8,128)(2,1)S(1)}, u32[]{:S(2)}, u32[]{:S(2)}) collective-permute-start(bf16[144,384]{1,0:T(8,128)(2,1)S(1)} %chip1.1), channel_id=1, source_target_pairs={{0,224},{16,240},{32,0},{48,16},{64,32},{80,48},{96,64},{112,80},{... | collective-permute-start | bytes 331784 | tf_op jit(solution)/shard_map/ppermute | solution.py:319
  132.4 6.9 %inside1.1.own_ref = bf16[2048,384]{1,0:T(8,128)(2,1)} custom-call(f32[16]{0:T(128)} %gain_ref.3, bf16[16,224,384]{2,1,0:T(8,128)(2,1)} %copy-done.4, bf16[16,192,640]{2,1,0:T(8,128)(2,1)} %all_to_all.20.refs_1_.refs_2_.refs_3_.b_ref.x_ref, bf16[16,224,384]{2,1,0:T(8,128)(2,1)} %copy-done.4, bf16[16,224,384]{2,1,0:T(8,128)(2,1)} %copy-done.4, ...), custom_call_target="tpu_custom_call" | custom-call | flops 4294967296 | bytes 14680064 | tf_op jit(solution)/shard_map/inside1/pallas_call | solution.py:417
  139.4 3.2 %collective-permute-start.14 = (bf16[144,384]{1,0:T(8,128)(2,1)S(1)}, bf16[144,384]{1,0:T(8,128)(2,1)S(1)}, u32[]{:S(2)}, u32[]{:S(2)}) collective-permute-start(bf16[144,384]{1,0:T(8,128)(2,1)S(1)} %collective-permute-done.10.refs_6_), channel_id=1, source_target_pairs={{0,224},{16,240},{32,0},{48,16},{64,32},{80,48},{96,64},{112,80},{... | collective-permute-start | bytes 331784 | tf_op jit(solution)/shard_map/ppermute | solution.py:319
  142.6 2.8 %collective-permute-done.11.refs_1_ = bf16[144,384]{1,0:T(8,128)(2,1)S(1)} collective-permute-done((bf16[144,384]{1,0:T(8,128)(2,1)S(1)}, bf16[144,384]{1,0:T(8,128)(2,1)S(1)}, u32[]{:S(2)}, u32[]{:S(2)}) %collective-permute-start.11) | collective-permute-done | bytes 110624 | tf_op jit(solution)/shard_map/ppermute | solution.py:317
  146.0 2.5 %collective-permute-start.15 = (bf16[144,384]{1,0:T(8,128)(2,1)S(1)}, bf16[144,384]{1,0:T(8,128)(2,1)S(1)}, u32[]{:S(2)}, u32[]{:S(2)}) collective-permute-start(bf16[144,384]{1,0:T(8,128)(2,1)S(1)} %collective-permute-done.14.refs_5_), channel_id=1, source_target_pairs={{0,224},{16,240},{32,0},{48,16},{64,32},{80,48},{96,64},{112,80},{... | collective-permute-start | bytes 331784 | tf_op jit(solution)/shard_map/ppermute | solution.py:319
  148.5 2.7 %collective-permute-done.12.refs_2_ = bf16[144,384]{1,0:T(8,128)(2,1)S(1)} collective-permute-done((bf16[144,384]{1,0:T(8,128)(2,1)S(1)}, bf16[144,384]{1,0:T(8,128)(2,1)S(1)}, u32[]{:S(2)}, u32[]{:S(2)}) %collective-permute-start.12) | collective-permute-done | bytes 110624 | tf_op jit(solution)/shard_map/ppermute | solution.py:317
  151.8 5.4 %collective-permute-done.13.refs_3_ = bf16[144,384]{1,0:T(8,128)(2,1)S(1)} collective-permute-done((bf16[144,384]{1,0:T(8,128)(2,1)S(1)}, bf16[144,384]{1,0:T(8,128)(2,1)S(1)}, u32[]{:S(2)}, u32[]{:S(2)}) %collective-permute-start.13) | collective-permute-done | bytes 110624 | tf_op jit(solution)/shard_map/ppermute | solution.py:317
  159.9 4.8 %join1.1 = bf16[16,128,384]{2,1,0:T(8,128)(2,1)} custom-call(s32[1]{0:T(128)S(6)} %select_n.12.refs_0_.core_ref, bf16[128,384]{1,0:T(8,128)(2,1)} %copy-done.3, bf16[128,384]{1,0:T(8,128)(2,1)} %copy-done.6, bf16[16,224,384]{2,1,0:T(8,128)(2,1)} %copy-done.4, bf16[16,224,384]{2,1,0:T(8,128)(2,1)} %copy-done.4, ...), custom_call_target="tpu_custom_call" | custom-call | flops 1073741824 | bytes 8388608 | tf_op jit(solution)/shard_map/join1/pallas_call | solution.py:462
  164.7 7.7 %all-to-all-start.3 = ((bf16[16,128,384]{2,1,0:T(8,128)(2,1)}), bf16[16,128,384]{2,1,0:T(8,128)(2,1)}, u32[]{:S(2)}, u32[]{:S(2)}) async-start(bf16[16,128,384]{2,1,0:T(8,128)(2,1)} %join1.1), calls=%async_computation.3 | async-start | bytes 3145728 | tf_op jit(solution)/shard_map/all_to_all | solution.py:508
  174.0 22.1 %all-to-all-done.3.refs_0_ = bf16[16,128,384]{2,1,0:T(8,128)(2,1)} async-done(((bf16[16,128,384]{2,1,0:T(8,128)(2,1)}), bf16[16,128,384]{2,1,0:T(8,128)(2,1)}, u32[]{:S(2)}, u32[]{:S(2)}) %all-to-all-start.3) | async-done | bytes 1572896 | tf_op jit(solution)/shard_map/all_to_all | solution.py:508
  196.1 2.7 %unpack1.1 = bf16[128,16384]{1,0:T(8,128)(2,1)} custom-call(bf16[16,128,384]{2,1,0:T(8,128)(2,1)} %all-to-all-done.3.refs_0_, bf16[128,16384]{1,0:T(8,128)(2,1)} %unpack0.1.refs_1_), custom_call_target="tpu_custom_call", output_to_operand_aliasing={{}: (1, {})} | custom-call | bytes 4194304 | tf_op jit(solution)/shard_map/unpack1/pallas_call | solution.py:493
  (47 shorter events, 17.9 us)
Async XLA Ops:
  61.0 42.5 %all-to-all-start.1 = ((bf16[16,224,384]{2,1,0:T(8,128)(2,1)}), bf16[16,224,384]{2,1,0:T(8,128)(2,1)S(1)}, u32[]{:S(2)}, u32[]{:S(2)}) async-start(bf16[16,224,384]{2,1,0:T(8,128)(2,1)} %get-tuple-element.27), calls=%async_computation.1 | async-start | bytes 5505024 | tf_op jit(solution)/shard_map/all_to_all | solution.py:508
  71.4 1.6 collective-permute-start
  74.0 6.8 %collective-permute-start.1 = (bf16[144,640]{1,0:T(8,128)(2,1)S(1)}, bf16[144,640]{1,0:T(8,128)(2,1)S(1)}, u32[]{:S(2)}, u32[]{:S(2)}) collective-permute-start(bf16[144,640]{1,0:T(8,128)(2,1)S(1)} %chip0.1), channel_id=1, source_target_pairs={{0,32},{16,48},{32,64},{48,80},{64,96},{80,112},{96,128},{112,144}... | collective-permute-start | bytes 552968 | tf_op jit(solution)/shard_map/ppermute | solution.py:317
  76.0 6.7 %collective-permute-start.5 = (bf16[144,640]{1,0:T(8,128)(2,1)S(1)}, bf16[144,640]{1,0:T(8,128)(2,1)S(1)}, u32[]{:S(2)}, u32[]{:S(2)}) collective-permute-start(bf16[144,640]{1,0:T(8,128)(2,1)S(1)} %chip0.1), channel_id=1, source_target_pairs={{0,224},{16,240},{32,0},{48,16},{64,32},{80,48},{96,64},{112,80},{... | collective-permute-start | bytes 552968 | tf_op jit(solution)/shard_map/ppermute | solution.py:319
  80.8 8.7 %collective-permute-start.2 = (bf16[144,640]{1,0:T(8,128)(2,1)S(1)}, bf16[144,640]{1,0:T(8,128)(2,1)S(1)}, u32[]{:S(2)}, u32[]{:S(2)}) collective-permute-start(bf16[144,640]{1,0:T(8,128)(2,1)S(1)} %collective-permute-done.1.refs_0_), channel_id=1, source_target_pairs={{0,32},{16,48},{32,64},{48,80},{64,96},{80,112},{96,128},{112,144}... | collective-permute-start | bytes 552968 | tf_op jit(solution)/shard_map/ppermute | solution.py:317
  82.7 7.1 %collective-permute-start.6 = (bf16[144,640]{1,0:T(8,128)(2,1)S(1)}, bf16[144,640]{1,0:T(8,128)(2,1)S(1)}, u32[]{:S(2)}, u32[]{:S(2)}) collective-permute-start(bf16[144,640]{1,0:T(8,128)(2,1)S(1)} %collective-permute-done.5.refs_6_), channel_id=1, source_target_pairs={{0,224},{16,240},{32,0},{48,16},{64,32},{80,48},{96,64},{112,80},{... | collective-permute-start | bytes 552968 | tf_op jit(solution)/shard_map/ppermute | solution.py:319
  89.4 6.5 %collective-permute-start.3 = (bf16[144,640]{1,0:T(8,128)(2,1)S(1)}, bf16[144,640]{1,0:T(8,128)(2,1)S(1)}, u32[]{:S(2)}, u32[]{:S(2)}) collective-permute-start(bf16[144,640]{1,0:T(8,128)(2,1)S(1)} %collective-permute-done.2.refs_1_), channel_id=1, source_target_pairs={{0,32},{16,48},{32,64},{48,80},{64,96},{80,112},{96,128},{112,144}... | collective-permute-start | bytes 552968 | tf_op jit(solution)/shard_map/ppermute | solution.py:317
  89.8 6.5 %collective-permute-start.7 = (bf16[144,640]{1,0:T(8,128)(2,1)S(1)}, bf16[144,640]{1,0:T(8,128)(2,1)S(1)}, u32[]{:S(2)}, u32[]{:S(2)}) collective-permute-start(bf16[144,640]{1,0:T(8,128)(2,1)S(1)} %collective-permute-done.6.refs_5_), channel_id=1, source_target_pairs={{0,224},{16,240},{32,0},{48,16},{64,32},{80,48},{96,64},{112,80},{... | collective-permute-start | bytes 552968 | tf_op jit(solution)/shard_map/ppermute | solution.py:319
  95.9 6.7 %collective-permute-start.4 = (bf16[144,640]{1,0:T(8,128)(2,1)S(1)}, bf16[144,640]{1,0:T(8,128)(2,1)S(1)}, u32[]{:S(2)}, u32[]{:S(2)}) collective-permute-start(bf16[144,640]{1,0:T(8,128)(2,1)S(1)} %collective-permute-done.3.refs_2_), channel_id=1, source_target_pairs={{0,32},{16,48},{32,64},{48,80},{64,96},{80,112},{96,128},{112,144}... | collective-permute-start | bytes 552968 | tf_op jit(solution)/shard_map/ppermute | solution.py:317
  103.6 6.4 %collective-permute-start.17 = (bf16[128,640]{1,0:T(8,128)(2,1)S(1)}, bf16[128,640]{1,0:T(8,128)(2,1)S(1)}, u32[]{:S(2)}, u32[]{:S(2)}) collective-permute-start(bf16[128,640]{1,0:T(8,128)(2,1)S(1)} %get-tuple-element.42), channel_id=1, source_target_pairs={{0,16},{16,0},{32,48},{48,32},{64,80},{80,64},{96,112},{112,96},{1... | collective-permute-start | bytes 491528 | tf_op jit(solution)/shard_map/ppermute | solution.py:325
  103.6 1.5 copy-start.4
  120.0 7.3 %copy-start.7 = (bf16[144,384]{1,0:T(8,128)(2,1)S(1)}, bf16[144,384]{1,0:T(8,128)(2,1)}, u32[]{:S(2)}) copy-start(bf16[144,384]{1,0:T(8,128)(2,1)} %get-tuple-element.35) | copy-start | bytes 331780
  120.0 8.8 %copy-start.1 = (bf16[144,384]{1,0:T(8,128)(2,1)S(1)}, bf16[144,384]{1,0:T(8,128)(2,1)}, u32[]{:S(2)}) copy-start(bf16[144,384]{1,0:T(8,128)(2,1)} %get-tuple-element.30.keep_ref) | copy-start | bytes 331780
  120.1 44.6 %all-to-all-start.2 = ((bf16[16,128,640]{2,1,0:T(8,128)(2,1)}), bf16[16,128,640]{2,1,0:T(8,128)(2,1)S(1)}, u32[]{:S(2)}, u32[]{:S(2)}) async-start(bf16[16,128,640]{2,1,0:T(8,128)(2,1)} %mix0.1), calls=%async_computation.2 | async-start | bytes 5242880 | tf_op jit(solution)/shard_map/all_to_all | solution.py:508
  127.4 1.4 collective-permute-start.8
  128.9 10.4 %collective-permute-start.9 = (bf16[144,384]{1,0:T(8,128)(2,1)S(1)}, bf16[144,384]{1,0:T(8,128)(2,1)S(1)}, u32[]{:S(2)}, u32[]{:S(2)}) collective-permute-start(bf16[144,384]{1,0:T(8,128)(2,1)S(1)} %chip1.1), channel_id=1, source_target_pairs={{0,32},{16,48},{32,64},{48,80},{64,96},{80,112},{96,128},{112,144}... | collective-permute-start | bytes 331784 | tf_op jit(solution)/shard_map/ppermute | solution.py:317
  129.2 10.1 %collective-permute-start.10 = (bf16[144,384]{1,0:T(8,128)(2,1)S(1)}, bf16[144,384]{1,0:T(8,128)(2,1)S(1)}, u32[]{:S(2)}, u32[]{:S(2)}) collective-permute-start(bf16[144,384]{1,0:T(8,128)(2,1)S(1)} %chip1.1), channel_id=1, source_target_pairs={{0,224},{16,240},{32,0},{48,16},{64,32},{80,48},{96,64},{112,80},{... | collective-permute-start | bytes 331784 | tf_op jit(solution)/shard_map/ppermute | solution.py:319
  139.3 6.1 %collective-permute-start.11 = (bf16[144,384]{1,0:T(8,128)(2,1)S(1)}, bf16[144,384]{1,0:T(8,128)(2,1)S(1)}, u32[]{:S(2)}, u32[]{:S(2)}) collective-permute-start(bf16[144,384]{1,0:T(8,128)(2,1)S(1)} %collective-permute-done.9.refs_0_), channel_id=1, source_target_pairs={{0,32},{16,48},{32,64},{48,80},{64,96},{80,112},{96,128},{112,144}... | collective-permute-start | bytes 331784 | tf_op jit(solution)/shard_map/ppermute | solution.py:317
  139.4 6.6 %collective-permute-start.14 = (bf16[144,384]{1,0:T(8,128)(2,1)S(1)}, bf16[144,384]{1,0:T(8,128)(2,1)S(1)}, u32[]{:S(2)}, u32[]{:S(2)}) collective-permute-start(bf16[144,384]{1,0:T(8,128)(2,1)S(1)} %collective-permute-done.10.refs_6_), channel_id=1, source_target_pairs={{0,224},{16,240},{32,0},{48,16},{64,32},{80,48},{96,64},{112,80},{... | collective-permute-start | bytes 331784 | tf_op jit(solution)/shard_map/ppermute | solution.py:319
  145.4 5.8 %collective-permute-start.12 = (bf16[144,384]{1,0:T(8,128)(2,1)S(1)}, bf16[144,384]{1,0:T(8,128)(2,1)S(1)}, u32[]{:S(2)}, u32[]{:S(2)}) collective-permute-start(bf16[144,384]{1,0:T(8,128)(2,1)S(1)} %collective-permute-done.11.refs_1_), channel_id=1, source_target_pairs={{0,32},{16,48},{32,64},{48,80},{64,96},{80,112},{96,128},{112,144}... | collective-permute-start | bytes 331784 | tf_op jit(solution)/shard_map/ppermute | solution.py:317
  146.0 5.8 %collective-permute-start.15 = (bf16[144,384]{1,0:T(8,128)(2,1)S(1)}, bf16[144,384]{1,0:T(8,128)(2,1)S(1)}, u32[]{:S(2)}, u32[]{:S(2)}) collective-permute-start(bf16[144,384]{1,0:T(8,128)(2,1)S(1)} %collective-permute-done.14.refs_5_), channel_id=1, source_target_pairs={{0,224},{16,240},{32,0},{48,16},{64,32},{80,48},{96,64},{112,80},{... | collective-permute-start | bytes 331784 | tf_op jit(solution)/shard_map/ppermute | solution.py:319
  151.2 6.0 %collective-permute-start.13 = (bf16[144,384]{1,0:T(8,128)(2,1)S(1)}, bf16[144,384]{1,0:T(8,128)(2,1)S(1)}, u32[]{:S(2)}, u32[]{:S(2)}) collective-permute-start(bf16[144,384]{1,0:T(8,128)(2,1)S(1)} %collective-permute-done.12.refs_2_), channel_id=1, source_target_pairs={{0,32},{16,48},{32,64},{48,80},{64,96},{80,112},{96,128},{112,144}... | collective-permute-start | bytes 331784 | tf_op jit(solution)/shard_map/ppermute | solution.py:317
  157.9 1.3 collective-permute-start.16
  164.7 31.4 %all-to-all-start.3 = ((bf16[16,128,384]{2,1,0:T(8,128)(2,1)}), bf16[16,128,384]{2,1,0:T(8,128)(2,1)}, u32[]{:S(2)}, u32[]{:S(2)}) async-start(bf16[16,128,384]{2,1,0:T(8,128)(2,1)} %join1.1), calls=%async_computation.3 | async-start | bytes 3145728 | tf_op jit(solution)/shard_map/all_to_all | solution.py:508
  (5 other events, 3.5 us)

commit v4 on v3

--- a/solution.py
+++ b/solution.py
@@ -23,6 +23,10 @@
 F32 = jnp.float32
 BF16 = jnp.bfloat16
 VMEM_LIMIT = 60 * 1024 * 1024
+
+
+def far(*arrays):
+    return [pltpu.with_memory_space_constraint(x, pltpu.HBM) for x in arrays]
 
 
 def dot(a, b, dims):
@@ -231,6 +235,7 @@
         functools.partial(states_kernel, part),
         "states%d" % part,
         (2**30, 5, 2**20),
+        limit=(60 - 20 * part) * 1024 * 1024,
         grid=(slabs // SLABS,),
         in_specs=[
             smem_spec(),
@@ -241,7 +246,7 @@
         out_specs=out_specs,
         out_shape=out_shape,
         scratch_shapes=[pltpu.VMEM((N, width), F32), pltpu.VMEM((1, width), F32)],
-    )(core, msg, first, first if part == 0 else sums)
+    )(core, msg, *far(first, first if part == 0 else sums))
 
 
 def halves(core_ref, keep_ref, got_ref):
@@ -391,6 +396,7 @@
         functools.partial(mix_kernel, part),
         "mix%d" % part,
         (4 * 2**30, 14, 2**22),
+        limit=44 * 1024 * 1024,
         grid=(slabs // SLABS,),
         in_specs=[smem_spec()] * 2
         + [half_spec(width)] * 2
@@ -398,7 +404,7 @@
         out_specs=x_spec(width),
         out_shape=jax.ShapeDtypeStruct((slabs, ROWS, width), BF16),
         scratch_shapes=[pltpu.VMEM((N, width), F32)],
-    )(core, gains, mine, got, (first, second)[part], first, second, second, sums)
+    )(core, gains, mine, got, *far(first, first), second, second, *far(sums))
 
 
 def inside_kernel(part, gain_ref, x_ref, b_ref, c_ref, more_ref, sums_ref, out_ref, state):
@@ -429,7 +435,7 @@
         out_specs=flat_spec(width),
         out_shape=jax.ShapeDtypeStruct((slabs * ROWS, width), BF16),
         scratch_shapes=[pltpu.VMEM((N, width), F32)],
-    )(gains, (first, second)[part], first, second, second, sums)
+    )(gains, *far((first, second)[part], first, second, second, sums))
 
 
 def join_kernel(
@@ -470,7 +476,7 @@
         out_specs=x_spec(width),
         out_shape=jax.ShapeDtypeStruct((slabs, ROWS, width), BF16),
         scratch_shapes=[pltpu.VMEM((N, width), BF16), pltpu.VMEM((1, width), F32)],
-    )(core, mine, got, second, second, sums, own)
+    )(core, mine, got, *far(second, second, sums, own))
 
 
 def unpack_kernel(part, *refs):

time: 202 us -> 199 us (0.985)
    unnamed x16 -> x12, local copies, waits for them, and re-layouts: 5.04 us -> 3.72 us
where the time goes in v4:
time: 199 us; the launch traced here: 196 us
  waiting for transfers between devices  57.8 us (29%)
  blocking collectives  55.3 us (28%)
  Pallas kernels  41.4 us (21%)
  starting transfers between devices  37.2 us (19%)
  local copies, waits for them, and re-layouts  3.72 us (2%)
    all_to_all x1, blocking collectives, exchange(): return lax.all_to_all(msg, 'head', split_axis=0, concat_axis=0, tiled=True)  55.3 us
    ppermute x8, waiting for transfers between devices, incoming(): forward.append(lax.ppermute(forward[-1], 'ctx', ahead))  29.8 us
    all_to_all x3, waiting for transfers between devices, exchange(): return lax.all_to_all(msg, 'head', split_axis=0, concat_axis=0, tiled=True)  22.1 us
    all_to_all x3, starting transfers between devices, exchange(): return lax.all_to_all(msg, 'head', split_axis=0, concat_axis=0, tiled=True)  18.4 us
    ppermute x6, starting transfers between devices, incoming(): backward.append(lax.ppermute(backward[-1], 'ctx', back))  14 us
    pallas_call x2, Pallas kernels, end_states(): call(functools.partial(states_kernel, part), 'states%d' % part, (2 ** 30,...  10.9 us
    pallas_call x1, Pallas kernels, mix(): call(functools.partial(mix_kernel, part), 'mix%d' % part, (4 * 2 ** 30, 1...  8.34 us
    pallas_call x1, Pallas kernels, inside(): call(functools.partial(inside_kernel, part), 'inside%d' % part, (4 * 2 **...  6.87 us
  transfers between devices with their start and end apart: 21, of which 15 were waited for; matrix products, arithmetic and copies ran while one was open for 0% of the time, Pallas kernels for 13%

profile of v4, /device:TPU:32, one launch (start us, length us, event | category | flops | bytes accessed | tf_op | source)
XLA Modules:
  0.0 195.9 jit_solution(16159257242486326484)
XLA Ops:
  0.0 5.7 %pack.1 = (bf16[16,192,640]{2,1,0:T(8,128)(2,1)}, bf16[16,224,384]{2,1,0:T(8,128)(2,1)}) custom-call(bf16[128,16384]{1,0:T(8,128)(2,1)} %x_ref.1, bf16[128,2048]{1,0:T(8,128)(2,1)} %b_ref.1, bf16[128,2048]{1,0:T(8,128)(2,1)} %c_ref.1, bf16[128,256]{1,0:T(8,128)(2,1)} %d_ref.1), custom_call_target="tpu_custom_call" | custom-call | bytes 12582912 | tf_op jit(solution)/shard_map/pack/pallas_call | solution.py:81
  5.7 55.3 %all_to_all.20.refs_1_.refs_2_.refs_3_.b_ref.x_ref = bf16[16,192,640]{2,1,0:T(8,128)(2,1)} all-to-all(bf16[16,192,640]{2,1,0:T(8,128)(2,1)} %get-tuple-element.26), channel_id=1, replica_groups=mesh['ctx'=16,'head'=16] {'head'}, dimensions={0} | all-to-all | bytes 7864320 | tf_op jit(solution)/shard_map/all_to_all | solution.py:514
  61.0 3.8 %all-to-all-start.1 = ((bf16[16,224,384]{2,1,0:T(8,128)(2,1)}), bf16[16,224,384]{2,1,0:T(8,128)(2,1)S(1)}, u32[]{:S(2)}, u32[]{:S(2)}) async-start(bf16[16,224,384]{2,1,0:T(8,128)(2,1)} %get-tuple-element.27), calls=%async_computation.1 | async-start | bytes 5505024 | tf_op jit(solution)/shard_map/all_to_all | solution.py:514
  64.9 6.5 %states0.1 = (bf16[144,640]{1,0:T(8,128)(2,1)}, bf16[144,640]{1,0:T(8,128)(2,1)}, bf16[2048,128]{1,0:T(8,128)(2,1)}) custom-call(s32[1]{0:T(128)S(6)} %select_n.12.refs_0_.core_ref, bf16[16,192,640]{2,1,0:T(8,128)(2,1)} %all_to_all.20.refs_1_.refs_2_.refs_3_.b_ref.x_ref, bf16[16,192,640]{2,1,0:T(8,128)(2,1)} %all_to_all.20.refs_1_.refs_2_.refs_3_.b_ref.x_ref, ...), custom_call_target="tpu_custom_call" | custom-call | flops 1073741824 | bytes 5242880 | tf_op jit(solution)/shard_map/states0/pallas_call | solution.py:234
  76.1 4.7 %collective-permute-done.1.refs_0_ = bf16[144,640]{1,0:T(8,128)(2,1)S(1)} collective-permute-done((bf16[144,640]{1,0:T(8,128)(2,1)S(1)}, bf16[144,640]{1,0:T(8,128)(2,1)S(1)}, u32[]{:S(2)}, u32[]{:S(2)}) %collective-permute-start.1) | collective-permute-done | bytes 184352 | tf_op jit(solution)/shard_map/ppermute | solution.py:322
  82.7 2.3 %collective-permute-start.6 = (bf16[144,640]{1,0:T(8,128)(2,1)S(1)}, bf16[144,640]{1,0:T(8,128)(2,1)S(1)}, u32[]{:S(2)}, u32[]{:S(2)}) collective-permute-start(bf16[144,640]{1,0:T(8,128)(2,1)S(1)} %collective-permute-done.5.refs_6_), channel_id=1, source_target_pairs={{0,224},{16,240},{32,0},{48,16},{64,32},{80,48},{96,64},{112,80},{... | collective-permute-start | bytes 552968 | tf_op jit(solution)/shard_map/ppermute | solution.py:324
  85.0 4.4 %collective-permute-done.2.refs_1_ = bf16[144,640]{1,0:T(8,128)(2,1)S(1)} collective-permute-done((bf16[144,640]{1,0:T(8,128)(2,1)S(1)}, bf16[144,640]{1,0:T(8,128)(2,1)S(1)}, u32[]{:S(2)}, u32[]{:S(2)}) %collective-permute-start.2) | collective-permute-done | bytes 184352 | tf_op jit(solution)/shard_map/ppermute | solution.py:322
  89.8 2.6 %collective-permute-start.7 = (bf16[144,640]{1,0:T(8,128)(2,1)S(1)}, bf16[144,640]{1,0:T(8,128)(2,1)S(1)}, u32[]{:S(2)}, u32[]{:S(2)}) collective-permute-start(bf16[144,640]{1,0:T(8,128)(2,1)S(1)} %collective-permute-done.6.refs_5_), channel_id=1, source_target_pairs={{0,224},{16,240},{32,0},{48,16},{64,32},{80,48},{96,64},{112,80},{... | collective-permute-start | bytes 552968 | tf_op jit(solution)/shard_map/ppermute | solution.py:324
  92.4 3.5 %collective-permute-done.3.refs_2_ = bf16[144,640]{1,0:T(8,128)(2,1)S(1)} collective-permute-done((bf16[144,640]{1,0:T(8,128)(2,1)S(1)}, bf16[144,640]{1,0:T(8,128)(2,1)S(1)}, u32[]{:S(2)}, u32[]{:S(2)}) %collective-permute-start.3) | collective-permute-done | bytes 184352 | tf_op jit(solution)/shard_map/ppermute | solution.py:322
  96.3 6.3 %collective-permute-done.4.refs_3_ = bf16[144,640]{1,0:T(8,128)(2,1)S(1)} collective-permute-done((bf16[144,640]{1,0:T(8,128)(2,1)S(1)}, bf16[144,640]{1,0:T(8,128)(2,1)S(1)}, u32[]{:S(2)}, u32[]{:S(2)}) %collective-permute-start.4) | collective-permute-done | bytes 184352 | tf_op jit(solution)/shard_map/ppermute | solution.py:322
  103.0 4.4 %states1.1 = (bf16[144,384]{1,0:T(8,128)(2,1)S(1)}, bf16[144,384]{1,0:T(8,128)(2,1)S(1)}) custom-call(s32[1]{0:T(128)S(6)} %select_n.12.refs_0_.core_ref, bf16[16,224,384]{2,1,0:T(8,128)(2,1)S(1)} %all-to-all-done.1.refs_1_.x_ref.c_ref.more_ref, bf16[16,192,640]{2,1,0:T(8,128)(2,1)} %all_to_all.20.refs_1_.refs_2_.refs_3_.b_ref.x_ref, ...), custom_call_target="tpu_custom_call" | custom-call | flops 1073741824 | bytes 5242880 | tf_op jit(solution)/shard_map/states1/pallas_call | solution.py:234
  107.5 8.3 %mix0.1 = bf16[16,128,640]{2,1,0:T(8,128)(2,1)S(1)} custom-call(s32[1]{0:T(128)S(6)} %select_n.12.refs_0_.core_ref, f32[16]{0:T(128)S(1)} %copy-done.4, bf16[128,640]{1,0:T(8,128)(2,1)S(1)} %get-tuple-element.41.mine_ref, bf16[128,640]{1,0:T(8,128)(2,1)S(1)} %collective-permute-done.17.got_ref, ...), custom_call_target="tpu_custom_call" | custom-call | flops 4294967296 | bytes 14680064 | tf_op jit(solution)/shard_map/mix0/pallas_call | solution.py:395
  117.4 7.2 %all-to-all-start.2 = ((bf16[16,128,640]{2,1,0:T(8,128)(2,1)}), bf16[16,128,640]{2,1,0:T(8,128)(2,1)S(1)}, u32[]{:S(2)}, u32[]{:S(2)}) async-start(bf16[16,128,640]{2,1,0:T(8,128)(2,1)} %copy-done.1), calls=%async_computation.2 | async-start | bytes 5242880 | tf_op jit(solution)/shard_map/all_to_all | solution.py:514
  126.3 3.3 %collective-permute-start.10 = (bf16[144,384]{1,0:T(8,128)(2,1)S(1)}, bf16[144,384]{1,0:T(8,128)(2,1)S(1)}, u32[]{:S(2)}, u32[]{:S(2)}) collective-permute-start(bf16[144,384]{1,0:T(8,128)(2,1)S(1)} %chip1.1), channel_id=1, source_target_pairs={{0,224},{16,240},{32,0},{48,16},{64,32},{80,48},{96,64},{112,80},{... | collective-permute-start | bytes 331784 | tf_op jit(solution)/shard_map/ppermute | solution.py:324
  129.6 6.9 %inside1.1.own_ref = bf16[2048,384]{1,0:T(8,128)(2,1)} custom-call(f32[16]{0:T(128)} %gain_ref.3, bf16[16,224,384]{2,1,0:T(8,128)(2,1)} %copy-done, bf16[16,192,640]{2,1,0:T(8,128)(2,1)} %all_to_all.20.refs_1_.refs_2_.refs_3_.b_ref.x_ref, bf16[16,224,384]{2,1,0:T(8,128)(2,1)} %copy-done, bf16[16,224,384]{2,1,0:T(8,128)(2,1)} %copy-done, ...), custom_call_target="tpu_custom_call" | custom-call | flops 4294967296 | bytes 14680064 | tf_op jit(solution)/shard_map/inside1/pallas_call | solution.py:423
  136.6 3.2 %collective-permute-start.14 = (bf16[144,384]{1,0:T(8,128)(2,1)S(1)}, bf16[144,384]{1,0:T(8,128)(2,1)S(1)}, u32[]{:S(2)}, u32[]{:S(2)}) collective-permute-start(bf16[144,384]{1,0:T(8,128)(2,1)S(1)} %collective-permute-done.10.refs_6_), channel_id=1, source_target_pairs={{0,224},{16,240},{32,0},{48,16},{64,32},{80,48},{96,64},{112,80},{... | collective-permute-start | bytes 331784 | tf_op jit(solution)/shard_map/ppermute | solution.py:324
  139.8 2.7 %collective-permute-done.11.refs_1_ = bf16[144,384]{1,0:T(8,128)(2,1)S(1)} collective-permute-done((bf16[144,384]{1,0:T(8,128)(2,1)S(1)}, bf16[144,384]{1,0:T(8,128)(2,1)S(1)}, u32[]{:S(2)}, u32[]{:S(2)}) %collective-permute-start.11) | collective-permute-done | bytes 110624 | tf_op jit(solution)/shard_map/ppermute | solution.py:322
  143.1 2.6 %collective-permute-start.15 = (bf16[144,384]{1,0:T(8,128)(2,1)S(1)}, bf16[144,384]{1,0:T(8,128)(2,1)S(1)}, u32[]{:S(2)}, u32[]{:S(2)}) collective-permute-start(bf16[144,384]{1,0:T(8,128)(2,1)S(1)} %collective-permute-done.14.refs_5_), channel_id=1, source_target_pairs={{0,224},{16,240},{32,0},{48,16},{64,32},{80,48},{96,64},{112,80},{... | collective-permute-start | bytes 331784 | tf_op jit(solution)/shard_map/ppermute | solution.py:324
  145.7 2.7 %collective-permute-done.12.refs_2_ = bf16[144,384]{1,0:T(8,128)(2,1)S(1)} collective-permute-done((bf16[144,384]{1,0:T(8,128)(2,1)S(1)}, bf16[144,384]{1,0:T(8,128)(2,1)S(1)}, u32[]{:S(2)}, u32[]{:S(2)}) %collective-permute-start.12) | collective-permute-done | bytes 110624 | tf_op jit(solution)/shard_map/ppermute | solution.py:322
  148.9 5.4 %collective-permute-done.13.refs_3_ = bf16[144,384]{1,0:T(8,128)(2,1)S(1)} collective-permute-done((bf16[144,384]{1,0:T(8,128)(2,1)S(1)}, bf16[144,384]{1,0:T(8,128)(2,1)S(1)}, u32[]{:S(2)}, u32[]{:S(2)}) %collective-permute-start.13) | collective-permute-done | bytes 110624 | tf_op jit(solution)/shard_map/ppermute | solution.py:322
  157.1 4.8 %join1.1 = bf16[16,128,384]{2,1,0:T(8,128)(2,1)} custom-call(s32[1]{0:T(128)S(6)} %select_n.12.refs_0_.core_ref, bf16[128,384]{1,0:T(8,128)(2,1)} %copy-done.3, bf16[128,384]{1,0:T(8,128)(2,1)} %copy-done.5, bf16[16,224,384]{2,1,0:T(8,128)(2,1)} %copy-done, bf16[16,224,384]{2,1,0:T(8,128)(2,1)} %copy-done, ...), custom_call_target="tpu_custom_call" | custom-call | flops 1073741824 | bytes 8388608 | tf_op jit(solution)/shard_map/join1/pallas_call | solution.py:468
  161.9 7.4 %all-to-all-start.3 = ((bf16[16,128,384]{2,1,0:T(8,128)(2,1)}), bf16[16,128,384]{2,1,0:T(8,128)(2,1)}, u32[]{:S(2)}, u32[]{:S(2)}) async-start(bf16[16,128,384]{2,1,0:T(8,128)(2,1)} %join1.1), calls=%async_computation.3 | async-start | bytes 3145728 | tf_op jit(solution)/shard_map/all_to_all | solution.py:514
  170.9 22.1 %all-to-all-done.3.refs_0_ = bf16[16,128,384]{2,1,0:T(8,128)(2,1)} async-done(((bf16[16,128,384]{2,1,0:T(8,128)(2,1)}), bf16[16,128,384]{2,1,0:T(8,128)(2,1)}, u32[]{:S(2)}, u32[]{:S(2)}) %all-to-all-start.3) | async-done | bytes 1572896 | tf_op jit(solution)/shard_map/all_to_all | solution.py:514
  193.0 2.7 %unpack1.1 = bf16[128,16384]{1,0:T(8,128)(2,1)} custom-call(bf16[16,128,384]{2,1,0:T(8,128)(2,1)} %all-to-all-done.3.refs_0_, bf16[128,16384]{1,0:T(8,128)(2,1)} %unpack0.1.refs_1_), custom_call_target="tpu_custom_call", output_to_operand_aliasing={{}: (1, {})} | custom-call | bytes 4194304 | tf_op jit(solution)/shard_map/unpack1/pallas_call | solution.py:499
  (43 shorter events, 16.6 us)
Async XLA Ops:
  61.0 42.0 %all-to-all-start.1 = ((bf16[16,224,384]{2,1,0:T(8,128)(2,1)}), bf16[16,224,384]{2,1,0:T(8,128)(2,1)S(1)}, u32[]{:S(2)}, u32[]{:S(2)}) async-start(bf16[16,224,384]{2,1,0:T(8,128)(2,1)} %get-tuple-element.27), calls=%async_computation.1 | async-start | bytes 5505024 | tf_op jit(solution)/shard_map/all_to_all | solution.py:514
  71.4 1.6 collective-permute-start
  74.0 6.8 %collective-permute-start.1 = (bf16[144,640]{1,0:T(8,128)(2,1)S(1)}, bf16[144,640]{1,0:T(8,128)(2,1)S(1)}, u32[]{:S(2)}, u32[]{:S(2)}) collective-permute-start(bf16[144,640]{1,0:T(8,128)(2,1)S(1)} %chip0.1), channel_id=1, source_target_pairs={{0,32},{16,48},{32,64},{48,80},{64,96},{80,112},{96,128},{112,144}... | collective-permute-start | bytes 552968 | tf_op jit(solution)/shard_map/ppermute | solution.py:322
  76.0 6.7 %collective-permute-start.5 = (bf16[144,640]{1,0:T(8,128)(2,1)S(1)}, bf16[144,640]{1,0:T(8,128)(2,1)S(1)}, u32[]{:S(2)}, u32[]{:S(2)}) collective-permute-start(bf16[144,640]{1,0:T(8,128)(2,1)S(1)} %chip0.1), channel_id=1, source_target_pairs={{0,224},{16,240},{32,0},{48,16},{64,32},{80,48},{96,64},{112,80},{... | collective-permute-start | bytes 552968 | tf_op jit(solution)/shard_map/ppermute | solution.py:324
  80.8 8.7 %collective-permute-start.2 = (bf16[144,640]{1,0:T(8,128)(2,1)S(1)}, bf16[144,640]{1,0:T(8,128)(2,1)S(1)}, u32[]{:S(2)}, u32[]{:S(2)}) collective-permute-start(bf16[144,640]{1,0:T(8,128)(2,1)S(1)} %collective-permute-done.1.refs_0_), channel_id=1, source_target_pairs={{0,32},{16,48},{32,64},{48,80},{64,96},{80,112},{96,128},{112,144}... | collective-permute-start | bytes 552968 | tf_op jit(solution)/shard_map/ppermute | solution.py:322
  82.7 7.1 %collective-permute-start.6 = (bf16[144,640]{1,0:T(8,128)(2,1)S(1)}, bf16[144,640]{1,0:T(8,128)(2,1)S(1)}, u32[]{:S(2)}, u32[]{:S(2)}) collective-permute-start(bf16[144,640]{1,0:T(8,128)(2,1)S(1)} %collective-permute-done.5.refs_6_), channel_id=1, source_target_pairs={{0,224},{16,240},{32,0},{48,16},{64,32},{80,48},{96,64},{112,80},{... | collective-permute-start | bytes 552968 | tf_op jit(solution)/shard_map/ppermute | solution.py:324
  89.4 6.5 %collective-permute-start.3 = (bf16[144,640]{1,0:T(8,128)(2,1)S(1)}, bf16[144,640]{1,0:T(8,128)(2,1)S(1)}, u32[]{:S(2)}, u32[]{:S(2)}) collective-permute-start(bf16[144,640]{1,0:T(8,128)(2,1)S(1)} %collective-permute-done.2.refs_1_), channel_id=1, source_target_pairs={{0,32},{16,48},{32,64},{48,80},{64,96},{80,112},{96,128},{112,144}... | collective-permute-start | bytes 552968 | tf_op jit(solution)/shard_map/ppermute | solution.py:322
  89.8 6.5 %collective-permute-start.7 = (bf16[144,640]{1,0:T(8,128)(2,1)S(1)}, bf16[144,640]{1,0:T(8,128)(2,1)S(1)}, u32[]{:S(2)}, u32[]{:S(2)}) collective-permute-start(bf16[144,640]{1,0:T(8,128)(2,1)S(1)} %collective-permute-done.6.refs_5_), channel_id=1, source_target_pairs={{0,224},{16,240},{32,0},{48,16},{64,32},{80,48},{96,64},{112,80},{... | collective-permute-start | bytes 552968 | tf_op jit(solution)/shard_map/ppermute | solution.py:324
  95.9 6.7 %collective-permute-start.4 = (bf16[144,640]{1,0:T(8,128)(2,1)S(1)}, bf16[144,640]{1,0:T(8,128)(2,1)S(1)}, u32[]{:S(2)}, u32[]{:S(2)}) collective-permute-start(bf16[144,640]{1,0:T(8,128)(2,1)S(1)} %collective-permute-done.3.refs_2_), channel_id=1, source_target_pairs={{0,32},{16,48},{32,64},{48,80},{64,96},{80,112},{96,128},{112,144}... | collective-permute-start | bytes 552968 | tf_op jit(solution)/shard_map/ppermute | solution.py:322
  102.9 4.6 %collective-permute-start.17 = (bf16[128,640]{1,0:T(8,128)(2,1)S(1)}, bf16[128,640]{1,0:T(8,128)(2,1)S(1)}, u32[]{:S(2)}, u32[]{:S(2)}) collective-permute-start(bf16[128,640]{1,0:T(8,128)(2,1)S(1)} %get-tuple-element.42), channel_id=1, source_target_pairs={{0,16},{16,0},{32,48},{48,32},{64,80},{80,64},{96,112},{112,96},{1... | collective-permute-start | bytes 491528 | tf_op jit(solution)/shard_map/ppermute | solution.py:330
  103.0 4.5 %copy-start = (bf16[16,224,384]{2,1,0:T(8,128)(2,1)}, bf16[16,224,384]{2,1,0:T(8,128)(2,1)S(1)}, u32[]{:S(2)}) copy-start(bf16[16,224,384]{2,1,0:T(8,128)(2,1)S(1)} %all-to-all-done.1.refs_1_.x_ref.c_ref.more_ref) | copy-start | bytes 8257540
  103.0 4.5 %copy-start.4 = (f32[16]{0:T(128)S(1)}, f32[16]{0:T(128)}, u32[]{:S(2)}) copy-start(f32[16]{0:T(128)} %gain_ref.3) | copy-start | bytes 196
  115.9 1.5 copy-start.1
  117.4 44.5 %all-to-all-start.2 = ((bf16[16,128,640]{2,1,0:T(8,128)(2,1)}), bf16[16,128,640]{2,1,0:T(8,128)(2,1)S(1)}, u32[]{:S(2)}, u32[]{:S(2)}) async-start(bf16[16,128,640]{2,1,0:T(8,128)(2,1)} %copy-done.1), calls=%async_computation.2 | async-start | bytes 5242880 | tf_op jit(solution)/shard_map/all_to_all | solution.py:514
  124.6 1.6 collective-permute-start.8
  126.2 10.2 %collective-permute-start.9 = (bf16[144,384]{1,0:T(8,128)(2,1)S(1)}, bf16[144,384]{1,0:T(8,128)(2,1)S(1)}, u32[]{:S(2)}, u32[]{:S(2)}) collective-permute-start(bf16[144,384]{1,0:T(8,128)(2,1)S(1)} %chip1.1), channel_id=1, source_target_pairs={{0,32},{16,48},{32,64},{48,80},{64,96},{80,112},{96,128},{112,144}... | collective-permute-start | bytes 331784 | tf_op jit(solution)/shard_map/ppermute | solution.py:322
  126.3 10.1 %collective-permute-start.10 = (bf16[144,384]{1,0:T(8,128)(2,1)S(1)}, bf16[144,384]{1,0:T(8,128)(2,1)S(1)}, u32[]{:S(2)}, u32[]{:S(2)}) collective-permute-start(bf16[144,384]{1,0:T(8,128)(2,1)S(1)} %chip1.1), channel_id=1, source_target_pairs={{0,224},{16,240},{32,0},{48,16},{64,32},{80,48},{96,64},{112,80},{... | collective-permute-start | bytes 331784 | tf_op jit(solution)/shard_map/ppermute | solution.py:324
  136.5 6.1 %collective-permute-start.11 = (bf16[144,384]{1,0:T(8,128)(2,1)S(1)}, bf16[144,384]{1,0:T(8,128)(2,1)S(1)}, u32[]{:S(2)}, u32[]{:S(2)}) collective-permute-start(bf16[144,384]{1,0:T(8,128)(2,1)S(1)} %collective-permute-done.9.refs_0_), channel_id=1, source_target_pairs={{0,32},{16,48},{32,64},{48,80},{64,96},{80,112},{96,128},{112,144}... | collective-permute-start | bytes 331784 | tf_op jit(solution)/shard_map/ppermute | solution.py:322
  136.6 6.5 %collective-permute-start.14 = (bf16[144,384]{1,0:T(8,128)(2,1)S(1)}, bf16[144,384]{1,0:T(8,128)(2,1)S(1)}, u32[]{:S(2)}, u32[]{:S(2)}) collective-permute-start(bf16[144,384]{1,0:T(8,128)(2,1)S(1)} %collective-permute-done.10.refs_6_), channel_id=1, source_target_pairs={{0,224},{16,240},{32,0},{48,16},{64,32},{80,48},{96,64},{112,80},{... | collective-permute-start | bytes 331784 | tf_op jit(solution)/shard_map/ppermute | solution.py:324
  142.5 5.9 %collective-permute-start.12 = (bf16[144,384]{1,0:T(8,128)(2,1)S(1)}, bf16[144,384]{1,0:T(8,128)(2,1)S(1)}, u32[]{:S(2)}, u32[]{:S(2)}) collective-permute-start(bf16[144,384]{1,0:T(8,128)(2,1)S(1)} %collective-permute-done.11.refs_1_), channel_id=1, source_target_pairs={{0,32},{16,48},{32,64},{48,80},{64,96},{80,112},{96,128},{112,144}... | collective-permute-start | bytes 331784 | tf_op jit(solution)/shard_map/ppermute | solution.py:322
  143.1 5.8 %collective-permute-start.15 = (bf16[144,384]{1,0:T(8,128)(2,1)S(1)}, bf16[144,384]{1,0:T(8,128)(2,1)S(1)}, u32[]{:S(2)}, u32[]{:S(2)}) collective-permute-start(bf16[144,384]{1,0:T(8,128)(2,1)S(1)} %collective-permute-done.14.refs_5_), channel_id=1, source_target_pairs={{0,224},{16,240},{32,0},{48,16},{64,32},{80,48},{96,64},{112,80},{... | collective-permute-start | bytes 331784 | tf_op jit(solution)/shard_map/ppermute | solution.py:324
  148.4 6.0 %collective-permute-start.13 = (bf16[144,384]{1,0:T(8,128)(2,1)S(1)}, bf16[144,384]{1,0:T(8,128)(2,1)S(1)}, u32[]{:S(2)}, u32[]{:S(2)}) collective-permute-start(bf16[144,384]{1,0:T(8,128)(2,1)S(1)} %collective-permute-done.12.refs_2_), channel_id=1, source_target_pairs={{0,32},{16,48},{32,64},{48,80},{64,96},{80,112},{96,128},{112,144}... | collective-permute-start | bytes 331784 | tf_op jit(solution)/shard_map/ppermute | solution.py:322
  155.1 1.3 collective-permute-start.16
  161.9 31.2 %all-to-all-start.3 = ((bf16[16,128,384]{2,1,0:T(8,128)(2,1)}), bf16[16,128,384]{2,1,0:T(8,128)(2,1)}, u32[]{:S(2)}, u32[]{:S(2)}) async-start(bf16[16,128,384]{2,1,0:T(8,128)(2,1)} %join1.1), calls=%async_computation.3 | async-start | bytes 3145728 | tf_op jit(solution)/shard_map/all_to_all | solution.py:514
  (3 other events, 2.2 us)

commit v5 on v4

--- a/solution.py
+++ b/solution.py
@@ -228,6 +228,8 @@
     d_spec = pl.BlockSpec((SLABS, HEADS, LANES), lambda i: (i, ROWS // HEADS, 2 * N // LANES))
     out_specs = [pl.BlockSpec(shape, lambda i: (0, 0))] * 2
     out_shape = [jax.ShapeDtypeStruct(shape, BF16)] * 2
+    if part == 0:
+        out_shape[0] = pltpu.VMEM(shape, BF16)
     if part == 0:
         out_specs.append(flat_spec(LANES))
         out_shape.append(jax.ShapeDtypeStruct((slabs * ROWS, LANES), BF16))
@@ -469,12 +471,13 @@
         functools.partial(join_kernel, part),
         "join%d" % part,
         (2**30, 8, 2**20),
+        limit=44 * 1024 * 1024,
         grid=(slabs // SLABS,),
         in_specs=[smem_spec()]
         + [half_spec(width)] * 2
         + [*c_specs(), flat_spec(LANES), flat_spec(width)],
         out_specs=x_spec(width),
-        out_shape=jax.ShapeDtypeStruct((slabs, ROWS, width), BF16),
+        out_shape=pltpu.HBM((slabs, ROWS, width), BF16),
         scratch_shapes=[pltpu.VMEM((N, width), BF16), pltpu.VMEM((1, width), F32)],
     )(core, mine, got, *far(second, second, sums, own))
 

time: 199 us -> 197 us (0.990)
  local copies, waits for them, and re-layouts: 3.72 us -> 1.53 us
    unnamed x12 -> x6, local copies, waits for them, and re-layouts: 3.72 us -> 1.53 us
  transfers between devices with their start and end apart: 21 -> 21, of which waited for: 15 -> 16; matrix products, arithmetic and copies ran while one was open for 0% -> 0% of each run, Pallas kernels for 13% -> 13%
where the time goes in v5:
time: 197 us; the launch traced here: 194 us
  waiting for transfers between devices  58 us (29%)
  blocking collectives  55.3 us (28%)
  Pallas kernels  41.4 us (21%)
  starting transfers between devices  37.9 us (19%)
    all_to_all x1, blocking collectives, exchange(): return lax.all_to_all(msg, 'head', split_axis=0, concat_axis=0, tiled=True)  55.3 us
    ppermute x8, waiting for transfers between devices, incoming(): forward.append(lax.ppermute(forward[-1], 'ctx', ahead))  29.8 us
    all_to_all x3, waiting for transfers between devices, exchange(): return lax.all_to_all(msg, 'head', split_axis=0, concat_axis=0, tiled=True)  22.3 us
    all_to_all x3, starting transfers between devices, exchange(): return lax.all_to_all(msg, 'head', split_axis=0, concat_axis=0, tiled=True)  19.1 us
    ppermute x6, starting transfers between devices, incoming(): backward.append(lax.ppermute(backward[-1], 'ctx', back))  14 us
    pallas_call x2, Pallas kernels, end_states(): call(functools.partial(states_kernel, part), 'states%d' % part, (2 ** 30,...  10.9 us
    pallas_call x1, Pallas kernels, mix(): call(functools.partial(mix_kernel, part), 'mix%d' % part, (4 * 2 ** 30, 1...  8.34 us
    pallas_call x1, Pallas kernels, inside(): call(functools.partial(inside_kernel, part), 'inside%d' % part, (4 * 2 **...  6.89 us
  transfers between devices with their start and end apart: 21, of which 16 were waited for; matrix products, arithmetic and copies ran while one was open for 0% of the time, Pallas kernels for 13%

profile of v5, /device:TPU:32, one launch (start us, length us, event | category | flops | bytes accessed | tf_op | source)
XLA Modules:
  0.0 194.5 jit_solution(10564936193265332488)
XLA Ops:
  0.0 5.7 %pack.1 = (bf16[16,192,640]{2,1,0:T(8,128)(2,1)}, bf16[16,224,384]{2,1,0:T(8,128)(2,1)}) custom-call(bf16[128,16384]{1,0:T(8,128)(2,1)} %x_ref.1, bf16[128,2048]{1,0:T(8,128)(2,1)} %b_ref.1, bf16[128,2048]{1,0:T(8,128)(2,1)} %c_ref.1, bf16[128,256]{1,0:T(8,128)(2,1)} %d_ref.1), custom_call_target="tpu_custom_call" | custom-call | bytes 12582912 | tf_op jit(solution)/shard_map/pack/pallas_call | solution.py:81
  5.7 55.3 %all_to_all.20.refs_1_.refs_2_.refs_3_.b_ref.x_ref = bf16[16,192,640]{2,1,0:T(8,128)(2,1)} all-to-all(bf16[16,192,640]{2,1,0:T(8,128)(2,1)} %get-tuple-element.26), channel_id=1, replica_groups=mesh['ctx'=16,'head'=16] {'head'}, dimensions={0} | all-to-all | bytes 7864320 | tf_op jit(solution)/shard_map/all_to_all | solution.py:517
  61.0 3.8 %all-to-all-start.1 = ((bf16[16,224,384]{2,1,0:T(8,128)(2,1)}), bf16[16,224,384]{2,1,0:T(8,128)(2,1)S(1)}, u32[]{:S(2)}, u32[]{:S(2)}) async-start(bf16[16,224,384]{2,1,0:T(8,128)(2,1)} %get-tuple-element.27), calls=%async_computation.1 | async-start | bytes 5505024 | tf_op jit(solution)/shard_map/all_to_all | solution.py:517
  64.9 6.4 %states0.1 = (bf16[144,640]{1,0:T(8,128)(2,1)S(1)}, bf16[144,640]{1,0:T(8,128)(2,1)}, bf16[2048,128]{1,0:T(8,128)(2,1)}) custom-call(s32[1]{0:T(128)S(6)} %select_n.12.refs_0_.core_ref, bf16[16,192,640]{2,1,0:T(8,128)(2,1)} %all_to_all.20.refs_1_.refs_2_.refs_3_.b_ref.x_ref, bf16[16,192,640]{2,1,0:T(8,128)(2,1)} %all_to_all.20.refs_1_.refs_2_.refs_3_.b_ref.x_ref, ...), custom_call_target="tpu_custom_call" | custom-call | flops 1073741824 | bytes 5242880 | tf_op jit(solution)/shard_map/states0/pallas_call | solution.py:236
  75.2 4.7 %collective-permute-done.1.refs_0_ = bf16[144,640]{1,0:T(8,128)(2,1)S(1)} collective-permute-done((bf16[144,640]{1,0:T(8,128)(2,1)S(1)}, bf16[144,640]{1,0:T(8,128)(2,1)S(1)}, u32[]{:S(2)}, u32[]{:S(2)}) %collective-permute-start.1) | collective-permute-done | bytes 184352 | tf_op jit(solution)/shard_map/ppermute | solution.py:324
  81.7 2.3 %collective-permute-start.6 = (bf16[144,640]{1,0:T(8,128)(2,1)S(1)}, bf16[144,640]{1,0:T(8,128)(2,1)S(1)}, u32[]{:S(2)}, u32[]{:S(2)}) collective-permute-start(bf16[144,640]{1,0:T(8,128)(2,1)S(1)} %collective-permute-done.5.refs_6_), channel_id=1, source_target_pairs={{0,224},{16,240},{32,0},{48,16},{64,32},{80,48},{96,64},{112,80},{... | collective-permute-start | bytes 552968 | tf_op jit(solution)/shard_map/ppermute | solution.py:326
  84.0 4.4 %collective-permute-done.2.refs_1_ = bf16[144,640]{1,0:T(8,128)(2,1)S(1)} collective-permute-done((bf16[144,640]{1,0:T(8,128)(2,1)S(1)}, bf16[144,640]{1,0:T(8,128)(2,1)S(1)}, u32[]{:S(2)}, u32[]{:S(2)}) %collective-permute-start.2) | collective-permute-done | bytes 184352 | tf_op jit(solution)/shard_map/ppermute | solution.py:324
  88.9 2.6 %collective-permute-start.7 = (bf16[144,640]{1,0:T(8,128)(2,1)S(1)}, bf16[144,640]{1,0:T(8,128)(2,1)S(1)}, u32[]{:S(2)}, u32[]{:S(2)}) collective-permute-start(bf16[144,640]{1,0:T(8,128)(2,1)S(1)} %collective-permute-done.6.refs_5_), channel_id=1, source_target_pairs={{0,224},{16,240},{32,0},{48,16},{64,32},{80,48},{96,64},{112,80},{... | collective-permute-start | bytes 552968 | tf_op jit(solution)/shard_map/ppermute | solution.py:326
  91.4 3.5 %collective-permute-done.3.refs_2_ = bf16[144,640]{1,0:T(8,128)(2,1)S(1)} collective-permute-done((bf16[144,640]{1,0:T(8,128)(2,1)S(1)}, bf16[144,640]{1,0:T(8,128)(2,1)S(1)}, u32[]{:S(2)}, u32[]{:S(2)}) %collective-permute-start.3) | collective-permute-done | bytes 184352 | tf_op jit(solution)/shard_map/ppermute | solution.py:324
  95.3 6.3 %collective-permute-done.4.refs_3_ = bf16[144,640]{1,0:T(8,128)(2,1)S(1)} collective-permute-done((bf16[144,640]{1,0:T(8,128)(2,1)S(1)}, bf16[144,640]{1,0:T(8,128)(2,1)S(1)}, u32[]{:S(2)}, u32[]{:S(2)}) %collective-permute-start.4) | collective-permute-done | bytes 184352 | tf_op jit(solution)/shard_map/ppermute | solution.py:324
  102.0 4.5 %states1.1 = (bf16[144,384]{1,0:T(8,128)(2,1)S(1)}, bf16[144,384]{1,0:T(8,128)(2,1)S(1)}) custom-call(s32[1]{0:T(128)S(6)} %select_n.12.refs_0_.core_ref, bf16[16,224,384]{2,1,0:T(8,128)(2,1)S(1)} %all-to-all-done.1.refs_1_.x_ref.c_ref.more_ref, bf16[16,192,640]{2,1,0:T(8,128)(2,1)} %all_to_all.20.refs_1_.refs_2_.refs_3_.b_ref.x_ref, ...), custom_call_target="tpu_custom_call" | custom-call | flops 1073741824 | bytes 5242880 | tf_op jit(solution)/shard_map/states1/pallas_call | solution.py:236
  106.5 8.3 %mix0.1 = bf16[16,128,640]{2,1,0:T(8,128)(2,1)S(1)} custom-call(s32[1]{0:T(128)S(6)} %select_n.12.refs_0_.core_ref, f32[16]{0:T(128)S(1)} %copy-done.2, bf16[128,640]{1,0:T(8,128)(2,1)S(1)} %get-tuple-element.41.mine_ref, bf16[128,640]{1,0:T(8,128)(2,1)S(1)} %collective-permute-done.17.got_ref, ...), custom_call_target="tpu_custom_call" | custom-call | flops 4294967296 | bytes 14680064 | tf_op jit(solution)/shard_map/mix0/pallas_call | solution.py:397
  116.4 7.2 %all-to-all-start.2 = ((bf16[16,128,640]{2,1,0:T(8,128)(2,1)}), bf16[16,128,640]{2,1,0:T(8,128)(2,1)S(1)}, u32[]{:S(2)}, u32[]{:S(2)}) async-start(bf16[16,128,640]{2,1,0:T(8,128)(2,1)} %copy-done.1), calls=%async_computation.2 | async-start | bytes 5242880 | tf_op jit(solution)/shard_map/all_to_all | solution.py:517
  125.4 3.3 %collective-permute-start.10 = (bf16[144,384]{1,0:T(8,128)(2,1)S(1)}, bf16[144,384]{1,0:T(8,128)(2,1)S(1)}, u32[]{:S(2)}, u32[]{:S(2)}) collective-permute-start(bf16[144,384]{1,0:T(8,128)(2,1)S(1)} %chip1.1), channel_id=1, source_target_pairs={{0,224},{16,240},{32,0},{48,16},{64,32},{80,48},{96,64},{112,80},{... | collective-permute-start | bytes 331784 | tf_op jit(solution)/shard_map/ppermute | solution.py:326
  128.6 6.9 %inside1.1.own_ref = bf16[2048,384]{1,0:T(8,128)(2,1)} custom-call(f32[16]{0:T(128)} %gain_ref.3, bf16[16,224,384]{2,1,0:T(8,128)(2,1)} %copy-done, bf16[16,192,640]{2,1,0:T(8,128)(2,1)} %all_to_all.20.refs_1_.refs_2_.refs_3_.b_ref.x_ref, bf16[16,224,384]{2,1,0:T(8,128)(2,1)} %copy-done, bf16[16,224,384]{2,1,0:T(8,128)(2,1)} %copy-done, ...), custom_call_target="tpu_custom_call" | custom-call | flops 4294967296 | bytes 14680064 | tf_op jit(solution)/shard_map/inside1/pallas_call | solution.py:425
  135.6 3.2 %collective-permute-start.14 = (bf16[144,384]{1,0:T(8,128)(2,1)S(1)}, bf16[144,384]{1,0:T(8,128)(2,1)S(1)}, u32[]{:S(2)}, u32[]{:S(2)}) collective-permute-start(bf16[144,384]{1,0:T(8,128)(2,1)S(1)} %collective-permute-done.10.refs_6_), channel_id=1, source_target_pairs={{0,224},{16,240},{32,0},{48,16},{64,32},{80,48},{96,64},{112,80},{... | collective-permute-start | bytes 331784 | tf_op jit(solution)/shard_map/ppermute | solution.py:326
  138.8 2.7 %collective-permute-done.11.refs_1_ = bf16[144,384]{1,0:T(8,128)(2,1)S(1)} collective-permute-done((bf16[144,384]{1,0:T(8,128)(2,1)S(1)}, bf16[144,384]{1,0:T(8,128)(2,1)S(1)}, u32[]{:S(2)}, u32[]{:S(2)}) %collective-permute-start.11) | collective-permute-done | bytes 110624 | tf_op jit(solution)/shard_map/ppermute | solution.py:324
  142.2 2.5 %collective-permute-start.15 = (bf16[144,384]{1,0:T(8,128)(2,1)S(1)}, bf16[144,384]{1,0:T(8,128)(2,1)S(1)}, u32[]{:S(2)}, u32[]{:S(2)}) collective-permute-start(bf16[144,384]{1,0:T(8,128)(2,1)S(1)} %collective-permute-done.14.refs_5_), channel_id=1, source_target_pairs={{0,224},{16,240},{32,0},{48,16},{64,32},{80,48},{96,64},{112,80},{... | collective-permute-start | bytes 331784 | tf_op jit(solution)/shard_map/ppermute | solution.py:326
  144.7 2.7 %collective-permute-done.12.refs_2_ = bf16[144,384]{1,0:T(8,128)(2,1)S(1)} collective-permute-done((bf16[144,384]{1,0:T(8,128)(2,1)S(1)}, bf16[144,384]{1,0:T(8,128)(2,1)S(1)}, u32[]{:S(2)}, u32[]{:S(2)}) %collective-permute-start.12) | collective-permute-done | bytes 110624 | tf_op jit(solution)/shard_map/ppermute | solution.py:324
  148.0 5.4 %collective-permute-done.13.refs_3_ = bf16[144,384]{1,0:T(8,128)(2,1)S(1)} collective-permute-done((bf16[144,384]{1,0:T(8,128)(2,1)S(1)}, bf16[144,384]{1,0:T(8,128)(2,1)S(1)}, u32[]{:S(2)}, u32[]{:S(2)}) %collective-permute-start.13) | collective-permute-done | bytes 110624 | tf_op jit(solution)/shard_map/ppermute | solution.py:324
  154.9 4.8 %join1.1 = bf16[16,128,384]{2,1,0:T(8,128)(2,1)} custom-call(s32[1]{0:T(128)S(6)} %select_n.12.refs_0_.core_ref, bf16[128,384]{1,0:T(8,128)(2,1)S(1)} %get-tuple-element.38.mine_ref, bf16[128,384]{1,0:T(8,128)(2,1)S(1)} %collective-permute-done.16.got_ref, bf16[16,224,384]{2,1,0:T(8,128)(2,1)} %copy-done, bf16[16,224,384]{2,1,0:T(8,128)(2,1)} %copy-done, ...), custom_call_target="tpu_custom_call" | custom-call | flops 1073741824 | bytes 8388608 | tf_op jit(solution)/shard_map/join1/pallas_call | solution.py:470
  160.2 8.0 %all-to-all-start.3 = ((bf16[16,128,384]{2,1,0:T(8,128)(2,1)}), bf16[16,128,384]{2,1,0:T(8,128)(2,1)}, u32[]{:S(2)}, u32[]{:S(2)}) async-start(bf16[16,128,384]{2,1,0:T(8,128)(2,1)} %join1.1), calls=%async_computation.3 | async-start | bytes 3145728 | tf_op jit(solution)/shard_map/all_to_all | solution.py:517
  169.9 21.7 %all-to-all-done.3.refs_0_ = bf16[16,128,384]{2,1,0:T(8,128)(2,1)} async-done(((bf16[16,128,384]{2,1,0:T(8,128)(2,1)}), bf16[16,128,384]{2,1,0:T(8,128)(2,1)}, u32[]{:S(2)}, u32[]{:S(2)}) %all-to-all-start.3) | async-done | bytes 1572896 | tf_op jit(solution)/shard_map/all_to_all | solution.py:517
  191.6 2.7 %unpack1.1 = bf16[128,16384]{1,0:T(8,128)(2,1)} custom-call(bf16[16,128,384]{2,1,0:T(8,128)(2,1)} %all-to-all-done.3.refs_0_, bf16[128,16384]{1,0:T(8,128)(2,1)} %unpack0.1.refs_1_), custom_call_target="tpu_custom_call", output_to_operand_aliasing={{}: (1, {})} | custom-call | bytes 4194304 | tf_op jit(solution)/shard_map/unpack1/pallas_call | solution.py:502
  (37 shorter events, 15.1 us)
Async XLA Ops:
  61.0 41.0 %all-to-all-start.1 = ((bf16[16,224,384]{2,1,0:T(8,128)(2,1)}), bf16[16,224,384]{2,1,0:T(8,128)(2,1)S(1)}, u32[]{:S(2)}, u32[]{:S(2)}) async-start(bf16[16,224,384]{2,1,0:T(8,128)(2,1)} %get-tuple-element.27), calls=%async_computation.1 | async-start | bytes 5505024 | tf_op jit(solution)/shard_map/all_to_all | solution.py:517
  71.3 1.6 collective-permute-start
  73.1 6.8 %collective-permute-start.1 = (bf16[144,640]{1,0:T(8,128)(2,1)S(1)}, bf16[144,640]{1,0:T(8,128)(2,1)S(1)}, u32[]{:S(2)}, u32[]{:S(2)}) collective-permute-start(bf16[144,640]{1,0:T(8,128)(2,1)S(1)} %chip0.1), channel_id=1, source_target_pairs={{0,32},{16,48},{32,64},{48,80},{64,96},{80,112},{96,128},{112,144}... | collective-permute-start | bytes 552968 | tf_op jit(solution)/shard_map/ppermute | solution.py:324
  75.0 6.7 %collective-permute-start.5 = (bf16[144,640]{1,0:T(8,128)(2,1)S(1)}, bf16[144,640]{1,0:T(8,128)(2,1)S(1)}, u32[]{:S(2)}, u32[]{:S(2)}) collective-permute-start(bf16[144,640]{1,0:T(8,128)(2,1)S(1)} %chip0.1), channel_id=1, source_target_pairs={{0,224},{16,240},{32,0},{48,16},{64,32},{80,48},{96,64},{112,80},{... | collective-permute-start | bytes 552968 | tf_op jit(solution)/shard_map/ppermute | solution.py:326
  79.8 8.7 %collective-permute-start.2 = (bf16[144,640]{1,0:T(8,128)(2,1)S(1)}, bf16[144,640]{1,0:T(8,128)(2,1)S(1)}, u32[]{:S(2)}, u32[]{:S(2)}) collective-permute-start(bf16[144,640]{1,0:T(8,128)(2,1)S(1)} %collective-permute-done.1.refs_0_), channel_id=1, source_target_pairs={{0,32},{16,48},{32,64},{48,80},{64,96},{80,112},{96,128},{112,144}... | collective-permute-start | bytes 552968 | tf_op jit(solution)/shard_map/ppermute | solution.py:324
  81.7 7.1 %collective-permute-start.6 = (bf16[144,640]{1,0:T(8,128)(2,1)S(1)}, bf16[144,640]{1,0:T(8,128)(2,1)S(1)}, u32[]{:S(2)}, u32[]{:S(2)}) collective-permute-start(bf16[144,640]{1,0:T(8,128)(2,1)S(1)} %collective-permute-done.5.refs_6_), channel_id=1, source_target_pairs={{0,224},{16,240},{32,0},{48,16},{64,32},{80,48},{96,64},{112,80},{... | collective-permute-start | bytes 552968 | tf_op jit(solution)/shard_map/ppermute | solution.py:326
  88.5 6.5 %collective-permute-start.3 = (bf16[144,640]{1,0:T(8,128)(2,1)S(1)}, bf16[144,640]{1,0:T(8,128)(2,1)S(1)}, u32[]{:S(2)}, u32[]{:S(2)}) collective-permute-start(bf16[144,640]{1,0:T(8,128)(2,1)S(1)} %collective-permute-done.2.refs_1_), channel_id=1, source_target_pairs={{0,32},{16,48},{32,64},{48,80},{64,96},{80,112},{96,128},{112,144}... | collective-permute-start | bytes 552968 | tf_op jit(solution)/shard_map/ppermute | solution.py:324
  88.9 6.5 %collective-permute-start.7 = (bf16[144,640]{1,0:T(8,128)(2,1)S(1)}, bf16[144,640]{1,0:T(8,128)(2,1)S(1)}, u32[]{:S(2)}, u32[]{:S(2)}) collective-permute-start(bf16[144,640]{1,0:T(8,128)(2,1)S(1)} %collective-permute-done.6.refs_5_), channel_id=1, source_target_pairs={{0,224},{16,240},{32,0},{48,16},{64,32},{80,48},{96,64},{112,80},{... | collective-permute-start | bytes 552968 | tf_op jit(solution)/shard_map/ppermute | solution.py:326
  94.9 6.7 %collective-permute-start.4 = (bf16[144,640]{1,0:T(8,128)(2,1)S(1)}, bf16[144,640]{1,0:T(8,128)(2,1)S(1)}, u32[]{:S(2)}, u32[]{:S(2)}) collective-permute-start(bf16[144,640]{1,0:T(8,128)(2,1)S(1)} %collective-permute-done.3.refs_2_), channel_id=1, source_target_pairs={{0,32},{16,48},{32,64},{48,80},{64,96},{80,112},{96,128},{112,144}... | collective-permute-start | bytes 552968 | tf_op jit(solution)/shard_map/ppermute | solution.py:324
  101.9 4.6 %collective-permute-start.17 = (bf16[128,640]{1,0:T(8,128)(2,1)S(1)}, bf16[128,640]{1,0:T(8,128)(2,1)S(1)}, u32[]{:S(2)}, u32[]{:S(2)}) collective-permute-start(bf16[128,640]{1,0:T(8,128)(2,1)S(1)} %get-tuple-element.42), channel_id=1, source_target_pairs={{0,16},{16,0},{32,48},{48,32},{64,80},{80,64},{96,112},{112,96},{1... | collective-permute-start | bytes 491528 | tf_op jit(solution)/shard_map/ppermute | solution.py:332
  102.0 4.5 %copy-start = (bf16[16,224,384]{2,1,0:T(8,128)(2,1)}, bf16[16,224,384]{2,1,0:T(8,128)(2,1)S(1)}, u32[]{:S(2)}) copy-start(bf16[16,224,384]{2,1,0:T(8,128)(2,1)S(1)} %all-to-all-done.1.refs_1_.x_ref.c_ref.more_ref) | copy-start | bytes 8257540
  102.0 4.5 %copy-start.2 = (f32[16]{0:T(128)S(1)}, f32[16]{0:T(128)}, u32[]{:S(2)}) copy-start(f32[16]{0:T(128)} %gain_ref.3) | copy-start | bytes 196
  114.9 1.5 copy-start.1
  116.4 43.8 %all-to-all-start.2 = ((bf16[16,128,640]{2,1,0:T(8,128)(2,1)}), bf16[16,128,640]{2,1,0:T(8,128)(2,1)S(1)}, u32[]{:S(2)}, u32[]{:S(2)}) async-start(bf16[16,128,640]{2,1,0:T(8,128)(2,1)} %copy-done.1), calls=%async_computation.2 | async-start | bytes 5242880 | tf_op jit(solution)/shard_map/all_to_all | solution.py:517
  123.6 1.6 collective-permute-start.8
  125.3 10.2 %collective-permute-start.9 = (bf16[144,384]{1,0:T(8,128)(2,1)S(1)}, bf16[144,384]{1,0:T(8,128)(2,1)S(1)}, u32[]{:S(2)}, u32[]{:S(2)}) collective-permute-start(bf16[144,384]{1,0:T(8,128)(2,1)S(1)} %chip1.1), channel_id=1, source_target_pairs={{0,32},{16,48},{32,64},{48,80},{64,96},{80,112},{96,128},{112,144}... | collective-permute-start | bytes 331784 | tf_op jit(solution)/shard_map/ppermute | solution.py:324
  125.4 10.2 %collective-permute-start.10 = (bf16[144,384]{1,0:T(8,128)(2,1)S(1)}, bf16[144,384]{1,0:T(8,128)(2,1)S(1)}, u32[]{:S(2)}, u32[]{:S(2)}) collective-permute-start(bf16[144,384]{1,0:T(8,128)(2,1)S(1)} %chip1.1), channel_id=1, source_target_pairs={{0,224},{16,240},{32,0},{48,16},{64,32},{80,48},{96,64},{112,80},{... | collective-permute-start | bytes 331784 | tf_op jit(solution)/shard_map/ppermute | solution.py:326
  135.5 6.1 %collective-permute-start.11 = (bf16[144,384]{1,0:T(8,128)(2,1)S(1)}, bf16[144,384]{1,0:T(8,128)(2,1)S(1)}, u32[]{:S(2)}, u32[]{:S(2)}) collective-permute-start(bf16[144,384]{1,0:T(8,128)(2,1)S(1)} %collective-permute-done.9.refs_0_), channel_id=1, source_target_pairs={{0,32},{16,48},{32,64},{48,80},{64,96},{80,112},{96,128},{112,144}... | collective-permute-start | bytes 331784 | tf_op jit(solution)/shard_map/ppermute | solution.py:324
  135.6 6.6 %collective-permute-start.14 = (bf16[144,384]{1,0:T(8,128)(2,1)S(1)}, bf16[144,384]{1,0:T(8,128)(2,1)S(1)}, u32[]{:S(2)}, u32[]{:S(2)}) collective-permute-start(bf16[144,384]{1,0:T(8,128)(2,1)S(1)} %collective-permute-done.10.refs_6_), channel_id=1, source_target_pairs={{0,224},{16,240},{32,0},{48,16},{64,32},{80,48},{96,64},{112,80},{... | collective-permute-start | bytes 331784 | tf_op jit(solution)/shard_map/ppermute | solution.py:326
  141.6 5.8 %collective-permute-start.12 = (bf16[144,384]{1,0:T(8,128)(2,1)S(1)}, bf16[144,384]{1,0:T(8,128)(2,1)S(1)}, u32[]{:S(2)}, u32[]{:S(2)}) collective-permute-start(bf16[144,384]{1,0:T(8,128)(2,1)S(1)} %collective-permute-done.11.refs_1_), channel_id=1, source_target_pairs={{0,32},{16,48},{32,64},{48,80},{64,96},{80,112},{96,128},{112,144}... | collective-permute-start | bytes 331784 | tf_op jit(solution)/shard_map/ppermute | solution.py:324
  142.2 5.8 %collective-permute-start.15 = (bf16[144,384]{1,0:T(8,128)(2,1)S(1)}, bf16[144,384]{1,0:T(8,128)(2,1)S(1)}, u32[]{:S(2)}, u32[]{:S(2)}) collective-permute-start(bf16[144,384]{1,0:T(8,128)(2,1)S(1)} %collective-permute-done.14.refs_5_), channel_id=1, source_target_pairs={{0,224},{16,240},{32,0},{48,16},{64,32},{80,48},{96,64},{112,80},{... | collective-permute-start | bytes 331784 | tf_op jit(solution)/shard_map/ppermute | solution.py:326
  147.4 6.0 %collective-permute-start.13 = (bf16[144,384]{1,0:T(8,128)(2,1)S(1)}, bf16[144,384]{1,0:T(8,128)(2,1)S(1)}, u32[]{:S(2)}, u32[]{:S(2)}) collective-permute-start(bf16[144,384]{1,0:T(8,128)(2,1)S(1)} %collective-permute-done.12.refs_2_), channel_id=1, source_target_pairs={{0,32},{16,48},{32,64},{48,80},{64,96},{80,112},{96,128},{112,144}... | collective-permute-start | bytes 331784 | tf_op jit(solution)/shard_map/ppermute | solution.py:324
  153.5 1.4 collective-permute-start.16
  160.2 31.4 %all-to-all-start.3 = ((bf16[16,128,384]{2,1,0:T(8,128)(2,1)}), bf16[16,128,384]{2,1,0:T(8,128)(2,1)}, u32[]{:S(2)}, u32[]{:S(2)}) async-start(bf16[16,128,384]{2,1,0:T(8,128)(2,1)} %join1.1), calls=%async_computation.3 | async-start | bytes 3145728 | tf_op jit(solution)/shard_map/all_to_all | solution.py:517
